TPU v7x, 32 devices: a whole 2x2x4 slice. The times are simulated.
32 devices in a mesh: dp: 8 (over z, x), mp: 4 (over y, core).
Axes of the slice: x: 2, y: 2, z: 4, core: 2. Of those that a mesh axis runs over, the one named last changes fastest.
Arguments:
- activations: bfloat16 [20480, 1024], P(('dp', 'mp')), may hold values from -6 to 6
- cotangent: bfloat16 [20480, 1024], P('dp'), may hold values from -6 to 6
- layout: int32 [32], P('dp'), may hold values from 0 to 2
- band_ids: int32 [32], P('dp'), may hold values from 0 to 7
- condition: float32 [8, 1024], replicated, may hold values from -6 to 6
- qkv_weight: float32 [1024, 3072], P('dp', 'mp'), may hold values from -0.1875 to 0.1875
- qkv_moment: float32 [1024, 3072], P('dp', 'mp'), may hold values from -40 to 40
- qkv_square: float32 [1024, 3072], P('dp', 'mp'), may hold values from 2.048 to 20.48
- out_weight: float32 [1024, 1024], P('dp', 'mp'), may hold values from -0.75 to 0.75
- out_moment: float32 [1024, 1024], P('dp', 'mp'), may hold values from -40 to 40
- out_square: float32 [1024, 1024], P('dp', 'mp'), may hold values from 2.048 to 20.48
- up_weight: float32 [1024, 4096], P('dp', 'mp'), may hold values from -0.1875 to 0.1875
- up_moment: float32 [1024, 4096], P('dp', 'mp'), may hold values from -40 to 40
- up_square: float32 [1024, 4096], P('dp', 'mp'), may hold values from 2.048 to 20.48
- down_weight: float32 [1024, 4096], P('dp', 'mp'), may hold values from -0.09375 to 0.09375
- down_moment: float32 [1024, 4096], P('dp', 'mp'), may hold values from -40 to 40
- down_square: float32 [1024, 4096], P('dp', 'mp'), may hold values from 2.048 to 20.48
- ada_weight: float32 [1024, 6144], P('dp'), may hold values from -0.375 to 0.375
- ada_moment: float32 [1024, 6144], P('dp'), may hold values from -40 to 40
- ada_square: float32 [1024, 6144], P('dp'), may hold values from 2.048 to 20.48
- bias_table: float32 [16, 45], P('mp'), may hold values from -4 to 4
- bias_moment: float32 [16, 45], P('mp'), may hold values from -40 to 40
- bias_square: float32 [16, 45], P('mp'), may hold values from 2.048 to 20.48
Outputs:
- layer_out: bfloat16 [20480, 1024], P(('dp', 'mp'))
- input_grad: float32 [20480, 1024], P(('dp', 'mp'))
- qkv_new: float32 [1024, 3072], P('dp', 'mp')
- qkv_moment_new: float32 [1024, 3072], P('dp', 'mp')
- qkv_square_new: float32 [1024, 3072], P('dp', 'mp')
- out_new: float32 [1024, 1024], P('dp', 'mp')
- out_moment_new: float32 [1024, 1024], P('dp', 'mp')
- out_square_new: float32 [1024, 1024], P('dp', 'mp')
- up_new: float32 [1024, 4096], P('dp', 'mp')
- up_moment_new: float32 [1024, 4096], P('dp', 'mp')
- up_square_new: float32 [1024, 4096], P('dp', 'mp')
- down_new: float32 [1024, 4096], P('dp', 'mp')
- down_moment_new: float32 [1024, 4096], P('dp', 'mp')
- down_square_new: float32 [1024, 4096], P('dp', 'mp')
- ada_new: float32 [1024, 6144], P('dp')
- ada_moment_new: float32 [1024, 6144], P('dp')
- ada_square_new: float32 [1024, 6144], P('dp')
- bias_new: float32 [16, 45], P('mp')
- bias_moment_new: float32 [16, 45], P('mp')
- bias_square_new: float32 [16, 45], P('mp')
- lamb_stats: float32 [3, 6], replicated
Inputs may be any that keep to these rules, and one draw needn't show every extreme that they name: `layout`: 0: two windows of 5 x 8 x 8 tokens; 1: one such window, then five single-frame 8 x 8 windows; 2: ten single-frame 8 x 8 windows.
All inputs are finite; a program needn't handle non-finite values.
Results may differ from a plain program's by a relative error of at most 0.02.
The roundings to bfloat16 on the way count: a program that leaves them out, or rounds other values in their place, can miss the bound.
Values may be sent and summed in bfloat16 or wider, within the bound.
No kernel may reach another device: no remote copies, remote signals or barrier semaphores. Data moves between devices by JAX's collectives and lax.ppermute only.
A program may use at most 192 MiB of HBM per device.

v0:
```python
from functools import partial

import jax
import jax.numpy as jnp
from jax import lax
from jax.sharding import PartitionSpec as P

BLOCK = 640
STEP = 10


precise = lax.Precision.HIGHEST
beta_first = 0.9
beta_second = 0.999
adam_eps = 1e-06
weight_decay = 0.01
learn_rate = 0.3
norm_eps = 1e-06


def window_layout(layout):
    places = jnp.arange(BLOCK, dtype=jnp.int32)[None, :]
    large = (2 - layout)[:, None]
    border = large * (BLOCK // 2)
    inside = places < border
    window_ids = jnp.where(
        inside, places // (BLOCK // 2), large + (places - border) // (BLOCK // 10)
    )
    frames = jnp.where(inside, places % (BLOCK // 2) // (BLOCK // 10), 0)
    rows_in = jnp.broadcast_to(places // 8 % 8, window_ids.shape)
    cols_in = jnp.broadcast_to(places % 8, window_ids.shape)
    return (window_ids, frames, rows_in, cols_in)


def normalize(values):
    centered = values - jnp.mean(values, axis=-1, keepdims=True)
    return centered * lax.rsqrt(jnp.mean(centered * centered, axis=-1, keepdims=True) + norm_eps)


def modulate(values, shift_rows, scale_rows):
    return normalize(values) * (1.0 + scale_rows) + shift_rows


def contract_rows(left, right):
    return lax.dot_general(
        left, right, (((0,), (0,)), ((), ())), preferred_element_type=jnp.float32
    )


def contract_exact(left, right):
    return lax.dot_general(
        left, right, (((0,), (0,)), ((), ())), precision=precise, preferred_element_type=jnp.float32
    )


def contract_cols(left, right):
    return lax.dot_general(
        left, right, (((1,), (1,)), ((), ())), preferred_element_type=jnp.float32
    )


def offset_table():
    grid_a = jnp.arange(64, dtype=jnp.int32) // 8
    grid_b = jnp.arange(64, dtype=jnp.int32) % 8
    return ((grid_a - grid_b + 7)[None, :] == jnp.arange(15, dtype=jnp.int32)[:, None]).astype(
        jnp.float32
    )


def position_bias(matrices, hots):
    left_part = jnp.einsum("pia,hpab->hpib", hots, matrices, precision=precise)
    return jnp.einsum("hpib,pjb->hij", left_part, hots, precision=precise)


def block_scores(queries, keys_blk, matrices, hots, window_ids, score_scale):
    scores = (
        jnp.einsum("ihe,jhe->hij", queries, keys_blk, preferred_element_type=jnp.float32)
        * score_scale
    )
    scores = scores + position_bias(matrices, hots)
    same = window_ids[:, None] == window_ids[None, :]
    return jnp.where(same[None], scores, -1e30)


def attend_block(matrices, score_scale, inputs):
    project, hots, window_ids = inputs
    scores = block_scores(
        project[:, :, 0], project[:, :, 1], matrices, hots, window_ids, score_scale
    )
    highest = jnp.max(scores, axis=-1, keepdims=True)
    log_total = highest + jnp.log(jnp.sum(jnp.exp(scores - highest), axis=-1, keepdims=True))
    probs = jnp.exp(scores - log_total).astype(jnp.bfloat16)
    attended = jnp.einsum(
        "hij,jhe->ihe", probs, project[:, :, 2], preferred_element_type=jnp.float32
    )
    return (attended.astype(jnp.bfloat16), log_total)


def attend_back(matrices, score_scale, inputs):
    project, hots, window_ids, log_total, grad_att = inputs
    queries = project[:, :, 0]
    keys_blk = project[:, :, 1]
    values_blk = project[:, :, 2]
    probs = jnp.exp(
        block_scores(queries, keys_blk, matrices, hots, window_ids, score_scale) - log_total
    )
    grad_probs = jnp.einsum(
        "ihe,jhe->hij", grad_att, values_blk, preferred_element_type=jnp.float32
    )
    inner = jnp.sum(probs * grad_probs, axis=-1, keepdims=True)
    grad_scores = (probs * (grad_probs - inner)).astype(jnp.bfloat16)
    grad_values = jnp.einsum(
        "hij,ihe->jhe", probs.astype(jnp.bfloat16), grad_att, preferred_element_type=jnp.float32
    )
    grad_queries = (
        jnp.einsum("hij,jhe->ihe", grad_scores, keys_blk, preferred_element_type=jnp.float32)
        * score_scale
    )
    grad_keys = (
        jnp.einsum("hij,ihe->jhe", grad_scores, queries, preferred_element_type=jnp.float32)
        * score_scale
    )
    hot_low = hots.astype(jnp.bfloat16)
    half_sum = jnp.einsum("pia,hij->hpaj", hot_low, grad_scores, preferred_element_type=jnp.float32)
    grad_mats = jnp.einsum("hpaj,pjb->hpab", half_sum, hots, precision=precise)
    grad_project = jnp.stack([grad_queries, grad_keys, grad_values], axis=2).astype(jnp.bfloat16)
    return (grad_project, grad_mats)


def lamb_direction(weight, moment, square, gradient):
    moment_new = beta_first * moment + (1.0 - beta_first) * gradient
    square_new = beta_second * square + (1.0 - beta_second) * gradient * gradient
    direction = (
        moment_new
        / (1.0 - beta_first**STEP)
        / (jnp.sqrt(square_new / (1.0 - beta_second**STEP)) + adam_eps)
        + weight_decay * weight
    )
    return (moment_new, square_new, direction)


def shards(
    activations,
    cotangent,
    layout,
    band_ids,
    condition,
    qkv_weight,
    qkv_moment,
    qkv_square,
    out_weight,
    out_moment,
    out_square,
    up_weight,
    up_moment,
    up_square,
    down_weight,
    down_moment,
    down_square,
    ada_weight,
    ada_moment,
    ada_square,
    bias_table,
    bias_moment,
    bias_square,
):
    model_count = lax.axis_size("mp")
    data_count = lax.axis_size("dp")
    rows_own, width = activations.shape
    group_rows = cotangent.shape[0]
    block_count = layout.shape[0]
    heads_local = bias_table.shape[0]
    head_dim = qkv_weight.shape[1] // (3 * heads_local)
    score_scale = head_dim ** (-0.5)
    qkv_full, out_full, up_full, down_full, ada_full = (
        lax.all_gather(qkv_weight.astype(jnp.bfloat16), "dp", axis=0, tiled=True),
        lax.all_gather(out_weight.astype(jnp.bfloat16), "dp", axis=0, tiled=True),
        lax.all_gather(up_weight.astype(jnp.bfloat16), "dp", axis=0, tiled=True),
        lax.all_gather(down_weight.astype(jnp.bfloat16), "dp", axis=0, tiled=True),
        lax.all_gather(ada_weight.astype(jnp.bfloat16), "dp", axis=0, tiled=True),
    )
    band_hot = (
        band_ids[:, None] == jnp.arange(condition.shape[0], dtype=jnp.int32)[None, :]
    ).astype(jnp.float32)
    cond_low = jax.nn.silu(jnp.dot(band_hot, condition, precision=precise)).astype(jnp.bfloat16)
    modulation = jnp.dot(cond_low, ada_full, preferred_element_type=jnp.float32)
    first_row = lax.axis_index("mp") * rows_own
    own_blocks = (first_row + jnp.arange(rows_own, dtype=jnp.int32)) // BLOCK
    own_hot = (own_blocks[:, None] == jnp.arange(block_count, dtype=jnp.int32)[None, :]).astype(
        jnp.float32
    )
    mod_rows = jnp.dot(own_hot, modulation, precision=precise)
    shift_one, scale_one, gate_one, shift_two, scale_two, gate_two = jnp.split(mod_rows, 6, axis=1)
    rows_x = activations.astype(jnp.float32)
    normed_one = lax.all_gather(
        modulate(rows_x, shift_one, scale_one).astype(jnp.bfloat16), "mp", axis=0, tiled=True
    )
    project = jnp.dot(normed_one, qkv_full, preferred_element_type=jnp.float32).astype(jnp.bfloat16)
    project = project.reshape(block_count, BLOCK, heads_local, 3, head_dim)
    window_ids, frames, rows_in, cols_in = window_layout(layout)
    hots = (
        jnp.stack([frames, rows_in, cols_in], axis=1)[..., None] == jnp.arange(8, dtype=jnp.int32)
    ).astype(jnp.float32)
    place = offset_table()
    matrices = jnp.einsum(
        "hpo,oq->hpq", bias_table.reshape(heads_local, 3, 15), place, precision=precise
    )
    matrices = matrices.reshape(heads_local, 3, 8, 8)
    attended, log_total = lax.map(
        partial(attend_block, matrices, score_scale), (project, hots, window_ids)
    )
    attended = attended.reshape(group_rows, heads_local * head_dim)
    branch_one = lax.psum_scatter(
        contract_cols(attended, out_full).astype(jnp.bfloat16),
        "mp",
        scatter_dimension=0,
        tiled=True,
    ).astype(jnp.float32)
    middle = rows_x + gate_one * branch_one
    normed_two = lax.all_gather(
        modulate(middle, shift_two, scale_two).astype(jnp.bfloat16), "mp", axis=0, tiled=True
    )
    hidden_pre = jnp.dot(normed_two, up_full, preferred_element_type=jnp.float32)
    hidden = jax.nn.gelu(hidden_pre, approximate=True).astype(jnp.bfloat16)
    branch_two = lax.psum_scatter(
        contract_cols(hidden, down_full).astype(jnp.bfloat16), "mp", scatter_dimension=0, tiled=True
    ).astype(jnp.float32)
    layer_out = (middle + gate_two * branch_two).astype(jnp.bfloat16)
    grad_rows = cotangent.astype(jnp.float32)
    group_blocks = jnp.arange(group_rows, dtype=jnp.int32) // BLOCK
    group_hot = (group_blocks[:, None] == jnp.arange(block_count, dtype=jnp.int32)[None, :]).astype(
        jnp.float32
    )
    gate_all = jnp.dot(group_hot, modulation[:, 5 * width :], precision=precise)
    grad_branch_two = (gate_all * grad_rows).astype(jnp.bfloat16)
    grad_hidden = jnp.dot(grad_branch_two, down_full, preferred_element_type=jnp.float32)
    gelu_back = jax.vjp(partial(jax.nn.gelu, approximate=True), hidden_pre)[1]
    grad_pre = gelu_back(grad_hidden)[0].astype(jnp.bfloat16)
    down_grad = contract_rows(grad_branch_two, hidden)
    up_grad = contract_rows(normed_two, grad_pre)
    grad_normed_two = lax.psum_scatter(
        contract_cols(grad_pre, up_full).astype(jnp.bfloat16), "mp", scatter_dimension=0, tiled=True
    ).astype(jnp.float32)
    grad_own = lax.dynamic_slice_in_dim(grad_rows, first_row, rows_own, 0)
    grad_mid, grad_shift_two, grad_scale_two = jax.vjp(modulate, middle, shift_two, scale_two)[1](
        grad_normed_two
    )
    grad_mid = grad_own + grad_mid
    grad_gate_two = grad_own * branch_two
    grad_branch_one = lax.all_gather(
        (gate_one * grad_mid).astype(jnp.bfloat16), "mp", axis=0, tiled=True
    )
    grad_attended = jnp.dot(grad_branch_one, out_full, preferred_element_type=jnp.float32).astype(
        jnp.bfloat16
    )
    out_grad = contract_rows(grad_branch_one, attended)
    grad_project, grad_mats = lax.map(
        partial(attend_back, matrices, score_scale),
        (
            project,
            hots,
            window_ids,
            log_total,
            grad_attended.reshape(block_count, BLOCK, heads_local, head_dim),
        ),
    )
    grad_project = grad_project.reshape(group_rows, 3 * heads_local * head_dim)
    qkv_grad = contract_rows(normed_one, grad_project)
    grad_normed_one = lax.psum_scatter(
        contract_cols(grad_project, qkv_full).astype(jnp.bfloat16),
        "mp",
        scatter_dimension=0,
        tiled=True,
    ).astype(jnp.float32)
    grad_input, grad_shift_one, grad_scale_one = jax.vjp(modulate, rows_x, shift_one, scale_one)[1](
        grad_normed_one
    )
    input_grad = grad_mid + grad_input
    grad_gate_one = grad_mid * branch_one
    grad_mod_rows = jnp.concatenate(
        [
            grad_shift_one,
            grad_scale_one,
            grad_gate_one,
            grad_shift_two,
            grad_scale_two,
            grad_gate_two,
        ],
        axis=1,
    )
    grad_mod = lax.psum(contract_exact(own_hot, grad_mod_rows).astype(jnp.bfloat16), "mp")
    mats_total = jnp.sum(grad_mats, axis=0).reshape(heads_local, 3, 64)
    table_local = jnp.einsum("hpq,oq->hpo", mats_total, place, precision=precise).reshape(
        heads_local, 45
    )
    qkv_sum, out_sum, up_sum, down_sum = (
        lax.psum_scatter(qkv_grad, "dp", scatter_dimension=0, tiled=True),
        lax.psum_scatter(out_grad, "dp", scatter_dimension=0, tiled=True),
        lax.psum_scatter(up_grad, "dp", scatter_dimension=0, tiled=True),
        lax.psum_scatter(down_grad, "dp", scatter_dimension=0, tiled=True),
    )
    ada_sum = lax.psum_scatter(
        contract_rows(cond_low, grad_mod), "dp", scatter_dimension=0, tiled=True
    )
    table_sum = lax.psum(table_local, "dp")
    entries = (
        (qkv_weight, qkv_moment, qkv_square, qkv_sum, 1.0),
        (out_weight, out_moment, out_square, out_sum, 1.0),
        (up_weight, up_moment, up_square, up_sum, 1.0),
        (down_weight, down_moment, down_square, down_sum, 1.0),
        (ada_weight, ada_moment, ada_square, ada_sum, 1.0 / model_count),
        (bias_table, bias_moment, bias_square, table_sum, 1.0 / data_count),
    )
    updates = [lamb_direction(entry[0], entry[1], entry[2], entry[3]) for entry in entries]
    weight_terms = jnp.stack([entry[4] * jnp.sum(entry[0] * entry[0]) for entry in entries])
    update_terms = jnp.stack(
        [entry[4] * jnp.sum(update[2] * update[2]) for entry, update in zip(entries, updates)]
    )
    norm_sums = lax.psum(jnp.stack([weight_terms, update_terms]), ("dp", "mp"))
    norms = jnp.sqrt(norm_sums)
    trust_ratio = norms[0] / norms[1]
    fresh = [
        entry[0] - learn_rate * trust_ratio[index] * update[2]
        for index, (entry, update) in enumerate(zip(entries, updates))
    ]
    lamb_stats = jnp.stack([norms[0], norms[1], trust_ratio])
    return (
        layer_out,
        input_grad,
        fresh[0],
        updates[0][0],
        updates[0][1],
        fresh[1],
        updates[1][0],
        updates[1][1],
        fresh[2],
        updates[2][0],
        updates[2][1],
        fresh[3],
        updates[3][0],
        updates[3][1],
        fresh[4],
        updates[4][0],
        updates[4][1],
        fresh[5],
        updates[5][0],
        updates[5][1],
        lamb_stats,
    )


def solution(mesh):
    return jax.shard_map(
        shards,
        mesh=mesh,
        in_specs=(
            P(("dp", "mp"), None),
            P("dp", None),
            P("dp"),
            P("dp"),
            P(),
            P("dp", "mp"),
            P("dp", "mp"),
            P("dp", "mp"),
            P("dp", "mp"),
            P("dp", "mp"),
            P("dp", "mp"),
            P("dp", "mp"),
            P("dp", "mp"),
            P("dp", "mp"),
            P("dp", "mp"),
            P("dp", "mp"),
            P("dp", "mp"),
            P("dp", None),
            P("dp", None),
            P("dp", None),
            P("mp", None),
            P("mp", None),
            P("mp", None),
        ),
        out_specs=(
            P(("dp", "mp"), None),
            P(("dp", "mp"), None),
            P("dp", "mp"),
            P("dp", "mp"),
            P("dp", "mp"),
            P("dp", "mp"),
            P("dp", "mp"),
            P("dp", "mp"),
            P("dp", "mp"),
            P("dp", "mp"),
            P("dp", "mp"),
            P("dp", "mp"),
            P("dp", "mp"),
            P("dp", "mp"),
            P("dp", None),
            P("dp", None),
            P("dp", None),
            P("mp", None),
            P("mp", None),
            P("mp", None),
            P(),
        ),
        check_vma=False,
    )
```

profile of v0, /device:TPU:0, one launch (start us, length us, event | category | flops | bytes accessed | tf_op | source)
XLA Modules:
  0.0 1737.5 jit_solution(10879939445293877574)
XLA Ops:
  13.1 176.9 %all-gather.8.cloned.1.call-done = bf16[1024,6144]{1,0:T(8,128)(2,1)} async-done(((bf16[128,6144]{1,0:T(8,128)(2,1)}), bf16[1024,6144]{1,0:T(8,128)(2,1)}) %all-gather.8.cloned.1.call-update) | async-done | bytes 12582928 | tf_op jit(solution)/shard_map/all_gather | solution.py:180
  190.0 6.3 fusion.136
  196.3 6.3 fusion.81
  202.7 5.5 copy-done.2
  210.8 32.8 %all_gather.27 = bf16[1024,256]{1,0:T(8,128)(2,1)S(1)} all-gather(bf16[128,256]{1,0:T(8,128)(2,1)S(1)} %convert_element_type.118), channel_id=1, replica_groups=mesh['dp'=8,'mp'=4] {'dp'}, dimensions={0}, use_global_device_ids=true | all-gather | bytes 589824 | tf_op jit(solution)/shard_map/all_gather | solution.py:177
  243.6 38.6 %all-gather.10.cloned.1.call-done = bf16[2560,1024]{1,0:T(8,128)(2,1)} async-done(((bf16[640,1024]{1,0:T(8,128)(2,1)}), bf16[2560,1024]{1,0:T(8,128)(2,1)}) %all-gather.10.cloned.1.call-update) | async-done | bytes 5242896 | tf_op jit(solution)/shard_map/all_gather | solution.py:195
  282.2 9.2 convolution_convert_fusion.5
  291.4 6.3 copy.107
  297.7 7.6 reshape.527
  310.0 54.2 %while.24 = (s32[]{:T(128)}, bf16[4,640,4,64]{1,3,2,0:T(8,128)(2,1)S(1)}, f32[4,4,640,1]{2,1,3,0:T(4,128)S(1)}, bf16[4,640,4,3,64]{1,4,2,3,0:T(8,128)(2,1)}, s32...) while((s32[]{:T(128)}, ...), condition=%wide.region_5.6_spmd, body=%wide.region_2.5_spmd.sunk | while | flops 910865920 | bytes 37617268 | solution.py:209
  312.0 5.4 fusion.210
  323.2 5.4 fusion.210
  334.4 5.4 fusion.210
  345.7 5.4 fusion.210
  372.2 49.7 %reduce-scatter.10.cloned.1.call-done = bf16[640,1024]{1,0:T(8,128)(2,1)} async-done(((bf16[2560,1024]{1,0:T(8,128)(2,1)}), bf16[640,1024]{1,0:T(8,128)(2,1)}) %reduce-scatter.10.cloned.1.call-update) | async-done | bytes 1310736 | tf_op jit(solution)/shard_map/reduce_scatter | solution.py:213
  430.1 8.0 multiply_convert_fusion.1
  438.0 36.1 %all-gather.16.cloned.1.call-done = bf16[1024,1024]{1,0:T(8,128)(2,1)} async-done(((bf16[128,1024]{1,0:T(8,128)(2,1)}), bf16[1024,1024]{1,0:T(8,128)(2,1)}) %all-gather.16.cloned.1.call-update) | async-done | bytes 2097168 | tf_op jit(solution)/shard_map/all_gather | solution.py:178
  474.1 41.0 %all-gather.14.cloned.1.call-done = bf16[2560,1024]{1,0:T(8,128)(2,1)} async-done(((bf16[640,1024]{1,0:T(8,128)(2,1)}), bf16[2560,1024]{1,0:T(8,128)(2,1)}) %all-gather.14.cloned.1.call-update) | async-done | bytes 5242896 | tf_op jit(solution)/shard_map/all_gather | solution.py:220
  515.2 8.4 fusion.137
  527.5 7.4 fusion.124
  535.0 88.0 %reduce-scatter.24.cloned.1.call-done = f32[128,1024]{1,0:T(8,128)} async-done(((f32[1024,1024]{1,0:T(8,128)}), f32[128,1024]{1,0:T(8,128)}) %reduce-scatter.24.cloned.1.call-update) | async-done | bytes 524304 | tf_op jit(solution)/shard_map/reduce_scatter | solution.py:300
  626.8 49.1 %all-gather.18.cloned.1.call-done = bf16[1024,1024]{1,0:T(8,128)(2,1)} async-done(((bf16[128,1024]{1,0:T(8,128)(2,1)}), bf16[1024,1024]{1,0:T(8,128)(2,1)}) %all-gather.18.cloned.1.call-update) | async-done | bytes 2097168 | tf_op jit(solution)/shard_map/all_gather | solution.py:179
  676.0 15.8 fusion.60
  694.0 7.4 convolution_convert_fusion.3
  701.5 11.4 convolution_convert_fusion.4
  712.9 8.1 convert_element_type.128
  721.1 30.4 %reduce-scatter.14.cloned.1.call-done = bf16[640,1024]{1,0:T(8,128)(2,1)} async-done(((bf16[2560,1024]{1,0:T(8,128)(2,1)}), bf16[640,1024]{1,0:T(8,128)(2,1)}) %reduce-scatter.14.cloned.1.call-update) | async-done | bytes 1310736 | tf_op jit(solution)/shard_map/reduce_scatter | solution.py:241
  754.2 51.2 %reduce-scatter.12.cloned.1.call-done = bf16[640,1024]{1,0:T(8,128)(2,1)} async-done(((bf16[2560,1024]{1,0:T(8,128)(2,1)}), bf16[640,1024]{1,0:T(8,128)(2,1)}) %reduce-scatter.12.cloned.1.call-update) | async-done | bytes 1310736 | tf_op jit(solution)/shard_map/reduce_scatter | solution.py:225
  805.5 5.5 fusion.132
  816.0 40.5 %all-gather.20.cloned.1.call-done = bf16[2560,1024]{1,0:T(8,128)(2,1)} async-done(((bf16[640,1024]{1,0:T(8,128)(2,1)}), bf16[2560,1024]{1,0:T(8,128)(2,1)}) %all-gather.20.cloned.1.call-update) | async-done | bytes 5242896 | tf_op jit(solution)/shard_map/all_gather | solution.py:250
  866.5 84.0 %while.25 = (s32[]{:T(128)}, bf16[4,640,4,3,64]{1,4,2,3,0:T(8,128)(2,1)}, f32[4,4,3,8,8]{3,4,1,2,0:T(8,128)}, bf16[4,640,4,3,64]{1,4,2,3,0:T(8,128)(2,1)}, s32[4...) while((s32[]{:T(128)}, ...), condition=%wide.region_15.16_spmd, body=%wide.region_13.15_spmd.sunk | while | flops 1631434240 | bytes 85406400 | solution.py:257
  889.5 5.4 fusion.227
  910.4 5.4 fusion.227
  931.2 5.4 fusion.227
  958.2 6.1 convolution_convert_fusion.2
  964.3 10.6 fusion.140
  981.4 10.4 fusion.138
  992.2 23.7 %reduce-scatter.16.cloned.1.call-done = bf16[640,1024]{1,0:T(8,128)(2,1)} async-done(((bf16[2560,1024]{1,0:T(8,128)(2,1)}), bf16[640,1024]{1,0:T(8,128)(2,1)}) %reduce-scatter.16.cloned.1.call-update) | async-done | bytes 1310736 | tf_op jit(solution)/shard_map/reduce_scatter | solution.py:269
  1034.6 11.3 psum.21
  1046.0 10.3 fusion.141
  1056.4 51.6 %reduce-scatter.22.cloned.1.call-done = f32[128,1024]{1,0:T(8,128)} async-done(((f32[1024,1024]{1,0:T(8,128)}), f32[128,1024]{1,0:T(8,128)}) %reduce-scatter.22.cloned.1.call-update) | async-done | bytes 524304 | tf_op jit(solution)/shard_map/reduce_scatter | solution.py:299
  1112.0 20.4 %psum.22 = f32[4,45]{1,0:T(4,128)S(1)} all-reduce(f32[4,45]{1,0:T(4,128)S(1)} %reshape.534), channel_id=1, replica_groups=mesh['dp'=8,'mp'=4] {'dp'}, use_global_device_ids=true, to_apply=%region_37.38 | all-reduce | flops 180 | bytes 1440 | tf_op jit(solution)/shard_map/psum | solution.py:305
  1134.9 40.1 %reduce-scatter.20.cloned.1.call-done = f32[128,256]{1,0:T(8,128)} async-done(((f32[1024,256]{1,0:T(8,128)}), f32[128,256]{1,0:T(8,128)}) %reduce-scatter.20.cloned.1.call-update) | async-done | bytes 131088 | tf_op jit(solution)/shard_map/reduce_scatter | solution.py:298
  1177.4 75.4 %reduce-scatter.18.cloned.1.call-done = f32[128,768]{1,0:T(8,128)} async-done(((f32[1024,768]{1,0:T(8,128)}), f32[128,768]{1,0:T(8,128)}) %reduce-scatter.18.cloned.1.call-update) | async-done | bytes 393232 | tf_op jit(solution)/shard_map/reduce_scatter | solution.py:297
  1255.9 404.0 %reduce-scatter.26.cloned.1.call-done = f32[128,6144]{1,0:T(8,128)} async-done(((f32[1024,6144]{1,0:T(8,128)}), f32[128,6144]{1,0:T(8,128)}) %reduce-scatter.26.cloned.1.call-update) | async-done | bytes 3145744 | tf_op jit(solution)/shard_map/reduce_scatter | solution.py:302
  1659.9 7.3 multiply_reduce_fusion.2
  1673.9 39.4 %psum.23 = f32[2,6]{1,0:T(2,128)S(1)} all-reduce(f32[2,6]{1,0:T(2,128)S(1)} %pad_maximum_fusion.1), channel_id=1, replica_groups=mesh['dp'=8,'mp'=4] {'dp','mp'}, use_global_device_ids=true, to_apply=%region_39.40 | all-reduce | flops 12 | bytes 96 | tf_op jit(solution)/shard_map/psum | solution.py:319
  1722.9 6.3 multiply_subtract_fusion
  (332 shorter events, 203.4 us)
Async XLA Ops:
  7.2 182.8 %all-gather.8.cloned.1.call-start = ((), (), s32[]{:S(2)}) async-start(), calls=%async_computation.9 | async-start | bytes 14155776 | tf_op jit(solution)/shard_map/all_gather | solution.py:180
  10.6 233.0 %all-gather.12.cloned.1.call-start = ((), (), s32[]{:S(2)}) async-start(), calls=%async_computation.11 | async-start | bytes 1769472 | tf_op jit(solution)/shard_map/all_gather | solution.py:176
  11.4 270.8 %all-gather.10.cloned.1.call-start = ((), (), s32[]{:S(2)}) async-start(), calls=%async_computation.10 | async-start | bytes 6553600 | tf_op jit(solution)/shard_map/all_gather | solution.py:195
  11.5 184.8 %copy-start.35 = (s32[640]{0:T(1024)}, s32[640]{0:T(1024)S(1)}, u32[]{:S(2)}) copy-start(s32[640]{0:T(1024)S(1)} %add_select_fusion.8) | copy-start | bytes 7684
  11.8 190.9 %copy-start.37 = (f32[640]{0:T(1024)}, f32[640]{0:T(1024)S(1)}, u32[]{:S(2)}) copy-start(f32[640]{0:T(1024)S(1)} %broadcast_multiply_fusion.1) | copy-start | bytes 7684
  12.9 189.8 %copy-start.43 = (f32[640]{0:T(1024)}, f32[640]{0:T(1024)S(1)}, u32[]{:S(2)}) copy-start(f32[640]{0:T(1024)S(1)} %fusion.117) | copy-start | bytes 7684
  13.1 183.2 %copy-start.41 = (bf16[4,1024]{1,0:T(4,128)(2,1)}, bf16[4,1024]{1,0:T(4,128)(2,1)S(1)}, u32[]{:S(2)}) copy-start(bf16[4,1024]{1,0:T(4,128)(2,1)S(1)} %fusion.88) | copy-start | bytes 24580
  209.8 212.1 %reduce-scatter.10.cloned.1.call-start = ((), (), s32[]{:S(2)}) async-start(), calls=%async_computation.12 | async-start | bytes 6553600 | tf_op jit(solution)/shard_map/reduce_scatter | solution.py:213
  243.5 121.9 %copy-start.25 = (bf16[1024,256]{1,0:T(8,128)(2,1)}, bf16[1024,256]{1,0:T(8,128)(2,1)S(1)}, u32[]{:S(2)}) copy-start(bf16[1024,256]{1,0:T(8,128)(2,1)S(1)} %all_gather.27) | copy-start | bytes 1572868
  370.4 103.7 %all-gather.16.cloned.1.call-start = ((), (), s32[]{:S(2)}) async-start(), calls=%async_computation.14 | async-start | bytes 2359296 | tf_op jit(solution)/shard_map/all_gather | solution.py:178
  372.2 143.0 %all-gather.14.cloned.1.call-start = ((), (), s32[]{:S(2)}) async-start(), calls=%async_computation.13 | async-start | bytes 6553600 | tf_op jit(solution)/shard_map/all_gather | solution.py:220
  424.9 380.5 %copy-start.3 = (f32[640,1024]{1,0:T(8,128)}, f32[640,1024]{1,0:T(8,128)S(1)}, u32[]{:S(2)}) copy-start(f32[640,1024]{1,0:T(8,128)S(1)} %get-tuple-element.256) | copy-start | bytes 7864324
  424.9 380.5 %copy-start.33 = (f32[640]{0:T(1024)}, f32[640]{0:T(1024)S(1)}, u32[]{:S(2)}) copy-start(f32[640]{0:T(1024)S(1)} %broadcast_multiply_fusion) | copy-start | bytes 7684
  425.4 380.1 %copy-start.39 = (f32[640]{0:T(1024)}, f32[640]{0:T(1024)S(1)}, u32[]{:S(2)}) copy-start(f32[640]{0:T(1024)S(1)} %fusion.118) | copy-start | bytes 7684
  430.0 193.0 %reduce-scatter.24.cloned.1.call-start = ((), (), s32[]{:S(2)}) async-start(), calls=%async_computation.23 | async-start | bytes 4718592 | tf_op jit(solution)/shard_map/reduce_scatter | solution.py:300
  515.1 12.4 copy-start.15
  535.0 141.0 %all-gather.18.cloned.1.call-start = ((), (), s32[]{:S(2)}) async-start(), calls=%async_computation.15 | async-start | bytes 2359296 | tf_op jit(solution)/shard_map/all_gather | solution.py:179
  626.8 124.7 %reduce-scatter.14.cloned.1.call-start = ((), (), s32[]{:S(2)}) async-start(), calls=%async_computation.17 | async-start | bytes 6553600 | tf_op jit(solution)/shard_map/reduce_scatter | solution.py:241
  676.0 18.1 %copy-start.53 = (bf16[1024,1024]{1,0:T(8,128)(2,1)S(1)}, bf16[1024,1024]{1,0:T(8,128)(2,1)}, u32[]{:S(2)}) copy-start(bf16[1024,1024]{1,0:T(8,128)(2,1)} %all-gather.16.cloned.1.call-done) | copy-start | bytes 6291460
  701.4 104.0 %reduce-scatter.12.cloned.1.call-start = ((), (), s32[]{:S(2)}) async-start(), calls=%async_computation.16 | async-start | bytes 6553600 | tf_op jit(solution)/shard_map/reduce_scatter | solution.py:225
  712.9 143.6 %all-gather.20.cloned.1.call-start = ((), (), s32[]{:S(2)}) async-start(), calls=%async_computation.18 | async-start | bytes 6553600 | tf_op jit(solution)/shard_map/all_gather | solution.py:250
  810.9 45.6 %copy-start.26 = (bf16[1024,256]{1,0:T(8,128)(2,1)S(1)}, bf16[1024,256]{1,0:T(8,128)(2,1)}, u32[]{:S(2)}) copy-start(bf16[1024,256]{1,0:T(8,128)(2,1)} %copy-done.25) | copy-start | bytes 1572868
  815.9 199.9 %reduce-scatter.16.cloned.1.call-start = ((), (), s32[]{:S(2)}) async-start(), calls=%async_computation.19 | async-start | bytes 6553600 | tf_op jit(solution)/shard_map/reduce_scatter | solution.py:269
  866.7 7.4 copy-start.9
  887.5 7.4 copy-start.9
  908.4 7.4 copy-start.9
  929.2 7.4 copy-start.9
  964.3 143.7 %reduce-scatter.22.cloned.1.call-start = ((), (), s32[]{:S(2)}) async-start(), calls=%async_computation.22 | async-start | bytes 4718592 | tf_op jit(solution)/shard_map/reduce_scatter | solution.py:299
  974.9 200.1 %reduce-scatter.20.cloned.1.call-start = ((), (), s32[]{:S(2)}) async-start(), calls=%async_computation.21 | async-start | bytes 1179648 | tf_op jit(solution)/shard_map/reduce_scatter | solution.py:298
  981.4 271.4 %reduce-scatter.18.cloned.1.call-start = ((), (), s32[]{:S(2)}) async-start(), calls=%async_computation.20 | async-start | bytes 3538944 | tf_op jit(solution)/shard_map/reduce_scatter | solution.py:297
  991.9 24.0 %copy-start.6 = (bf16[640,1024]{1,0:T(8,128)(2,1)S(1)}, bf16[640,1024]{1,0:T(8,128)(2,1)}, u32[]{:S(2)}) copy-start(bf16[640,1024]{1,0:T(8,128)(2,1)} %param.27) | copy-start | bytes 3932164
  991.9 24.0 %copy-start.38 = (f32[640]{0:T(1024)S(1)}, f32[640]{0:T(1024)}, u32[]{:S(2)}) copy-start(f32[640]{0:T(1024)} %copy-done.37) | copy-start | bytes 7684
  991.9 26.9 %copy-start.46 = (f32[640]{0:T(1024)S(1)}, f32[640]{0:T(1024)}, u32[]{:S(2)}) copy-start(f32[640]{0:T(1024)} %copy-done.45) | copy-start | bytes 7684
  991.9 26.9 %copy-start.44 = (f32[640]{0:T(1024)S(1)}, f32[640]{0:T(1024)}, u32[]{:S(2)}) copy-start(f32[640]{0:T(1024)} %copy-done.43) | copy-start | bytes 7684
  991.9 668.0 %reduce-scatter.26.cloned.1.call-start = ((), (), s32[]{:S(2)}) async-start(), calls=%async_computation.24 | async-start | bytes 28311552 | tf_op jit(solution)/shard_map/reduce_scatter | solution.py:302
  1029.4 16.6 copy-start.42
  1056.3 55.3 %copy-start.32 = (f32[4,4,3,8,8]{3,4,1,2,0:T(8,128)S(1)}, f32[4,4,3,8,8]{3,4,1,2,0:T(8,128)}, u32[]{:S(2)}) copy-start(f32[4,4,3,8,8]{3,4,1,2,0:T(8,128)} %get-tuple-element.110) | copy-start | bytes 36868
  1056.3 55.4 %copy-start.52 = (s32[64]{0:T(128)S(1)}, s32[64]{0:T(128)}, u32[]{:S(2)}) copy-start(s32[64]{0:T(128)} %copy-done.51) | copy-start | bytes 772
  1056.3 76.1 %copy-start.48 = (f32[4,45]{1,0:T(4,128)S(1)}, f32[4,45]{1,0:T(4,128)}, u32[]{:S(2)}) copy-start(f32[4,45]{1,0:T(4,128)} %param.47) | copy-start | bytes 2164
  1056.3 76.1 %copy-start.49 = (f32[4,45]{1,0:T(4,128)S(1)}, f32[4,45]{1,0:T(4,128)}, u32[]{:S(2)}) copy-start(f32[4,45]{1,0:T(4,128)} %param.48) | copy-start | bytes 2164
  1056.4 76.1 %copy-start.50 = (f32[4,45]{1,0:T(4,128)S(1)}, f32[4,45]{1,0:T(4,128)}, u32[]{:S(2)}) copy-start(f32[4,45]{1,0:T(4,128)} %param.49) | copy-start | bytes 2164
  1056.4 118.7 %copy-start.30 = (f32[128,256]{1,0:T(8,128)S(1)}, f32[128,256]{1,0:T(8,128)}, u32[]{:S(2)}) copy-start(f32[128,256]{1,0:T(8,128)} %param.35) | copy-start | bytes 393220
  1056.4 603.5 %copy-start.7 = (f32[128,6144]{1,0:T(8,128)S(1)}, f32[128,6144]{1,0:T(8,128)}, u32[]{:S(2)}) copy-start(f32[128,6144]{1,0:T(8,128)} %param.44) | copy-start | bytes 9437188
  1177.4 541.6 %copy-start.31 = (f32[128,256]{1,0:T(8,128)}, f32[128,256]{1,0:T(8,128)S(1)}, u32[]{:S(2)}) copy-start(f32[128,256]{1,0:T(8,128)S(1)} %get-tuple-element.245) | copy-start | bytes 393220
  1722.8 6.3 copy-start.24
  1722.8 6.3 copy-start.27
  1722.9 6.3 copy-start.28
  1722.9 7.9 copy-start.1
  (33 other events, 90.9 us)
Sparse Core Ops, SparseCore 0:
  10.8 179.1 all-gather.7
  192.7 47.0 all-gather.11
  242.0 40.2 all-gather.9
  370.5 51.3 reduce-scatter.9
  424.7 49.3 all-gather.15
  476.2 38.9 all-gather.13
  535.1 87.8 reduce-scatter.23
  626.9 49.0 all-gather.17
  701.6 49.8 reduce-scatter.13
  754.0 51.3 reduce-scatter.11
  816.1 40.4 all-gather.19
  964.4 51.3 reduce-scatter.15
  1019.9 88.0 reduce-scatter.21
  1111.8 63.1 reduce-scatter.19
  1179.5 73.2 reduce-scatter.17
  1257.0 402.8 reduce-scatter.25
where the time goes:
time: 1740 us
  waiting for transfers between devices  1200 us (69%)
  matrix products  239 us (14%)
  blocking collectives  104 us (6%)
  other arithmetic  96.1 us (6%)
  local copies, waits for them, and re-layouts  68.7 us (4%)
  between operations  21.5 us (1%)
    reduce_scatter x1, waiting for transfers between devices, shards(): lax.psum_scatter(contract_rows(cond_low, grad_mod), 'dp', scatter_dimensi...  404 us
    all_gather x1, waiting for transfers between devices, shards(): lax.all_gather(ada_weight.astype(jnp.bfloat16), 'dp', axis=0, tiled=True)  177 us
    reduce_scatter x1, waiting for transfers between devices, shards(): lax.psum_scatter(down_grad, 'dp', scatter_dimension=0, tiled=True)  88 us
    reduce_scatter x1, waiting for transfers between devices, shards(): lax.psum_scatter(qkv_grad, 'dp', scatter_dimension=0, tiled=True)  75.4 us
    reduce_scatter x1, waiting for transfers between devices, shards(): lax.psum_scatter(up_grad, 'dp', scatter_dimension=0, tiled=True)  51.6 us
    reduce_scatter x1, waiting for transfers between devices, shards(): lax.psum_scatter(contract_cols(hidden, down_full).astype(jnp.bfloat16), '...  51.2 us
    reduce_scatter x1, waiting for transfers between devices, shards(): lax.psum_scatter(contract_cols(attended, out_full).astype(jnp.bfloat16),...  49.7 us
    all_gather x1, waiting for transfers between devices, shards(): lax.all_gather(down_weight.astype(jnp.bfloat16), 'dp', axis=0, tiled=True)  49.1 us
  transfers between devices with their start and end apart: 16, of which 15 were waited for; matrix products, arithmetic and copies ran while one was open for 7% of the time, Pallas kernels for 0%

commit v1 on v0

v1 whole, which is shorter than its diff:
```python
from functools import partial

import jax
import jax.numpy as jnp
import numpy as np
from jax import lax
from jax.experimental import pallas as pl
from jax.experimental.pallas import tpu as pltpu
from jax.sharding import Mesh
from jax.sharding import PartitionSpec as P

BLOCK = 640
HALF = BLOCK // 2
FRAME = BLOCK // 10
LANES = 128
STEP = 10

precise = lax.Precision.HIGHEST
beta_first = 0.9
beta_second = 0.999
adam_eps = 1e-06
weight_decay = 0.01
learn_rate = 0.3
norm_eps = 1e-06
low = jnp.bfloat16
wide = jnp.float32
MIB = 1 << 20


def contract(left, right, left_dim, right_dim):
    return lax.dot_general(
        left, right, (((left_dim,), (right_dim,)), ((), ())), preferred_element_type=wide
    )


def lamb_direction(weight, moment, square, gradient):
    moment_new = beta_first * moment + (1.0 - beta_first) * gradient
    square_new = beta_second * square + (1.0 - beta_second) * gradient * gradient
    direction = (
        moment_new
        / (1.0 - beta_first**STEP)
        / (jnp.sqrt(square_new / (1.0 - beta_second**STEP)) + adam_eps)
        + weight_decay * weight
    )
    return (moment_new, square_new, direction)


def cut_sizes(count):
    sizes = []
    while count > 4:
        sizes.append(4)
        count //= 4
    sizes.append(count)
    return sizes


def from_xor(value, axes, mask):
    size = lax.axis_size(axes)
    return lax.ppermute(value, axes, [(at ^ mask, at) for at in range(size)])


def swap(value, axis):
    return from_xor(value, axis, 1)


def tree_sum(terms):
    while len(terms) > 1:
        terms = [terms[at] + terms[at + 1] for at in range(0, len(terms), 2)]
    return terms[0]


def sum_over(value, axes):
    size = lax.axis_size(axes)
    return tree_sum([value] + [from_xor(value, axes, mask) for mask in range(1, size)])


def in_pair(value, axis):
    other = swap(value, axis)
    first = lax.axis_index(axis) == 0
    return jnp.where(first, value, other), jnp.where(first, other, value)


def in_order(value, axis, dim):
    return jnp.concatenate(in_pair(value, axis), axis=dim)


def low_stages(low_axes):
    stages = []
    for axis in low_axes:
        size = lax.axis_size(axis)
        stages += [(axis, 3), (axis, 1)] if size == 4 else [(axis, 1)]
    return stages


def gather_low(shard, low_axes):
    stages = low_stages(low_axes)
    near = shard
    for axis, mask in stages[:-1]:
        near = jnp.concatenate([near, from_xor(near, axis, mask)], axis=0)
    return near, from_xor(near, *stages[-1])


def gather_rest(near, far, after):
    near_x = swap(near, "x")
    (near_x,) = gate((near_x,), after)
    near_both = jnp.concatenate([near, near_x], axis=0)
    far_other = swap(far, "y")
    near_other = swap(near_both, "y")
    far_x = swap(jnp.stack([far, far_other]), "x")
    return (near_both, far, near_other, far_other, far_x)


def gather_first(near, far):
    near_both = jnp.concatenate([near, swap(near, "x")], axis=0)
    (far,) = gate((far,), (near_both,))
    far_other = swap(far, "y")
    (near_both,) = gate((near_both,), (far_other,))
    near_other = swap(near_both, "y")
    stack = jnp.stack([far, far_other])
    return (near_both, far, near_other, far_other, swap(stack, "x")), stack


def chunk_order(low_axes):
    places = [{axis: lax.axis_index(axis) for axis in low_axes}]
    for axis, mask in low_stages(low_axes):
        places = places + [{**place, axis: place[axis] ^ mask} for place in places]
    order = []
    for place in places:
        base = jnp.int32(0)
        for axis in low_axes:
            base = base * lax.axis_size(axis) + place[axis]
        order.append(base)
    half = len(order) // 2
    x_here = lax.axis_index("x")
    full = []
    for part in (order[:half], order[half:]):
        for step in range(2):
            full = full + [base * 2 + (x_here ^ step) for base in part]
    return jnp.stack(full).astype(jnp.int32)


def sum_stages(value, low_axes):
    for axis, mask in low_stages(low_axes):
        value = value + from_xor(value, axis, mask)
    return value + swap(value, "x")


def is_large(shape):
    return np.prod(shape) >= 1 << 15


def stay(array):
    if is_large(array.shape):
        return pltpu.with_memory_space_constraint(array, pltpu.HBM)
    return array


FLOPS_PER_US = 1.15e9


def call(
    kernel,
    cost,
    grid,
    in_specs,
    out_specs,
    out_shapes,
    limit,
    args,
    scalars=(),
    deps=(),
    bases=(),
    stream=False,
):
    taken = len(scalars) + len(args)
    extra = (*bases, *deps)
    if stream:
        args = [stay(array) for array in args]

    def body(*refs):
        kernel(*refs[:taken], *refs[taken + len(extra) :])

    return pl.pallas_call(
        body,
        grid_spec=pltpu.PrefetchScalarGridSpec(
            num_scalar_prefetch=len(scalars),
            grid=grid,
            in_specs=[*in_specs, *[pl.BlockSpec(memory_space=pl.ANY)] * len(extra)],
            out_specs=out_specs,
        ),
        out_shape=[
            pltpu.HBM(shape, dtype)
            if stream and is_large(shape)
            else jax.ShapeDtypeStruct(shape, dtype)
            for shape, dtype in out_shapes
        ],
        input_output_aliases={taken + at: at for at in range(len(bases))},
        cost_estimate=pl.CostEstimate(
            flops=int(cost * FLOPS_PER_US), bytes_accessed=1, transcendentals=0
        ),
        compiler_params=pltpu.CompilerParams(vmem_limit_bytes=limit),
    )(*scalars, *args, *extra)


def gate_kernel(*_):
    pass


def gate(arrays, deps):
    return call(
        gate_kernel,
        0.5,
        (1,),
        [],
        [pl.BlockSpec(memory_space=pl.ANY)] * len(arrays),
        [(array.shape, array.dtype) for array in arrays],
        MIB,
        (),
        deps=deps,
        bases=arrays,
    )


def whole(array):
    zeros = (0,) * array.ndim
    return pl.BlockSpec(array.shape, lambda *_: zeros)


def take_chunks(values, order):
    rows, width = values.shape
    count = order.shape[0]
    return jnp.take(values.reshape(rows, count, width // count), order, axis=1).reshape(rows, width)


def inside(width, order):
    return width // order.shape[0] % LANES == 0


def load_chunks(ref, order_ref, moved):
    if not moved:
        return ref[...]
    count = order_ref.shape[0]
    chunk = ref.shape[1] // count
    return jnp.concatenate(
        [
            ref[:, pl.ds(pl.multiple_of(order_ref[at] * chunk, chunk), chunk)]
            for at in range(count)
        ],
        axis=1,
    )


def store_chunks(ref, order_ref, moved, values):
    if not moved:
        ref[...] = values
        return
    count = order_ref.shape[0]
    chunk = ref.shape[1] // count
    for at in range(count):
        ref[:, pl.ds(pl.multiple_of(order_ref[at] * chunk, chunk), chunk)] = values[
            :, at * chunk : (at + 1) * chunk
        ]


def normalize(values):
    centered = values - jnp.mean(values, axis=-1, keepdims=True)
    inverse = lax.rsqrt(jnp.mean(centered * centered, axis=-1, keepdims=True) + norm_eps)
    return centered * inverse, inverse


def norm_back(values, upstream, scale_row):
    normed, inverse = normalize(values)
    inner = upstream * (1.0 + scale_row)
    grad = (
        inner
        - jnp.mean(inner, axis=-1, keepdims=True)
        - normed * jnp.mean(inner * normed, axis=-1, keepdims=True)
    ) * inverse
    return normed, grad


def add_sums(ref, first, values):
    sums = jnp.concatenate([jnp.sum(value, axis=0, keepdims=True) for value in values], axis=0)

    @pl.when(first)
    def _():
        ref[...] = sums

    @pl.when(jnp.logical_not(first))
    def _():
        ref[...] += sums


ROWS = 128


def row_spec(width):
    return pl.BlockSpec((ROWS, width), lambda at, *_: (at, 0))


def first_norm_kernel(moved, order_ref, x_ref, mods_ref, rows_ref, normed_ref):
    rows = load_chunks(x_ref, order_ref, moved)
    rows_ref[...] = rows
    normed, _ = normalize(rows.astype(wide))
    normed_ref[...] = (normed * (1.0 + mods_ref[0, 1:2]) + mods_ref[0, 0:1]).astype(low)


def first_norm(activations, mods, order, deps):
    rows, width = activations.shape
    moved = inside(width, order)
    if not moved:
        activations = take_chunks(activations, order)
    spec = row_spec(width)
    return call(
        partial(first_norm_kernel, moved),
        2.4,
        (rows // ROWS,),
        [spec, whole(mods)],
        [spec, spec],
        [((rows, width), low)] * 2,
        8 * MIB,
        (activations, mods),
        (order,),
        deps,
    )


def cotangent_kernel(moved, order_ref, place_ref, g_ref, mods_ref, rows_ref, branch_ref):
    rows = load_chunks(g_ref, order_ref, moved)
    rows_ref[...] = rows
    branch_ref[...] = (mods_ref[0, 5:6] * rows.astype(wide)).astype(low)


def cotangent_rows(cotangent, mods, order, places, rows, deps):
    width = cotangent.shape[1]
    moved = inside(width, order)
    if not moved:
        cotangent = take_chunks(cotangent, order)
    steps = rows // ROWS
    out_spec = pl.BlockSpec((ROWS, width), lambda part, at, *_: (part * steps + at, 0))
    return call(
        partial(cotangent_kernel, moved),
        2.5,
        (2, steps),
        [
            pl.BlockSpec(
                (ROWS, width), lambda part, at, order, place: (place[part] * steps + at, 0)
            ),
            pl.BlockSpec((1, 6, width), lambda part, at, *_: (part, 0, 0)),
        ],
        [out_spec, out_spec],
        [((2 * rows, width), low)] * 2,
        8 * MIB,
        (cotangent, mods),
        (order, places),
        deps,
    )


def second_norm_kernel(x_ref, mine_ref, sent_ref, mods_ref, middle_ref, branch_ref, normed_ref):
    branch = mine_ref[...] + sent_ref[...].astype(wide)
    branch_ref[...] = branch
    middle = x_ref[...].astype(wide) + mods_ref[0, 2:3] * branch
    middle_ref[...] = middle
    normed, _ = normalize(middle)
    normed_ref[...] = (normed * (1.0 + mods_ref[0, 4:5]) + mods_ref[0, 3:4]).astype(low)


def second_norm(rows_x, mine, sent, mods):
    rows, width = rows_x.shape
    spec = row_spec(width)
    return call(
        second_norm_kernel,
        1.6,
        (rows // ROWS,),
        [spec, spec, spec, whole(mods)],
        [spec, spec, spec],
        [((rows, width), wide)] * 2 + [((rows, width), low)],
        12 * MIB,
        (rows_x, mine, sent, mods),
    )


def finish_kernel(
    moved, order_ref, middle_ref, mine_ref, sent_ref, g_ref, mods_ref, out_ref, sum_ref
):
    branch = mine_ref[...] + sent_ref[...].astype(wide)
    result = (middle_ref[...] + mods_ref[0, 5:6] * branch).astype(low)
    store_chunks(out_ref, order_ref, moved, result)
    add_sums(sum_ref, pl.program_id(0) == 0, [g_ref[...].astype(wide) * branch])


def finish(middle, mine, sent, cot_rows, mods, order, back, deps):
    rows, width = middle.shape
    spec = row_spec(width)
    moved = inside(width, order)
    out, sums = call(
        partial(finish_kernel, moved),
        3.5,
        (rows // ROWS,),
        [spec, spec, spec, spec, whole(mods)],
        [spec, pl.BlockSpec((1, width), lambda *_: (0, 0))],
        [((rows, width), low), ((1, width), wide)],
        12 * MIB,
        (middle, mine, sent, cot_rows, mods),
        (order,),
        deps,
    )
    return (out if moved else take_chunks(out, back)), sums


def second_back_kernel(
    middle_ref, branch_ref, mine_ref, sent_ref, g_ref, mods_ref, grad_ref, gated_ref, sum_ref
):
    upstream = mine_ref[...] + sent_ref[...].astype(wide)
    normed, grad = norm_back(middle_ref[...], upstream, mods_ref[0, 4:5])
    grad = g_ref[...].astype(wide) + grad
    grad_ref[...] = grad
    gated_ref[...] = (mods_ref[0, 2:3] * grad).astype(low)
    add_sums(
        sum_ref,
        pl.program_id(0) == 0,
        [grad * branch_ref[...], upstream, upstream * normed],
    )


def second_back(middle, branch, mine, sent, cot_rows, mods, deps):
    rows, width = middle.shape
    spec = row_spec(width)
    return call(
        second_back_kernel,
        3.2,
        (rows // ROWS,),
        [spec, spec, spec, spec, spec, whole(mods)],
        [spec, spec, pl.BlockSpec((3, width), lambda *_: (0, 0))],
        [((rows, width), wide), ((rows, width), low), ((3, width), wide)],
        16 * MIB,
        (middle, branch, mine, sent, cot_rows, mods),
        deps=deps,
    )


def first_back_kernel(
    moved, order_ref, x_ref, mine_ref, sent_ref, grad_ref, mods_ref, out_ref, sum_ref
):
    upstream = mine_ref[...] + sent_ref[...].astype(wide)
    normed, grad = norm_back(x_ref[...].astype(wide), upstream, mods_ref[0, 1:2])
    store_chunks(out_ref, order_ref, moved, grad_ref[...] + grad)
    add_sums(sum_ref, pl.program_id(0) == 0, [upstream, upstream * normed])


def first_back(rows_x, mine, sent, grad_mid, mods, order, back, deps):
    rows, width = rows_x.shape
    spec = row_spec(width)
    moved = inside(width, order)
    out, sums = call(
        partial(first_back_kernel, moved),
        4.0,
        (rows // ROWS,),
        [spec, spec, spec, spec, whole(mods)],
        [spec, pl.BlockSpec((2, width), lambda *_: (0, 0))],
        [((rows, width), wide), ((2, width), wide)],
        16 * MIB,
        (rows_x, mine, sent, grad_mid, mods),
        (order,),
        deps,
    )
    return (out if moved else take_chunks(out, back)), sums


def piece_list(refs):
    near, far, near_other, far_other, far_x = refs
    return (
        ((near, None), (far, None), (far_x, 0)),
        ((near_other, None), (far_other, None), (far_x, 1)),
    )


def read_piece(piece, start, size):
    ref, place = piece
    if place is None:
        return ref[:, start : start + size]
    return ref[place, :, start : start + size]


TILE = 256
M_ROWS = 320


def part_spec(width, part):
    return pl.BlockSpec((M_ROWS, width), lambda at, *_: (part * (BLOCK // M_ROWS) + at, 0))


def forward_kernel(cols, finish_tile, left_ref, *refs):
    pieces = piece_list(refs[:5])
    tail = refs[5:]
    size = cols[1] - cols[0]
    for side in range(2):
        for start in range(0, size, TILE):
            total = None
            at = 0
            for piece in pieces[side]:
                right = read_piece(piece, cols[0] + start, TILE)
                depth = right.shape[0]
                term = jnp.dot(left_ref[:, at : at + depth], right, preferred_element_type=wide)
                total = term if total is None else total + term
                at += depth
            finish_tile(total, pl.ds(side * size + start, TILE), *tail)


def store_low(total, place, out_ref):
    out_ref[:, place] = total.astype(low)


GELU_A = 0.7978845608028654
GELU_B = 0.044715


def store_gelu(total, place, out_ref, slope_ref):
    square = total * total
    tanh = jnp.tanh(total * (GELU_A + (GELU_A * GELU_B) * square))
    half = 0.5 + 0.5 * tanh
    out_ref[:, place] = (total * half).astype(low)
    inner = GELU_A + (3.0 * GELU_A * GELU_B) * square
    slope_ref[:, place] = (half + 0.5 * total * (1.0 - tanh * tanh) * inner).astype(low)


def store_slope(total, place, slope_ref, out_ref):
    out_ref[:, place] = (total * slope_ref[:, place].astype(wide)).astype(low)


def forward_product(
    left, left_part, pieces, cols, finish_tile, outs, part, bases=(), extra=(), deps=()
):
    depth = left.shape[1]
    size = 2 * (cols[1] - cols[0])
    return call(
        partial(forward_kernel, cols, finish_tile),
        0.8 + size / (300.0 if outs > 1 else 550.0),
        (BLOCK // M_ROWS,),
        [part_spec(depth, left_part)]
        + [whole(piece) for piece in pieces]
        + [part_spec(size, part)] * len(extra),
        [part_spec(size, part)] * outs,
        [((2 * BLOCK, size), low)] * outs,
        24 * MIB,
        (left, *pieces, *extra),
        deps=deps,
        bases=bases,
    )


def backward_kernel(cols, left_ref, *refs):
    pieces = piece_list(refs[:5])
    out_ref = refs[5]
    size = cols[1] - cols[0]
    at = 0
    for own, other in zip(*pieces):
        depth = own[0].shape[-2]
        for start in range(0, depth, TILE):
            total = None
            for side, (ref, place) in enumerate((own, other)):
                index = (pl.ds(start, TILE), pl.ds(cols[0], size))
                right = ref[index] if place is None else ref[(place, *index)]
                term = contract(left_ref[:, side * size : (side + 1) * size], right, 1, 1)
                total = term if total is None else total + term
            out_ref[:, at + start : at + start + TILE] = total.astype(out_ref.dtype)
        at += depth


def backward_product(left, part, pieces, cols, kind, deps=()):
    depth = left.shape[1]
    width = 2 * pieces[0].shape[0]
    return call(
        partial(backward_kernel, cols),
        0.6 + depth / 500.0,
        (BLOCK // M_ROWS,),
        [part_spec(depth, part)] + [whole(piece) for piece in pieces],
        [pl.BlockSpec((M_ROWS, width), lambda at, *_: (at, 0))],
        [((BLOCK, width), kind)],
        24 * MIB,
        (left, *pieces),
        deps=deps,
    )[0]


SLICES = 2


def row_product(lefts, right_ref, start, size):
    total = None
    for part, left_ref in enumerate(lefts):
        term = contract(
            left_ref[:, start : start + size], right_ref[part * BLOCK : (part + 1) * BLOCK], 0, 0
        )
        total = term if total is None else total + term
    return total


def quarter_of(left_ref):
    return left_ref.shape[1] // 4


def sent_kernel(products, *refs):
    step = pl.program_id(0)
    near_ref, far_ref = refs[3 * products :]
    half = pl.num_programs(0) // 2
    at = 0
    for product in range(products):
        *lefts, right_ref = refs[3 * product : 3 * product + 3]
        quarter = quarter_of(lefts[0])
        cols = right_ref.shape[1]
        place = pl.ds(at, cols)
        far_ref[:, place] = row_product(lefts, right_ref, 3 * quarter, quarter).astype(low)

        @pl.when(step >= half)
        def _(lefts=lefts, right_ref=right_ref, place=place, quarter=quarter):
            near_ref[:, place] = row_product(lefts, right_ref, 0, 2 * quarter).astype(low)

        at += cols


def kept_kernel(products, *refs):
    step = pl.program_id(0)
    near_in, far_in, near_keep, far_keep, near_send, far_send = refs[3 * products :]
    half = pl.num_programs(0) // 2
    at = 0
    for product in range(products):
        *lefts, right_ref = refs[3 * product : 3 * product + 3]
        quarter = quarter_of(lefts[0])
        cols = right_ref.shape[1]
        place = pl.ds(at, cols)
        far = row_product(lefts, right_ref, 2 * quarter, quarter) + far_in[:, place].astype(wide)

        @pl.when(step < half)
        def _(lefts=lefts, right_ref=right_ref, place=place, quarter=quarter, far=far):
            near = row_product(lefts, right_ref, 0, 2 * quarter) + near_in[:, place].astype(wide)
            near_keep[:, place] = near[:quarter]
            near_send[:, place] = near[quarter:].astype(low)
            far_keep[:, place] = far

        @pl.when(step >= half)
        def _(place=place, far=far):
            far_send[:, place] = far.astype(low)

        at += cols


def gradient_layout(products):
    width = products[0][0][0].shape[1]
    args, specs, total = [], [], 0
    for *lefts, right in products:
        for array, part in lefts:
            args.append(array)
            specs.append(pl.BlockSpec((BLOCK, width), lambda *_, part=part: (part, 0)))
        cols = right.shape[1] // SLICES
        args.append(right)
        specs.append(pl.BlockSpec((right.shape[0], cols), lambda at, *_: (0, at)))
        total += cols
    return args, specs, SLICES, width // 4, total


def near_spec(rows, cols, steps, late):
    half = steps // 2
    if late:
        return pl.BlockSpec((rows, cols), lambda at, *_: (0, jnp.maximum(at - half, 0)))
    return pl.BlockSpec((rows, cols), lambda at, *_: (0, jnp.minimum(at, half - 1)))


def sent_gradient(products, deps=()):
    args, specs, steps, quarter, cols = gradient_layout(products)
    return call(
        partial(sent_kernel, len(products)),
        3.0,
        (steps,),
        specs,
        [
            near_spec(2 * quarter, cols, steps, True),
            pl.BlockSpec((quarter, cols), lambda at, *_: (0, at)),
        ],
        [((2 * quarter, cols * steps // 2), low), ((quarter, cols * steps), low)],
        24 * MIB,
        args,
        deps=deps,
    )


def kept_gradient(products, moved, deps=()):
    args, specs, steps, quarter, cols = gradient_layout(products)
    size = cols * steps // 2
    early = near_spec(quarter, cols, steps, False)
    near_keep, far_keep, *sent = call(
        partial(kept_kernel, len(products)),
        4.0,
        (steps,),
        specs
        + [
            near_spec(2 * quarter, cols, steps, False),
            pl.BlockSpec((quarter, cols), lambda at, *_: (0, at)),
        ],
        [early, early, early, near_spec(quarter, cols, steps, True)],
        [((quarter, size), wide)] * 2 + [((quarter, size), low)] * 2,
        32 * MIB,
        (*args, *moved),
        deps=deps,
    )
    return (near_keep, far_keep), sent


def third_kernel(near_ref, far_ref, near_in, far_in, keep_ref, send_ref):
    keep_ref[...] = near_ref[...] + near_in[...].astype(wide)
    send_ref[...] = (far_ref[...] + far_in[...].astype(wide)).astype(low)


def third_gradient(kept, moved, deps=()):
    rows, cols = kept[0].shape
    step = min(64, rows)
    spec = pl.BlockSpec((step, cols), lambda at, *_: (at, 0))
    return call(
        third_kernel,
        1.0,
        (rows // step,),
        [spec] * 4,
        [spec] * 2,
        [((rows, cols), wide), ((rows, cols), low)],
        16 * MIB,
        (*kept, *moved),
        deps=deps,
    )


def fourth_kernel(keep_ref, in_ref, out_ref, send_ref):
    half = out_ref.shape[0]
    out_ref[...] = keep_ref[:half] + in_ref[:half].astype(wide)
    send_ref[...] = (keep_ref[half:] + in_ref[half:].astype(wide)).astype(low)


def fourth_gradient(keep, moved, low_axes, deps=()):
    send = None
    for axis, mask in reversed(low_stages(low_axes)[:-1]):
        rows, cols = keep.shape
        keep, send = call(
            fourth_kernel,
            1.0,
            (1,),
            [whole(keep), whole(moved)],
            [pl.BlockSpec((rows // 2, cols), lambda *_: (0, 0))] * 2,
            [((rows // 2, cols), wide), ((rows // 2, cols), low)],
            16 * MIB,
            (keep, moved),
            deps=deps,
        )
        moved = from_xor(send, axis, mask)
    return (keep, moved), send


def lanes_below(shape):
    return lax.broadcasted_iota(jnp.int32, shape, 1) < LANES // 2


def turned(tile):
    return jnp.concatenate([tile[:, LANES // 2 :], tile[:, : LANES // 2]], axis=1)


def head_tiles(x_ref, rows):
    first = x_ref[rows, 0:LANES]
    second = x_ref[rows, LANES : 2 * LANES]
    third = x_ref[rows, 2 * LANES : 3 * LANES]
    return first, second, third


def attend_kernel(kind_ref, x_ref, bias_ref, out_ref, log_ref):
    left = lanes_below((HALF, LANES))
    top = lax.broadcasted_iota(jnp.int32, (LANES, HALF), 0) < LANES // 2
    zero = jnp.zeros((HALF, LANES), low)
    one = jnp.ones((HALF, LANES), low)
    for half in range(2):
        rows = pl.ds(half * HALF, HALF)
        first, second, third = head_tiles(x_ref, rows)
        kind = kind_ref[half]
        sides = (
            (turned(first), jnp.where(left, first * 0.125, zero), jnp.where(left, second, one)),
            (turned(third), jnp.where(left, zero, second * 0.125), jnp.where(left, one, third)),
        )
        parts = []
        for head, (keys, queries, values) in enumerate(sides):
            scores = contract(keys, queries, 1, 1) + bias_ref[head, kind]
            highest = jnp.max(scores, axis=0, keepdims=True)
            weights = jnp.exp(scores - highest).astype(low)
            total = contract(values, weights, 0, 0)
            spot = (1 - head) * (LANES // 2)
            count = total[spot : spot + 1]
            log_ref[0, 2 * half + head : 2 * half + head + 1] = highest + jnp.log(count)
            parts.append(total / count)
        out_ref[rows, :] = jnp.where(top, parts[0], parts[1]).T.astype(low)


def attend_back_kernel(
    kind_ref, x_ref, grad_ref, bias_ref, log_ref, hots_ref, out_ref, table_ref
):
    left = lanes_below((HALF, LANES))
    zero = jnp.zeros((HALF, LANES), low)
    hots = hots_ref[...]
    for half in range(2):
        rows = pl.ds(half * HALF, HALF)
        first, second, third = head_tiles(x_ref, rows)
        grads = grad_ref[rows, :]
        kind = kind_ref[half]
        first_turned, second_turned, third_turned = turned(first), turned(second), turned(third)
        sides = (
            (
                jnp.where(left, first_turned, zero),
                jnp.where(left, first * 0.125, zero),
                second,
                jnp.where(left, grads, zero),
                jnp.where(left, hots, first_turned * 0.125),
            ),
            (
                jnp.where(left, zero, third_turned),
                jnp.where(left, zero, second * 0.125),
                third,
                jnp.where(left, zero, grads),
                jnp.where(left, second_turned * 0.125, hots),
            ),
        )
        query_grad = None
        key_grads = []
        value_grads = []
        for head, (keys, queries, values, grad, queries_turned) in enumerate(sides):
            scores = contract(keys, queries, 1, 1) + bias_ref[head, kind]
            probs = jnp.exp(scores - log_ref[0, 2 * half + head : 2 * half + head + 1])
            grad_probs = contract(values, grad, 1, 1)
            inner = jnp.sum(probs * grad_probs, axis=0, keepdims=True)
            grad_scores = (probs * (grad_probs - inner)).astype(low)
            value_grads.append(jnp.dot(probs.astype(low), grad, preferred_element_type=wide))
            key_grads.append(jnp.dot(grad_scores, queries_turned, preferred_element_type=wide))
            term = contract(keys, grad_scores, 0, 0)
            query_grad = term if query_grad is None else query_grad + term
        table = jnp.where(left, key_grads[0], key_grads[1])
        total = table if half == 0 else total + table
        query_rows = (query_grad * 0.125).T
        out_ref[rows, 0:LANES] = jnp.where(left, query_rows, key_grads[0]).astype(low)
        out_ref[rows, LANES : 2 * LANES] = jnp.where(left, value_grads[0], query_rows).astype(low)
        out_ref[rows, 2 * LANES :] = jnp.where(left, key_grads[1], value_grads[1]).astype(low)
    table_ref[0] = lax.dot_general(
        hots.astype(wide),
        total,
        (((0,), (0,)), ((), ())),
        precision=precise,
        preferred_element_type=wide,
    )


def attention_specs(part):
    return (
        pl.BlockSpec((BLOCK, 3 * LANES), lambda at, *_: (part, at)),
        pl.BlockSpec((BLOCK, LANES), lambda at, *_: (part, at)),
        pl.BlockSpec((2, 2, HALF, HALF), lambda at, *_: (at, 0, 0, 0)),
        pl.BlockSpec((1, 4, HALF), lambda at, *_: (at, 0, 0)),
        pl.BlockSpec((1, LANES, LANES), lambda at, *_: (at, 0, 0)),
    )


def attend(project, part, bias, kinds, bases=(), deps=()):
    pairs = project.shape[1] // (3 * LANES)
    wide_spec, out_spec, bias_spec, log_spec, _ = attention_specs(part)
    return call(
        attend_kernel,
        7.0,
        (pairs,),
        [wide_spec, bias_spec],
        [out_spec, log_spec],
        [((2 * BLOCK, pairs * LANES), low), ((pairs, 4, HALF), wide)],
        24 * MIB,
        (project, bias),
        (kinds,),
        deps,
        bases,
    )


def attend_back(project, grad, part, bias, logs, kinds, bases=(), deps=()):
    pairs = project.shape[1] // (3 * LANES)
    wide_spec, out_spec, bias_spec, log_spec, table_spec = attention_specs(part)
    hots = np.zeros((HALF, LANES), np.float32)
    hots[:, :24] = place_hots()
    hots[:, LANES // 2 : LANES // 2 + 24] = place_hots()
    hots = jnp.asarray(hots, low)
    return call(
        attend_back_kernel,
        11.0,
        (pairs,),
        [wide_spec, out_spec, bias_spec, log_spec, whole(hots)],
        [wide_spec, table_spec],
        [((2 * BLOCK, pairs * 3 * LANES), low), ((pairs, LANES, LANES), wide)],
        24 * MIB,
        (project, grad, bias, logs, hots),
        (kinds,),
        deps,
        bases,
    )


def place_hots():
    places = np.arange(HALF)
    hots = [places // FRAME, places // 8 % 8, places % 8]
    return np.concatenate([np.eye(8, dtype=np.float32)[hot] for hot in hots], axis=1)


def offset_table():
    offsets = np.zeros((45, 24, 24), np.float32)
    for part in range(3):
        for key in range(8):
            for query in range(8):
                offsets[15 * part + query - key + 7, 8 * part + key, 8 * part + query] = 1.0
    return offsets


def terms_kernel(hots_ref, inner_ref, out_ref, done_ref):
    done_ref[...] = jnp.zeros(done_ref.shape, wide)
    terms = jnp.dot(
        hots_ref[...], inner_ref[0], precision=precise, preferred_element_type=wide
    )
    frames = [
        lax.broadcasted_iota(jnp.int32, (HALF, HALF), dim) // FRAME for dim in range(2)
    ]
    out_ref[0, 0] = terms
    out_ref[0, 1] = jnp.where(frames[0] == frames[1], terms, -1e30)


def position_terms(table, deps):
    heads = table.shape[0]
    hots = place_hots()
    spread = np.einsum("oab,ib->oai", offset_table(), hots)
    inner = jnp.einsum("ho,oai->hai", table, spread, precision=precise)
    hots = jnp.asarray(hots)
    return call(
        terms_kernel,
        3.0,
        (heads,),
        [whole(hots), pl.BlockSpec((1, 24, HALF), lambda at, *_: (at, 0, 0))],
        [
            pl.BlockSpec((1, 2, HALF, HALF), lambda at, *_: (at, 0, 0, 0)),
            pl.BlockSpec((8, LANES), lambda *_: (0, 0)),
        ],
        [((heads, 2, HALF, HALF), wide), ((8, LANES), wide)],
        12 * MIB,
        (hots, inner),
        deps=deps,
    )


def table_gradient(sums):
    pairs = sums.shape[0]
    half = LANES // 2
    grads = jnp.stack(
        [sums[:, at : at + 24, at : at + 24] for at in (0, half)], axis=1
    )
    table = jnp.einsum("peab,oab->peo", grads, offset_table(), precision=precise)
    return table.reshape(2 * pairs, 45)


def lane_sums(values):
    rows, cols = values.shape
    values = values * values
    parts = [values[at : at + 8] for at in range(0, rows, 8)]
    total = sum(parts[1:], parts[0])
    parts = [total[:, at : at + LANES] for at in range(0, cols, LANES)]
    total = sum(parts[1:], parts[0])
    return jnp.sum(total, axis=0, keepdims=True)


def lamb_step(first, weight_ref, moment_ref, square_ref, gradient, outs):
    moment_out, square_out, direction_out, sums_out = outs
    weight = weight_ref[...]
    moment, square, direction = lamb_direction(
        weight, moment_ref[...], square_ref[...], gradient
    )
    moment_out[...] = moment
    square_out[...] = square
    direction_out[...] = direction
    sums = jnp.concatenate([lane_sums(weight), lane_sums(direction)], axis=0)

    @pl.when(first)
    def _():
        sums_out[...] = sums

    @pl.when(jnp.logical_not(first))
    def _():
        sums_out[...] += sums


def lamb_kernel(start, weight_ref, moment_ref, square_ref, keep_ref, moved_ref, *outs):
    place = pl.ds(start, weight_ref.shape[1])
    gradient = keep_ref[:, place] + moved_ref[:, place].astype(wide)
    lamb_step(pl.program_id(0) == 0, weight_ref, moment_ref, square_ref, gradient, outs)


def lamb_outs(weight, spec):
    shapes = [(weight.shape, wide)] * 3 + [((2, LANES), wide)]
    return [spec, spec, spec, pl.BlockSpec((2, LANES), lambda *_: (0, 0))], shapes


def lamb(weight, moment, square, terms, start=0, deps=()):
    rows, cols = weight.shape
    step = min(64, rows)
    spec = pl.BlockSpec((step, cols), lambda at, *_: (at, 0))
    term_spec = pl.BlockSpec((step, terms[0].shape[1]), lambda at, *_: (at, 0))
    out_specs, shapes = lamb_outs(weight, spec)
    return call(
        partial(lamb_kernel, start),
        1.5,
        (rows // step,),
        [spec, spec, spec, term_spec, term_spec],
        out_specs,
        shapes,
        16 * MIB,
        (weight, moment, square, *terms),
        deps=deps,
    )


def lamb_ada_kernel(parts, weight_ref, moment_ref, square_ref, *refs):
    gradient = None
    for cond_ref, mod_ref in zip(refs[:parts], refs[parts : 2 * parts]):
        term = contract(cond_ref[...], mod_ref[...], 0, 0)
        gradient = term if gradient is None else gradient + term
    first = pl.program_id(0) == 0
    lamb_step(first, weight_ref, moment_ref, square_ref, gradient, refs[2 * parts :])


def lamb_ada(weight, moment, square, conds, mods, deps):
    rows, cols = weight.shape
    step = 1024
    spec = pl.BlockSpec((rows, step), lambda at, *_: (0, at))
    out_specs, shapes = lamb_outs(weight, spec)
    return call(
        partial(lamb_ada_kernel, len(conds)),
        8.0,
        (cols // step,),
        [spec, spec, spec]
        + [whole(cond) for cond in conds]
        + [pl.BlockSpec((mod.shape[0], step), lambda at, *_: (0, at)) for mod in mods],
        out_specs,
        shapes,
        24 * MIB,
        (weight, moment, square, *conds, *mods),
        deps=deps,
        stream=True,
    )


def update_kernel(terms, copies_ref, *refs):
    total = tree_sum([ref[...] for ref in refs[:terms]])
    norms = jnp.sqrt(jnp.sum(total, axis=1, keepdims=True) * copies_ref[...])
    refs = refs[terms:]
    count = (len(refs) - 1) // 3
    weights, directions, outs = refs[:count], refs[count : 2 * count], refs[2 * count : 3 * count]
    lane = lax.broadcasted_iota(jnp.int32, (1, count), 1)
    stats = [jnp.zeros((1, count), wide)] * 3
    for at in range(count):
        weight_norm, update_norm = norms[2 * at : 2 * at + 1], norms[2 * at + 1 : 2 * at + 2]
        trust = weight_norm / update_norm
        outs[at][...] = weights[at][...] - learn_rate * trust * directions[at][...]
        values = (weight_norm, update_norm, trust)
        stats = [jnp.where(lane == at, value, row) for value, row in zip(values, stats)]
    refs[-1][...] = jnp.concatenate(stats, axis=0)


def update_weights(terms, copies, weights, directions):
    rows = weights[0].shape[0]
    step = min(32, rows)

    def spec(array):
        if array.shape[0] != rows:
            return whole(array)
        return pl.BlockSpec((step, array.shape[1]), lambda at, *_: (at, 0))

    specs = [spec(weight) for weight in weights]
    stats = (3, len(weights))
    return call(
        partial(update_kernel, len(terms)),
        5.0,
        (rows // step,),
        [whole(copies)] + [whole(term) for term in terms] + specs * 2,
        specs + [pl.BlockSpec(stats, lambda *_: (0, 0))],
        [(weight.shape, wide) for weight in weights] + [(stats, wide)],
        24 * MIB,
        (copies, *terms, *weights, *directions),
        stream=True,
    )


def shards(
    low_axes,
    activations,
    cotangent,
    layout,
    band_ids,
    condition,
    qkv_weight,
    qkv_moment,
    qkv_square,
    out_weight,
    out_moment,
    out_square,
    up_weight,
    up_moment,
    up_square,
    down_weight,
    down_moment,
    down_square,
    ada_weight,
    ada_moment,
    ada_square,
    bias_table,
    bias_moment,
    bias_square,
):
    data_axes = (*low_axes, "x")
    model_axes = ("y", "pair")
    model_count = lax.axis_size(model_axes)
    data_count = lax.axis_size(data_axes)
    data_at = lax.axis_index(data_axes)
    model_at = lax.axis_index(model_axes)
    partner_at = model_at + 1 - 2 * lax.axis_index("pair")
    rows_own, width = activations.shape
    heads_own = bias_table.shape[0]
    qkv_cols = qkv_weight.shape[1]
    attn_cols = qkv_cols + out_weight.shape[1]
    hidden_cols = up_weight.shape[1]
    chunk = width // data_count
    bands = condition.shape[0]

    order = chunk_order(low_axes)
    back = jnp.argsort(order).astype(jnp.int32)

    attn_shard = jnp.concatenate([qkv_weight.astype(low), out_weight.astype(low)], axis=1)
    attn_near, attn_far = gather_low(attn_shard, low_axes)
    attn, attn_stack = gather_first(attn_near, attn_far)
    up_halves = gather_low(*gate((up_weight.astype(low),), (attn_far,)), low_axes)
    up_near, up_far = up_halves
    up_halves = gate(up_halves, attn[2:])
    down_halves = gather_low(*gate((down_weight.astype(low),), (up_halves[1],)), low_axes)
    near_both, far, _, far_other, _ = range(5)

    cond_bands = jax.nn.silu(condition).astype(low)
    cond_mine = lax.dynamic_slice_in_dim(cond_bands, data_at * chunk, chunk, 1)
    (cond_mine,) = gate((cond_mine,), (attn_shard,))
    share = ada_weight.shape[1] // model_count
    ada_cols = lax.dynamic_slice_in_dim(ada_weight, model_at * share, share, 1).astype(low)
    mod_bands = jnp.dot(cond_mine, ada_cols, preferred_element_type=wide)
    mod_bands = mod_bands + swap(mod_bands, "x")
    mod_bands, table_own = gate((mod_bands, bias_table), (attn_near,))
    table_two = jnp.concatenate([table_own, swap(table_own, "y")], axis=0)
    halves = jnp.stack(in_pair(mod_bands, "y"), axis=1)
    (halves,) = gate((halves,), (attn_far,))
    halves = jnp.stack(in_pair(halves, "pair"), axis=2)
    for axis, mask in low_stages(low_axes)[:-1]:
        halves = halves + from_xor(halves, axis, mask)
    (halves,) = gate((halves,), (attn[near_both], attn_stack))
    halves = halves + from_xor(halves, *low_stages(low_axes)[-1])
    mod_bands = halves.reshape(condition.shape[0], model_count * share)

    places = jnp.stack([model_at, partner_at]).astype(jnp.int32)
    layouts = jnp.take(layout, places)
    mods = jnp.take(mod_bands, jnp.take(band_ids, places), axis=0)
    mods = jnp.take(mods.reshape(2, 6, data_count, chunk), order, axis=2).reshape(2, 6, width)
    kinds = (jnp.arange(2, dtype=jnp.int32)[None, :] >= 2 - layouts[:, None]).astype(jnp.int32)
    bias, bias_done = position_terms(table_two, (attn[near_both], attn_stack, up_near))

    qkv_range = (0, qkv_cols)
    out_range = (qkv_cols, attn_cols)
    all_range = (0, hidden_cols)

    rows_x, normed_one = first_norm(activations, mods, order, (bias_done, up_far))
    normed_one_other = swap(normed_one, "pair")
    project = forward_product(
        normed_one, 0, attn, qkv_range, store_low, 1, 0, deps=(up_halves[1],)
    )
    (project,) = forward_product(
        normed_one_other, 0, attn, qkv_range, store_low, 1, 1, bases=project
    )
    attended, logs_other = attend(project, 1, bias, kinds[1])
    up = gather_rest(*up_halves, (attended,))
    down_halves = gate(down_halves, up[2:])
    down = gather_rest(*down_halves, (up[near_both],))
    sent = swap(
        backward_product(
            attended, 1, attn, out_range, low, (up[near_both], up[far_other])
        ),
        "pair",
    )
    attended, logs = attend(project, 0, bias, kinds[0], (attended,))
    mine = backward_product(attended, 0, attn, out_range, wide)
    middle, branch_one, normed_two = second_norm(rows_x, mine, sent, mods)
    normed_two_other = swap(normed_two, "pair")
    hidden = forward_product(
        normed_two, 0, up, all_range, store_gelu, 2, 0, deps=(down_halves[1],)
    )
    hidden, slope = forward_product(
        normed_two_other,
        0,
        up,
        all_range,
        store_gelu,
        2,
        1,
        bases=hidden,
        deps=(down[near_both], down[far_other]),
    )


    low_stage = low_stages(low_axes)[-1]
    cot_rows, grad_branch_two = cotangent_rows(cotangent, mods, order, places, rows_own, (bias_done,))
    down_product = (((grad_branch_two, 0), (grad_branch_two, 1), hidden),)
    down_sent = sent_gradient(down_product, (down[near_both], down[far_other]))
    down_sent = gate(down_sent, down[2:])
    down_moved = swap(down_sent[0], "y"), swap(down_sent[1], "x")
    grad_pre = forward_product(
        grad_branch_two,
        1,
        down,
        all_range,
        store_slope,
        1,
        1,
        extra=(slope,),
        deps=(down_sent[0],),
    )
    other_rows = backward_product(grad_pre[0], 1, up, all_range, low)
    sent = swap(other_rows, "pair")
    (grad_pre,) = forward_product(
        grad_branch_two, 0, down, all_range, store_slope, 1, 0, bases=grad_pre, extra=(slope,)
    )
    mine = backward_product(grad_pre, 0, up, all_range, wide)
    sent_two_rows = backward_product(hidden, 1, down, all_range, low, (mine,))
    sent_two = swap(sent_two_rows, "pair")
    down_kept, down_sent = kept_gradient(down_product, down_moved, (sent_two_rows,))
    down_moved = swap(down_sent[0], "x"), swap(down_sent[1], "y")
    grad_mid, grad_branch_one, middle_sums = second_back(
        middle, branch_one, mine, sent, cot_rows, mods, (down_sent[0],)
    )
    grad_branch_one_other = swap(grad_branch_one, "pair")
    up_product = (((normed_two, 0), (normed_two_other, 0), grad_pre),)
    up_sent = sent_gradient(up_product, (grad_branch_one,))
    up_moved = swap(up_sent[0], "y"), swap(up_sent[1], "x")
    grad_attended = forward_product(
        grad_branch_one, 0, attn, out_range, store_low, 1, 0, deps=(up_sent[0],)
    )
    (grad_attended,) = forward_product(
        grad_branch_one_other, 0, attn, out_range, store_low, 1, 1, bases=grad_attended
    )
    grad_project, sums_other = attend_back(
        project, grad_attended, 1, bias, logs_other, kinds[1], deps=(sent_two,)
    )
    other_rows = backward_product(grad_project, 1, attn, qkv_range, low)
    sent = swap(other_rows, "pair")
    down_kept, down_sent = third_gradient(down_kept, down_moved, (other_rows,))
    down_moved = from_xor(down_sent, *low_stage)
    grad_project, sums_own = attend_back(
        project, grad_attended, 0, bias, logs, kinds[0], (grad_project,), (down_sent,)
    )
    qkv_product = (
        ((normed_one, 0), (normed_one_other, 0), grad_project),
        ((grad_branch_one, 0), (grad_branch_one_other, 0), attended),
    )
    qkv_sent = sent_gradient(qkv_product, (sent,))
    qkv_moved = swap(qkv_sent[0], "y"), swap(qkv_sent[1], "x")
    down_terms, down_sent = fourth_gradient(down_kept, down_moved, low_axes, (qkv_sent[0],))
    mine = backward_product(grad_project, 0, attn, qkv_range, wide, (down_sent,))
    up_kept, up_sent = kept_gradient(up_product, up_moved, (mine,))
    up_moved = swap(up_sent[0], "x"), swap(up_sent[1], "y")
    input_grad, input_sums = first_back(
        rows_x, mine, sent, grad_mid, mods, order, back, (up_sent[0],)
    )
    down_update = lamb(down_weight, down_moment, down_square, down_terms, deps=(input_sums,))
    mine_two = backward_product(hidden, 0, down, all_range, wide, (down_update[3],))
    layer_out, gate_two_sum = finish(
        middle, mine_two, sent_two, cot_rows, mods, order, back, ()
    )
    up_kept, up_sent_third = third_gradient(up_kept, up_moved, (gate_two_sum,))
    up_moved = from_xor(up_sent_third, *low_stage)
    up_terms, up_sent = fourth_gradient(up_kept, up_moved, low_axes)
    qkv_kept, qkv_sent = kept_gradient(qkv_product, qkv_moved, (up_sent,))
    qkv_sent_second = qkv_sent[0]
    qkv_moved = swap(qkv_sent[0], "x"), swap(qkv_sent[1], "y")
    qkv_kept, qkv_sent = third_gradient(qkv_kept, qkv_moved)
    qkv_moved = from_xor(qkv_sent, *low_stage)
    qkv_terms, qkv_sent_last = fourth_gradient(qkv_kept, qkv_moved, low_axes)

    grad_mod = jnp.concatenate([input_sums, middle_sums, gate_two_sum], axis=0).astype(low)
    grad_mod = jnp.take(grad_mod.reshape(6, data_count, chunk), back, axis=1)
    band_own = jnp.take(band_ids, model_at).astype(low)
    (sums_own,) = gate((sums_own,), (mine_two,))
    table = table_gradient(sums_own + sums_other).reshape(1, 2 * heads_own * 45)
    table_low = table.astype(low)
    table_rest = (table - table_low.astype(wide)).astype(low)
    message = jnp.concatenate(
        [
            grad_mod.reshape(1, 6 * width),
            jnp.broadcast_to(band_own, (1, LANES)),
            table_low,
            table_rest,
        ],
        axis=1,
    )
    (message,) = gate((message,), (qkv_sent_second,))
    message = in_order(in_order(message, "pair", 0), "y", 0)
    (message,) = gate((message,), (qkv_sent,))
    for axis, mask in low_stages(low_axes)[:-1]:
        message = jnp.concatenate([message, from_xor(message, axis, mask)], axis=0)
    (message,) = gate((message,), (qkv_sent_last,))
    message = jnp.concatenate([message, from_xor(message, *low_stages(low_axes)[-1])], axis=0)
    messages = (message, swap(message, "x"))
    conds, tables = [], []
    y_first = lax.axis_index("y") == 0
    pair_first = lax.axis_index("pair") == 0
    for message in messages:
        band_hot = (
            message[:, 6 * width].astype(jnp.int32)[:, None]
            == jnp.arange(bands, dtype=jnp.int32)[None, :]
        ).astype(low)
        conds.append(jnp.dot(band_hot, cond_mine, preferred_element_type=wide).astype(low))
        shares = message[:, 6 * width + LANES :].astype(wide).reshape(-1, 2, 2, 2, 2, heads_own * 45)
        shares = shares[:, :, :, 0] + shares[:, :, :, 1]
        shares = jnp.where(pair_first, shares[:, :, 0], shares[:, :, 1])
        shares = jnp.where(
            y_first, shares[:, 0, 0] + shares[:, 1, 1], shares[:, 1, 0] + shares[:, 0, 1]
        )
        tables.append(tree_sum(list(shares)))
    table_sum = (tables[0] + tables[1]).reshape(heads_own, 45)

    weights = (qkv_weight, out_weight, up_weight, down_weight, ada_weight, bias_table)
    bias_update = lamb_direction(bias_table, bias_moment, bias_square, table_sum)
    pad = ((0, 4 - heads_own), (0, LANES - 45))
    bias_sums = jnp.stack(
        [
            jnp.sum(jnp.pad(values * values, pad), axis=0)
            for values in (bias_table, bias_update[2])
        ]
    )
    updates = [
        lamb(qkv_weight, qkv_moment, qkv_square, qkv_terms),
        lamb(out_weight, out_moment, out_square, qkv_terms, qkv_cols),
        lamb(up_weight, up_moment, up_square, up_terms, deps=(qkv_sent_last,)),
        down_update,
        lamb_ada(ada_weight, ada_moment, ada_square, conds, messages, (qkv_sent_last,)),
        (*bias_update, bias_sums),
    ]
    copies = np.array([1.0, 1.0, 1.0, 1.0, 1.0 / model_count, 1.0 / data_count], np.float32)
    norm_sums = jnp.concatenate([update[3] for update in updates], axis=0)
    for axis in low_axes:
        norm_sums = sum_over(norm_sums, axis)
    last_axes = ("x", "y", "pair")
    terms = [norm_sums] + [
        from_xor(norm_sums, last_axes, mask) for mask in range(1, lax.axis_size(last_axes))
    ]
    *fresh, lamb_stats = update_weights(
        terms,
        jnp.asarray(np.repeat(copies, 2)[:, None]),
        weights,
        [update[2] for update in updates],
    )
    outputs = [layer_out, input_grad]
    for new, update in zip(fresh, updates):
        outputs += [new, update[0], update[1]]
    return (*outputs, lamb_stats)


def solution(mesh):
    data_count, model_count = mesh.shape["dp"], mesh.shape["mp"]
    low_sizes = cut_sizes(data_count // 2)
    low_axes = tuple(f"low{at}" for at in range(len(low_sizes)))
    view = Mesh(
        mesh.devices.reshape(*low_sizes, 2, model_count // 2, 2), (*low_axes, "x", "y", "pair")
    )
    data = (*low_axes, "x")
    model = ("y", "pair")
    rows = P((*data, *model), None)
    weight = P(data, model)
    ada = P(data, None)
    table = P(model, None)
    return jax.shard_map(
        partial(shards, low_axes),
        mesh=view,
        in_specs=(
            rows,
            P(data, None),
            P(data),
            P(data),
            P(),
            *([weight] * 12),
            *([ada] * 3),
            *([table] * 3),
        ),
        out_specs=(rows, rows, *([weight] * 12), *([ada] * 3), *([table] * 3), P()),
        check_vma=False,
    )
```

time: 1740 us -> 421 us (0.24)
  waiting for transfers between devices: 1200 us -> 109 us
  matrix products: 239 us -> 3.07 us
  Pallas kernels: 0 us -> 175 us
  blocking collectives: 104 us -> 0 us
  other arithmetic: 96.1 us -> 13.3 us
  starting transfers between devices: 0.84 us -> 79.3 us
  local copies, waits for them, and re-layouts: 68.7 us -> 34.3 us
  between operations: 21.5 us -> 3.46 us
    reduce_scatter x9 -> x0, waiting for transfers between devices: 814 us -> none  [the longest x1 404 us: shards(): lax.psum_scatter(contract_rows(cond_low, grad_mod), 'dp', scatter_dimensi...]
    all_gather x7 -> x0, waiting for transfers between devices: 382 us -> none  [the longest x1 177 us: shards(): lax.all_gather(ada_weight.astype(jnp.bfloat16), 'dp', axis=0, tiled=True)]
    dot_general x72 -> x5, matrix products: 239 us -> 3.07 us  [the longest x1 1.3 us: shards(): mod_bands = jnp.dot(cond_mine, ada_cols, preferred_element_type=wide)]
    pallas_call x0 -> x62, Pallas kernels: none -> 175 us  [call(): pl.pallas_call(body, grid_spec=pltpu.PrefetchScalarGridSpec(num_scalar_pr...]
    ppermute x0 -> x64, waiting for transfers between devices: none -> 109 us  [from_xor(): return lax.ppermute(value, axes, [(at ^ mask, at) for at in range(size)])]
    ppermute x0 -> x64, starting transfers between devices: none -> 79.3 us  [from_xor(): return lax.ppermute(value, axes, [(at ^ mask, at) for at in range(size)])]
    psum x3 -> x0, blocking collectives: 71.1 us -> none  [the longest x1 39.4 us: shards(): norm_sums = lax.psum(jnp.stack([weight_terms, update_terms]), ('dp', 'mp'))]
    reduce_sum x18 -> x2, other arithmetic: 40.4 us -> 0.04 us  [shards(): jnp.sum(jnp.pad(values * values, pad), axis=0)]
  transfers between devices with their start and end apart: 16 -> 64, of which waited for: 15 -> 24; matrix products, arithmetic and copies ran while one was open for 7% -> 5% of each run, Pallas kernels for 0% -> 35%
where the time goes in v1:
time: 421 us; the launch traced here: 417 us
  Pallas kernels  175 us (42%)
  waiting for transfers between devices  109 us (26%)
  starting transfers between devices  79.3 us (19%)
  local copies, waits for them, and re-layouts  34.3 us (8%)
  other arithmetic  13.3 us (3%)
    pallas_call x62, Pallas kernels, call(): pl.pallas_call(body, grid_spec=pltpu.PrefetchScalarGridSpec(num_scalar_pr...  175 us
    ppermute x64, waiting for transfers between devices, from_xor(): return lax.ppermute(value, axes, [(at ^ mask, at) for at in range(size)])  109 us
    ppermute x64, starting transfers between devices, from_xor(): return lax.ppermute(value, axes, [(at ^ mask, at) for at in range(size)])  79.3 us
    unnamed x221, local copies, waits for them, and re-layouts  26.6 us
  transfers between devices with their start and end apart: 64, of which 24 were waited for; matrix products, arithmetic and copies ran while one was open for 5% of the time, Pallas kernels for 35%

profile of v1, /device:TPU:0, one launch (start us, length us, event | category | flops | bytes accessed | tf_op | source)
XLA Modules:
  0.0 416.8 jit_solution(6579305705573490324)
XLA Ops:
  2.7 5.1 %collective-permute-start.1 = (bf16[128,1024]{1,0:T(8,128)(2,1)S(1)}, bf16[128,1024]{1,0:T(8,128)(2,1)S(1)}, u32[]{:S(2)}, u32[]{:S(2)}) collective-permute-start(bf16[128,1024]{1,0:T(8,128)(2,1)S(1)} %pad_maximum_fusion.10.refs_1_), channel_id=1, source_target_pairs={{24,0},{16,8},{8,16},{0,24},{25,1},{17,9},{9,17},{1,25},{26,2},{18... | collective-permute-start | bytes 786440 | tf_op jit(solution)/shard_map/ppermute | solution.py:59
  16.8 5.0 %collective-permute-start.3 = (bf16[256,1024]{1,0:T(8,128)(2,1)S(1)}, bf16[256,1024]{1,0:T(8,128)(2,1)S(1)}, u32[]{:S(2)}, u32[]{:S(2)}) collective-permute-start(bf16[256,1024]{1,0:T(8,128)(2,1)S(1)} %pad_maximum_fusion.6.refs_2_), channel_id=1, source_target_pairs={{8,0},{0,8},{24,16},{16,24},{9,1},{1,9},{25,17},{17,25},{10,2},{2,... | collective-permute-start | bytes 1572872 | tf_op jit(solution)/shard_map/ppermute | solution.py:59
  24.0 8.7 %collective-permute-done.3.refs_1_.refs_0_ = bf16[256,1024]{1,0:T(8,128)(2,1)S(1)} collective-permute-done((bf16[256,1024]{1,0:T(8,128)(2,1)S(1)}, bf16[256,1024]{1,0:T(8,128)(2,1)S(1)}, u32[]{:S(2)}, u32[]{:S(2)}) %collective-permute-start.3) | collective-permute-done | bytes 524320 | tf_op jit(solution)/shard_map/ppermute | solution.py:59
  38.9 6.0 %collective-permute-done.10 = bf16[128,1024]{1,0:T(8,128)(2,1)S(1)} collective-permute-done((bf16[128,1024]{1,0:T(8,128)(2,1)S(1)}, bf16[128,1024]{1,0:T(8,128)(2,1)S(1)}, u32[]{:S(2)}, u32[]{:S(2)}) %collective-permute-start.10) | collective-permute-done | bytes 262176 | tf_op jit(solution)/shard_map/ppermute | solution.py:59
  45.7 9.7 %collective-permute-start.11 = (bf16[256,1024]{1,0:T(8,128)(2,1)}, bf16[256,1024]{1,0:T(8,128)(2,1)}, u32[]{:S(2)}, u32[]{:S(2)}) collective-permute-start(bf16[256,1024]{1,0:T(8,128)(2,1)} %pad_maximum_fusion.7.refs_4_.refs_0_), channel_id=1, source_target_pairs={{8,0},{0,8},{24,16},{16,24},{9,1},{1,9},{25,17},{17,25},{10,2},{2,... | collective-permute-start | bytes 1572872 | tf_op jit(solution)/shard_map/ppermute | solution.py:59
  58.7 3.0 collective-permute-start.8
  61.7 4.9 %shard_map.443 = (f32[8,2,320,320]{3,2,1,0:T(8,128)S(1)}, f32[8,128]{1,0:T(8,128)S(1)}) custom-call(f32[320,24]{1,0:T(8,128)S(1)} %copy-done.56, f32[8,24,320]{2,1,0:T(8,128)S(1)} %copy.92.refs_1_, bf16[512,1024]{1,0:T(8,128)(2,1)S(1)} %shard_map.440.refs_1_.refs_2_, bf16[2,256,1024]{2,1,0:T(8,128)(2,1)} %pad_maximum_fusion.1.refs_2_.refs_3_, ...), custom_call_target="tpu_custom_call" | custom-call | flops 3449999872 | bytes 1 | tf_op jit(solution)/shard_map/pallas_call | solution.py:183
  66.6 3.2 copy-done.83
  77.4 3.5 shard_map.444
  89.1 3.7 shard_map.446.refs_6_
  92.8 3.7 shard_map.447.refs_1_
  96.5 6.9 %shard_map.448 = (bf16[1280,512]{1,0:T(8,128)(2,1)S(1)}, f32[4,4,320]{2,1,0:T(4,128)S(1)}) custom-call(s32[2]{0:T(128)S(1)} %get-tuple-element.246.refs_0_, bf16[1280,1536]{1,0:T(8,128)(2,1)S(1)} %shard_map.447.refs_1_, f32[8,2,320,320]{3,2,1,0:T(8,128)S(1)} %bitcast.88), custom_call_target="tpu_custom_call" | custom-call | flops 8049999872 | bytes 1 | tf_op jit(solution)/shard_map/pallas_call | solution.py:183
  110.4 6.9 %shard_map.449 = (bf16[1280,512]{1,0:T(8,128)(2,1)S(1)}, f32[4,4,320]{2,1,0:T(4,128)S(1)}) custom-call(s32[2]{0:T(128)S(1)} %get-tuple-element.247.refs_0_, bf16[1280,1536]{1,0:T(8,128)(2,1)S(1)} %shard_map.447.refs_1_, f32[8,2,320,320]{3,2,1,0:T(8,128)S(1)} %bitcast.90, ...), custom_call_target="tpu_custom_call", output_to_operand_aliasing={{0}: (3, {})} | custom-call | flops 8049999872 | bytes 1 | tf_op jit(solution)/shard_map/pallas_call | solution.py:183
  125.6 7.1 %collective-permute-done.19.refs_2_.refs_3_ = bf16[512,1024]{1,0:T(8,128)(2,1)S(1)} collective-permute-done((bf16[512,1024]{1,0:T(8,128)(2,1)S(1)}, bf16[512,1024]{1,0:T(8,128)(2,1)S(1)}, u32[]{:S(2)}, u32[]{:S(2)}) %collective-permute-start.19) | collective-permute-done | bytes 1048608 | tf_op jit(solution)/shard_map/ppermute | solution.py:59
  136.3 6.5 %shard_map.456 = (bf16[1280,2048]{1,0:T(8,128)(2,1)S(1)}, bf16[1280,2048]{1,0:T(8,128)(2,1)S(1)}) custom-call(bf16[640,1024]{1,0:T(8,128)(2,1)S(1)} %get-tuple-element.127.refs_0_, bf16[512,1024]{1,0:T(8,128)(2,1)S(1)} %pad_maximum_fusion.2.refs_6_.refs_1_, bf16[256,1024]{1,0:T(8,128)(2,1)} %get-tuple-element.121.refs_6_.refs_1_.refs_2_, ...), custom_call_target="tpu_custom_call" | custom-call | flops 8770666496 | bytes 1 | tf_op jit(solution)/shard_map/pallas_call | solution.py:183
  142.9 4.9 %collective-permute-done.23.refs_0_ = bf16[256,1024]{1,0:T(8,128)(2,1)S(1)} collective-permute-done((bf16[256,1024]{1,0:T(8,128)(2,1)S(1)}, bf16[256,1024]{1,0:T(8,128)(2,1)S(1)}, u32[]{:S(2)}, u32[]{:S(2)}) %collective-permute-start.23) | collective-permute-done | bytes 524320 | tf_op jit(solution)/shard_map/ppermute | solution.py:59
  149.9 7.0 %shard_map.458 = (bf16[1280,2048]{1,0:T(8,128)(2,1)S(1)}, bf16[1280,2048]{1,0:T(8,128)(2,1)S(1)}) custom-call(bf16[640,1024]{1,0:T(8,128)(2,1)S(1)} %collective-permute-done.18.refs_0_.refs_1_, bf16[512,1024]{1,0:T(8,128)(2,1)S(1)} %pad_maximum_fusion.2.refs_6_.refs_1_, ...), custom_call_target="tpu_custom_call", output_to_operand_aliasing={{0}: (6, {}), {1}: (7, {})} | custom-call | flops 8770666496 | bytes 1 | tf_op jit(solution)/shard_map/pallas_call | solution.py:183
  156.9 4.3 %shard_map.460 = (bf16[512,1024]{1,0:T(8,128)(2,1)S(1)}, bf16[256,2048]{1,0:T(8,128)(2,1)S(1)}) custom-call(bf16[1280,1024]{1,0:T(8,128)(2,1)S(1)} %get-tuple-element.133.refs_0_.refs_1_, bf16[1280,1024]{1,0:T(8,128)(2,1)S(1)} %get-tuple-element.133.refs_0_.refs_1_, bf16[1280,2048]{1,0:T(8,128)(2,1)S(1)} %get-tuple-element.132.refs_2_.refs_0_, ...), custom_call_target="tpu_custom_call" | custom-call | flops 3449999872 | bytes 1 | tf_op jit(solution)/shard_map/pallas_call | solution.py:183
  161.3 9.8 %collective-permute-done.25.refs_2_.refs_3_ = bf16[512,1024]{1,0:T(8,128)(2,1)S(1)} collective-permute-done((bf16[512,1024]{1,0:T(8,128)(2,1)S(1)}, bf16[512,1024]{1,0:T(8,128)(2,1)S(1)}, u32[]{:S(2)}, u32[]{:S(2)}) %collective-permute-start.25) | collective-permute-done | bytes 1048608 | tf_op jit(solution)/shard_map/ppermute | solution.py:59
  173.6 3.1 shard_map.462.refs_7_.refs_0_
  176.6 4.2 %shard_map.467 = bf16[640,1024]{1,0:T(8,128)(2,1)S(1)} custom-call(bf16[1280,2048]{1,0:T(8,128)(2,1)S(1)} %shard_map.462.refs_7_.refs_0_, bf16[512,1024]{1,0:T(8,128)(2,1)S(1)} %pad_maximum_fusion.2.refs_6_.refs_1_, bf16[256,1024]{1,0:T(8,128)(2,1)} %get-tuple-element.121.refs_6_.refs_1_.refs_2_, ...), custom_call_target="tpu_custom_call" | custom-call | flops 5400399872 | bytes 1 | tf_op jit(solution)/shard_map/pallas_call | solution.py:183
  180.9 3.1 shard_map.463.refs_0_.refs_2_
  184.0 4.6 %shard_map.464.refs_6_.refs_2_ = f32[640,1024]{1,0:T(8,128)S(1)} custom-call(bf16[1280,2048]{1,0:T(8,128)(2,1)S(1)} %shard_map.463.refs_0_.refs_2_, bf16[512,1024]{1,0:T(8,128)(2,1)S(1)} %pad_maximum_fusion.2.refs_6_.refs_1_, bf16[256,1024]{1,0:T(8,128)(2,1)} %get-tuple-element.121.refs_6_.refs_1_.refs_2_, ...), custom_call_target="tpu_custom_call" | custom-call | flops 5400399872 | bytes 1 | tf_op jit(solution)/shard_map/pallas_call | solution.py:183
  188.6 4.0 shard_map.465.refs_5_
  194.7 4.6 %shard_map.466 = (f32[256,1024]{1,0:T(8,128)S(1)}, f32[256,1024]{1,0:T(8,128)S(1)}, bf16[256,1024]{1,0:T(8,128)(2,1)S(1)}, bf16[256,1024]{1,0:T(8,128)(2,1)S(1)}) custom-call(bf16[1280,1024]{1,0:T(8,128)(2,1)S(1)} %get-tuple-element.133.refs_0_.refs_1_, bf16[1280,1024]{1,0:T(8,128)(2,1)S(1)} %get-tuple-element.133.refs_0_.refs_1_, ...), custom_call_target="tpu_custom_call" | custom-call | flops 4600000000 | bytes 1 | tf_op jit(solution)/shard_map/pallas_call | solution.py:183
  199.5 4.1 shard_map.468
  208.9 2.5 copy-done.13
  214.0 4.3 %shard_map.469 = (bf16[512,1024]{1,0:T(8,128)(2,1)S(1)}, bf16[256,2048]{1,0:T(8,128)(2,1)S(1)}) custom-call(bf16[640,1024]{1,0:T(8,128)(2,1)S(1)} %copy-done.41, bf16[640,1024]{1,0:T(8,128)(2,1)S(1)} %copy-done.44, bf16[1280,2048]{1,0:T(8,128)(2,1)S(1)} %copy-done.13, bf16[640,1024]{1,0:T(8,128)(2,1)} %get-tuple-element.145.refs_3_.refs_0_), custom_call_target="tpu_custom_call" | custom-call | flops 3449999872 | bytes 1 | tf_op jit(solution)/shard_map/pallas_call | solution.py:183
  225.2 9.8 %shard_map.472 = (bf16[1280,1536]{1,0:T(8,128)(2,1)S(1)}, f32[4,128,128]{2,1,0:T(8,128)S(1)}) custom-call(s32[2]{0:T(128)S(1)} %get-tuple-element.246.refs_0_, bf16[1280,1536]{1,0:T(8,128)(2,1)S(1)} %copy-done.75, bf16[1280,512]{1,0:T(8,128)(2,1)S(1)} %shard_map.471.refs_2_, f32[8,2,320,320]{3,2,1,0:T(8,128)S(1)} %bitcast.92, ...), custom_call_target="tpu_custom_call" | custom-call | flops 12650000384 | bytes 1 | tf_op jit(solution)/shard_map/pallas_call | solution.py:183
  235.0 2.5 shard_map.473.refs_4_
  239.2 9.8 %shard_map.475 = (bf16[1280,1536]{1,0:T(8,128)(2,1)S(1)}, f32[4,128,128]{2,1,0:T(8,128)S(1)}) custom-call(s32[2]{0:T(128)S(1)} %get-tuple-element.247.refs_0_, bf16[1280,1536]{1,0:T(8,128)(2,1)S(1)} %copy-done.75, bf16[1280,512]{1,0:T(8,128)(2,1)S(1)} %shard_map.471.refs_2_, f32[8,2,320,320]{3,2,1,0:T(8,128)S(1)} %bitcast.92, ...), custom_call_target="tpu_custom_call", output_to_operand_aliasing={{0}: (6, {})} | custom-call | flops 12650000384 | bytes 1 | tf_op jit(solution)/shard_map/pallas_call | solution.py:183
  249.0 9.6 %shard_map.476 = (bf16[512,1024]{1,0:T(8,128)(2,1)}, bf16[256,2048]{1,0:T(8,128)(2,1)}) custom-call(bf16[640,1024]{1,0:T(8,128)(2,1)} %get-tuple-element.120.refs_0_, bf16[640,1024]{1,0:T(8,128)(2,1)} %collective-permute-done.12.refs_0_.refs_1_, bf16[1280,1536]{1,0:T(8,128)(2,1)S(1)} %get-tuple-element.152.refs_2_.refs_0_, ...), custom_call_target="tpu_custom_call" | custom-call | flops 3449999872 | bytes 1 | tf_op jit(solution)/shard_map/pallas_call | solution.py:183
  262.4 2.4 shard_map.478.refs_5_.refs_2_
  264.9 5.4 %shard_map.479 = (f32[256,1024]{1,0:T(8,128)S(1)}, f32[256,1024]{1,0:T(8,128)S(1)}, bf16[256,1024]{1,0:T(8,128)(2,1)}, bf16[256,1024]{1,0:T(8,128)(2,1)}) custom-call(bf16[640,1024]{1,0:T(8,128)(2,1)S(1)} %copy-done.42, bf16[640,1024]{1,0:T(8,128)(2,1)S(1)} %copy-done.45, bf16[1280,2048]{1,0:T(8,128)(2,1)S(1)} %bitcast.79, ...), custom_call_target="tpu_custom_call" | custom-call | flops 4600000000 | bytes 1 | tf_op jit(solution)/shard_map/pallas_call | solution.py:183
  273.4 4.6 %shard_map.480 = (f32[640,1024]{1,0:T(8,128)}, f32[2,1024]{1,0:T(2,128)S(1)}) custom-call(s32[8]{0:T(128)S(1)} %stack.122.refs_0_, bf16[640,1024]{1,0:T(8,128)(2,1)S(1)} %copy-done.82, f32[640,1024]{1,0:T(8,128)S(1)} %shard_map.478.refs_5_.refs_2_, bf16[640,1024]{1,0:T(8,128)(2,1)S(1)} %collective-permute-done.35.refs_6_.refs_3_, ...), custom_call_target="tpu_custom_call" | custom-call | flops 4600000000 | bytes 1 | tf_op jit(solution)/shard_map/pallas_call | solution.py:183
  280.7 3.1 shard_map.482.refs_2_.refs_1_
  283.9 5.1 %shard_map.483 = (bf16[640,1024]{1,0:T(8,128)(2,1)}, f32[1,1024]{1,0:T(1,128)S(1)}) custom-call(s32[8]{0:T(128)S(1)} %stack.122.refs_0_, f32[640,1024]{1,0:T(8,128)S(1)} %copy-done.64, f32[640,1024]{1,0:T(8,128)S(1)} %shard_map.482.refs_2_.refs_1_, bf16[640,1024]{1,0:T(8,128)(2,1)} %collective-permute-done.33.refs_6_.refs_3_, ...), custom_call_target="tpu_custom_call" | custom-call | flops 4024999936 | bytes 1 | tf_op jit(solution)/shard_map/pallas_call | solution.py:183
  290.0 7.5 %collective-permute-done.41.refs_2_ = bf16[256,1024]{1,0:T(8,128)(2,1)} collective-permute-done((bf16[256,1024]{1,0:T(8,128)(2,1)}, bf16[256,1024]{1,0:T(8,128)(2,1)}, u32[]{:S(2)}, u32[]{:S(2)}) %collective-permute-start.41) | collective-permute-done | bytes 524320 | tf_op jit(solution)/shard_map/ppermute | solution.py:59
  300.7 11.7 %collective-permute-done.43.refs_1_ = bf16[256,1024]{1,0:T(8,128)(2,1)S(1)} collective-permute-done((bf16[256,1024]{1,0:T(8,128)(2,1)S(1)}, bf16[256,1024]{1,0:T(8,128)(2,1)S(1)}, u32[]{:S(2)}, u32[]{:S(2)}) %collective-permute-start.43) | collective-permute-done | bytes 524320 | tf_op jit(solution)/shard_map/ppermute | solution.py:59
  315.9 8.0 %shard_map.486 = (f32[256,1024]{1,0:T(8,128)S(1)}, f32[256,1024]{1,0:T(8,128)S(1)}, bf16[256,1024]{1,0:T(8,128)(2,1)S(1)}, bf16[256,1024]{1,0:T(8,128)(2,1)S(1)}) custom-call(bf16[640,1024]{1,0:T(8,128)(2,1)} %get-tuple-element.120.refs_0_, bf16[640,1024]{1,0:T(8,128)(2,1)} %collective-permute-done.12.refs_0_.refs_1_, bf16[1280,1536]{1,0:T(8,128)(2,1)S(1)} %copy-done.61, ...), custom_call_target="tpu_custom_call" | custom-call | flops 4600000000 | bytes 1 | tf_op jit(solution)/shard_map/pallas_call | solution.py:183
  329.4 10.8 %collective-permute-done.44.refs_2_ = bf16[256,1024]{1,0:T(8,128)(2,1)S(1)} collective-permute-done((bf16[256,1024]{1,0:T(8,128)(2,1)S(1)}, bf16[256,1024]{1,0:T(8,128)(2,1)S(1)}, u32[]{:S(2)}, u32[]{:S(2)}) %collective-permute-start.44) | collective-permute-done | bytes 524320 | tf_op jit(solution)/shard_map/ppermute | solution.py:59
  345.0 2.9 collective-permute-done.51
  347.9 15.2 %collective-permute-done.46.refs_1_ = bf16[256,1024]{1,0:T(8,128)(2,1)S(1)} collective-permute-done((bf16[256,1024]{1,0:T(8,128)(2,1)S(1)}, bf16[256,1024]{1,0:T(8,128)(2,1)S(1)}, u32[]{:S(2)}, u32[]{:S(2)}) %collective-permute-start.46) | collective-permute-done | bytes 524320 | tf_op jit(solution)/shard_map/ppermute | solution.py:59
  367.9 7.3 %collective-permute-done.52 = bf16[8,6992]{1,0:T(8,128)(2,1)S(1)} collective-permute-done((bf16[8,6992]{1,0:T(8,128)(2,1)S(1)}, bf16[8,6992]{1,0:T(8,128)(2,1)S(1)}, u32[]{:S(2)}, u32[]{:S(2)}) %collective-permute-start.52) | collective-permute-done | bytes 111904 | tf_op jit(solution)/shard_map/ppermute | solution.py:59
  379.3 3.8 collective-permute-done.53.refs_6_
  384.4 10.5 %shard_map.496 = (f32[128,6144]{1,0:T(8,128)}, f32[128,6144]{1,0:T(8,128)}, f32[128,6144]{1,0:T(8,128)}, f32[2,128]{1,0:T(2,128)S(1)}) custom-call(f32[128,6144]{1,0:T(8,128)} %refs_13_.1, f32[128,6144]{1,0:T(8,128)} %refs_1_.12, f32[128,6144]{1,0:T(8,128)} %refs_2_.11, bf16[16,128]{1,0:T(8,128)(2,1)S(1)} %convolution_convert_fusion.1.refs_3_, ...), custom_call_target="tpu_custom_call" | custom-call | flops 9200000000 | bytes 1 | tf_op jit(solution)/shard_map/pallas_call | solution.py:183
  395.0 2.5 collective-permute-start.56
  410.2 6.4 %shard_map.497 = (f32[128,768]{1,0:T(8,128)}, f32[128,256]{1,0:T(8,128)}, f32[128,1024]{1,0:T(8,128)}, f32[128,1024]{1,0:T(8,128)}, f32[128,6144]{1,0:T(8,128)}, /*index=5*/f32[4,45]{1,0:T(4,128)}, f32[3,6]{1,0:T(4,128)}) custom-call(f32[12,1]{1,0:T(8,128)S(1)} %copy-done.58, f32[12,128]{1,0:T(8,128)S(1)} %add_add_fusion.refs_1_, ...), custom_call_target="tpu_custom_call" | custom-call | flops 5750000128 | bytes 1 | tf_op jit(solution)/shard_map/pallas_call | solution.py:183
  (471 shorter events, 130.3 us)
Async XLA Ops:
  2.7 11.8 %collective-permute-start.1 = (bf16[128,1024]{1,0:T(8,128)(2,1)S(1)}, bf16[128,1024]{1,0:T(8,128)(2,1)S(1)}, u32[]{:S(2)}, u32[]{:S(2)}) collective-permute-start(bf16[128,1024]{1,0:T(8,128)(2,1)S(1)} %pad_maximum_fusion.10.refs_1_), channel_id=1, source_target_pairs={{24,0},{16,8},{8,16},{0,24},{25,1},{17,9},{9,17},{1,25},{26,2},{18... | collective-permute-start | bytes 786440 | tf_op jit(solution)/shard_map/ppermute | solution.py:59
  15.2 8.6 %collective-permute-start.2 = (f32[8,1536]{1,0:T(8,128)S(1)}, f32[8,1536]{1,0:T(8,128)S(1)}, u32[]{:S(2)}, u32[]{:S(2)}) collective-permute-start(f32[8,1536]{1,0:T(8,128)S(1)} %get-tuple-element.116), channel_id=1, source_target_pairs={{2,0},{0,2},{3,1},{1,3},{6,4},{4,6},{7,5},{5,7},{10,8},{8,10},{11,... | collective-permute-start | bytes 147464 | tf_op jit(solution)/shard_map/ppermute | solution.py:59
  16.8 16.0 %collective-permute-start.3 = (bf16[256,1024]{1,0:T(8,128)(2,1)S(1)}, bf16[256,1024]{1,0:T(8,128)(2,1)S(1)}, u32[]{:S(2)}, u32[]{:S(2)}) collective-permute-start(bf16[256,1024]{1,0:T(8,128)(2,1)S(1)} %pad_maximum_fusion.6.refs_2_), channel_id=1, source_target_pairs={{8,0},{0,8},{24,16},{16,24},{9,1},{1,9},{25,17},{17,25},{10,2},{2,... | collective-permute-start | bytes 1572872 | tf_op jit(solution)/shard_map/ppermute | solution.py:59
  21.8 16.4 %collective-permute-start.6 = (bf16[256,1024]{1,0:T(8,128)(2,1)S(1)}, bf16[256,1024]{1,0:T(8,128)(2,1)S(1)}, u32[]{:S(2)}, u32[]{:S(2)}) collective-permute-start(bf16[256,1024]{1,0:T(8,128)(2,1)S(1)} %pad_maximum_fusion.6.refs_2_), channel_id=1, source_target_pairs={{4,0},{0,4},{5,1},{1,5},{6,2},{2,6},{7,3},{3,7},{12,8},{8,12},{13,... | collective-permute-start | bytes 1572872 | tf_op jit(solution)/shard_map/ppermute | solution.py:59
  23.3 9.5 %collective-permute-start.9 = (f32[4,45]{1,0:T(4,128)S(1)}, f32[4,45]{1,0:T(4,128)S(1)}, u32[]{:S(2)}, u32[]{:S(2)}) collective-permute-start(f32[4,45]{1,0:T(4,128)S(1)} %get-tuple-element.117), channel_id=1, source_target_pairs={{2,0},{0,2},{3,1},{1,3},{6,4},{4,6},{7,5},{5,7},{10,8},{8,10},{11,... | collective-permute-start | bytes 2168 | tf_op jit(solution)/shard_map/ppermute | solution.py:59
  33.8 11.1 %collective-permute-start.10 = (bf16[128,1024]{1,0:T(8,128)(2,1)S(1)}, bf16[128,1024]{1,0:T(8,128)(2,1)S(1)}, u32[]{:S(2)}, u32[]{:S(2)}) collective-permute-start(bf16[128,1024]{1,0:T(8,128)(2,1)S(1)} %shard_map.442), channel_id=1, source_target_pairs={{24,0},{16,8},{8,16},{0,24},{25,1},{17,9},{9,17},{1,25},{26,2},{18... | collective-permute-start | bytes 786440 | tf_op jit(solution)/shard_map/ppermute | solution.py:59
  36.6 18.8 %collective-permute-start.5 = (f32[8,2,2,1536]{3,2,1,0:T(2,128)S(1)}, f32[8,2,2,1536]{3,2,1,0:T(2,128)S(1)}, u32[]{:S(2)}, u32[]{:S(2)}) collective-permute-start(f32[8,2,2,1536]{3,2,1,0:T(2,128)S(1)} %pad_maximum_fusion.11), channel_id=1, source_target_pairs={{24,0},{16,8},{8,16},{0,24},{25,1},{17,9},{9,17},{1,25},{26,2},{18... | collective-permute-start | bytes 589832 | tf_op jit(solution)/shard_map/ppermute | solution.py:59
  38.3 17.3 %collective-permute-start.7 = (bf16[256,1024]{1,0:T(8,128)(2,1)S(1)}, bf16[256,1024]{1,0:T(8,128)(2,1)S(1)}, u32[]{:S(2)}, u32[]{:S(2)}) collective-permute-start(bf16[256,1024]{1,0:T(8,128)(2,1)S(1)} %shard_map.439.refs_2_), channel_id=1, source_target_pairs={{2,0},{0,2},{3,1},{1,3},{6,4},{4,6},{7,5},{5,7},{10,8},{8,10},{11,... | collective-permute-start | bytes 1572872 | tf_op jit(solution)/shard_map/ppermute | solution.py:59
  45.7 30.4 %collective-permute-start.11 = (bf16[256,1024]{1,0:T(8,128)(2,1)}, bf16[256,1024]{1,0:T(8,128)(2,1)}, u32[]{:S(2)}, u32[]{:S(2)}) collective-permute-start(bf16[256,1024]{1,0:T(8,128)(2,1)} %pad_maximum_fusion.7.refs_4_.refs_0_), channel_id=1, source_target_pairs={{8,0},{0,8},{24,16},{16,24},{9,1},{1,9},{25,17},{17,25},{10,2},{2,... | collective-permute-start | bytes 1572872 | tf_op jit(solution)/shard_map/ppermute | solution.py:59
  55.6 28.2 %collective-permute-start.13 = (bf16[512,1024]{1,0:T(8,128)(2,1)S(1)}, bf16[512,1024]{1,0:T(8,128)(2,1)S(1)}, u32[]{:S(2)}, u32[]{:S(2)}) collective-permute-start(bf16[512,1024]{1,0:T(8,128)(2,1)S(1)} %shard_map.440.refs_1_.refs_2_), channel_id=1, source_target_pairs={{2,0},{0,2},{3,1},{1,3},{6,4},{4,6},{7,5},{5,7},{10,8},{8,10},{11,... | collective-permute-start | bytes 3145736 | tf_op jit(solution)/shard_map/ppermute | solution.py:59
  57.2 26.5 %collective-permute-start.14 = (bf16[2,256,1024]{2,1,0:T(8,128)(2,1)}, bf16[2,256,1024]{2,1,0:T(8,128)(2,1)S(1)}, u32[]{:S(2)}, u32[]{:S(2)}) collective-permute-start(bf16[2,256,1024]{2,1,0:T(8,128)(2,1)} %pad_maximum_fusion.1.refs_2_.refs_3_), channel_id=1, source_target_pairs={{4,0},{0,4},{5,1},{1,5},{6,2},{2,6},{7,3},{3,7},{12,8},{8,12},{13,... | collective-permute-start | bytes 3145736 | tf_op jit(solution)/shard_map/ppermute | solution.py:59
  58.7 12.5 %collective-permute-start.8 = (f32[8,2,2,1536]{3,2,1,0:T(2,128)S(1)}, f32[8,2,2,1536]{3,2,1,0:T(2,128)S(1)}, u32[]{:S(2)}, u32[]{:S(2)}) collective-permute-start(f32[8,2,2,1536]{3,2,1,0:T(2,128)S(1)} %shard_map.441), channel_id=1, source_target_pairs={{8,0},{0,8},{24,16},{16,24},{9,1},{1,9},{25,17},{17,25},{10,2},{2,... | collective-permute-start | bytes 589832 | tf_op jit(solution)/shard_map/ppermute | solution.py:59
  81.9 10.9 %collective-permute-start.12 = (bf16[640,1024]{1,0:T(8,128)(2,1)}, bf16[640,1024]{1,0:T(8,128)(2,1)}, u32[]{:S(2)}, u32[]{:S(2)}) collective-permute-start(bf16[640,1024]{1,0:T(8,128)(2,1)} %get-tuple-element.120.refs_0_), channel_id=1, source_target_pairs={{1,0},{0,1},{3,2},{2,3},{5,4},{4,5},{7,6},{6,7},{9,8},{8,9},{11,10... | collective-permute-start | bytes 3932168 | tf_op jit(solution)/shard_map/ppermute | solution.py:59
  84.8 18.6 %collective-permute-start.15 = (bf16[256,1024]{1,0:T(8,128)(2,1)}, bf16[256,1024]{1,0:T(8,128)(2,1)S(1)}, u32[]{:S(2)}, u32[]{:S(2)}) collective-permute-start(bf16[256,1024]{1,0:T(8,128)(2,1)} %get-tuple-element.125), channel_id=1, source_target_pairs={{4,0},{0,4},{5,1},{1,5},{6,2},{2,6},{7,3},{3,7},{12,8},{8,12},{13,... | collective-permute-start | bytes 1572872 | tf_op jit(solution)/shard_map/ppermute | solution.py:59
  86.3 18.5 %collective-permute-start.16 = (bf16[256,1024]{1,0:T(8,128)(2,1)}, bf16[256,1024]{1,0:T(8,128)(2,1)S(1)}, u32[]{:S(2)}, u32[]{:S(2)}) collective-permute-start(bf16[256,1024]{1,0:T(8,128)(2,1)} %get-tuple-element.121.refs_6_.refs_1_.refs_2_), channel_id=1, source_target_pairs={{2,0},{0,2},{3,1},{1,3},{6,4},{4,6},{7,5},{5,7},{10,8},{8,10},{11,... | collective-permute-start | bytes 1572872 | tf_op jit(solution)/shard_map/ppermute | solution.py:59
  86.8 19.2 %collective-permute-start.21 = (bf16[128,1024]{1,0:T(8,128)(2,1)S(1)}, bf16[128,1024]{1,0:T(8,128)(2,1)S(1)}, u32[]{:S(2)}, u32[]{:S(2)}) collective-permute-start(bf16[128,1024]{1,0:T(8,128)(2,1)S(1)} %shard_map.454), channel_id=1, source_target_pairs={{24,0},{16,8},{8,16},{0,24},{25,1},{17,9},{9,17},{1,25},{26,2},{18... | collective-permute-start | bytes 786440 | tf_op jit(solution)/shard_map/ppermute | solution.py:59
  105.9 12.5 %collective-permute-start.17 = (bf16[640,1024]{1,0:T(8,128)(2,1)S(1)}, bf16[640,1024]{1,0:T(8,128)(2,1)S(1)}, u32[]{:S(2)}, u32[]{:S(2)}) collective-permute-start(bf16[640,1024]{1,0:T(8,128)(2,1)S(1)} %shard_map.452), channel_id=1, source_target_pairs={{1,0},{0,1},{3,2},{2,3},{5,4},{4,5},{7,6},{6,7},{9,8},{8,9},{11,10... | collective-permute-start | bytes 3932168 | tf_op jit(solution)/shard_map/ppermute | solution.py:59
  106.1 19.5 %collective-permute-start.22 = (bf16[256,1024]{1,0:T(8,128)(2,1)S(1)}, bf16[256,1024]{1,0:T(8,128)(2,1)S(1)}, u32[]{:S(2)}, u32[]{:S(2)}) collective-permute-start(bf16[256,1024]{1,0:T(8,128)(2,1)S(1)} %pad_maximum_fusion.8.refs_0_), channel_id=1, source_target_pairs={{8,0},{0,8},{24,16},{16,24},{9,1},{1,9},{25,17},{17,25},{10,2},{2,... | collective-permute-start | bytes 1572872 | tf_op jit(solution)/shard_map/ppermute | solution.py:59
  107.4 25.3 %collective-permute-start.19 = (bf16[512,1024]{1,0:T(8,128)(2,1)S(1)}, bf16[512,1024]{1,0:T(8,128)(2,1)S(1)}, u32[]{:S(2)}, u32[]{:S(2)}) collective-permute-start(bf16[512,1024]{1,0:T(8,128)(2,1)S(1)} %pad_maximum_fusion.2.refs_6_.refs_1_), channel_id=1, source_target_pairs={{2,0},{0,2},{3,1},{1,3},{6,4},{4,6},{7,5},{5,7},{10,8},{8,10},{11,... | collective-permute-start | bytes 3145736 | tf_op jit(solution)/shard_map/ppermute | solution.py:59
  109.8 25.1 %collective-permute-start.20 = (bf16[2,256,1024]{2,1,0:T(8,128)(2,1)S(1)}, bf16[2,256,1024]{2,1,0:T(8,128)(2,1)S(1)}, u32[]{:S(2)}, u32[]{:S(2)}) collective-permute-start(bf16[2,256,1024]{2,1,0:T(8,128)(2,1)S(1)} %pad_maximum_fusion.3), channel_id=1, source_target_pairs={{4,0},{0,4},{5,1},{1,5},{6,2},{2,6},{7,3},{3,7},{12,8},{8,12},{13,... | collective-permute-start | bytes 3145736 | tf_op jit(solution)/shard_map/ppermute | solution.py:59
  123.6 26.3 %collective-permute-start.18 = (bf16[640,1024]{1,0:T(8,128)(2,1)S(1)}, bf16[640,1024]{1,0:T(8,128)(2,1)S(1)}, u32[]{:S(2)}, u32[]{:S(2)}) collective-permute-start(bf16[640,1024]{1,0:T(8,128)(2,1)S(1)} %get-tuple-element.127.refs_0_), channel_id=1, source_target_pairs={{1,0},{0,1},{3,2},{2,3},{5,4},{4,5},{7,6},{6,7},{9,8},{8,9},{11,10... | collective-permute-start | bytes 3932168 | tf_op jit(solution)/shard_map/ppermute | solution.py:59
  134.8 12.9 %collective-permute-start.23 = (bf16[256,1024]{1,0:T(8,128)(2,1)S(1)}, bf16[256,1024]{1,0:T(8,128)(2,1)S(1)}, u32[]{:S(2)}, u32[]{:S(2)}) collective-permute-start(bf16[256,1024]{1,0:T(8,128)(2,1)S(1)} %get-tuple-element.131), channel_id=1, source_target_pairs={{4,0},{0,4},{5,1},{1,5},{6,2},{2,6},{7,3},{3,7},{12,8},{8,12},{13,... | collective-permute-start | bytes 1572872 | tf_op jit(solution)/shard_map/ppermute | solution.py:59
  135.4 13.5 %collective-permute-start.24 = (bf16[256,1024]{1,0:T(8,128)(2,1)S(1)}, bf16[256,1024]{1,0:T(8,128)(2,1)S(1)}, u32[]{:S(2)}, u32[]{:S(2)}) collective-permute-start(bf16[256,1024]{1,0:T(8,128)(2,1)S(1)} %get-tuple-element.128.refs_6_.refs_2_), channel_id=1, source_target_pairs={{2,0},{0,2},{3,1},{1,3},{6,4},{4,6},{7,5},{5,7},{10,8},{8,10},{11,... | collective-permute-start | bytes 1572872 | tf_op jit(solution)/shard_map/ppermute | solution.py:59
  147.8 23.3 %collective-permute-start.25 = (bf16[512,1024]{1,0:T(8,128)(2,1)S(1)}, bf16[512,1024]{1,0:T(8,128)(2,1)S(1)}, u32[]{:S(2)}, u32[]{:S(2)}) collective-permute-start(bf16[512,1024]{1,0:T(8,128)(2,1)S(1)} %pad_maximum_fusion.4.refs_8_.refs_3_.refs_1_), channel_id=1, source_target_pairs={{2,0},{0,2},{3,1},{1,3},{6,4},{4,6},{7,5},{5,7},{10,8},{8,10},{11,... | collective-permute-start | bytes 3145736 | tf_op jit(solution)/shard_map/ppermute | solution.py:59
  149.0 23.0 %collective-permute-start.26 = (bf16[2,256,1024]{2,1,0:T(8,128)(2,1)S(1)}, bf16[2,256,1024]{2,1,0:T(8,128)(2,1)S(1)}, u32[]{:S(2)}, u32[]{:S(2)}) collective-permute-start(bf16[2,256,1024]{2,1,0:T(8,128)(2,1)S(1)} %pad_maximum_fusion.5), channel_id=1, source_target_pairs={{4,0},{0,4},{5,1},{1,5},{6,2},{2,6},{7,3},{3,7},{12,8},{8,12},{13,... | collective-permute-start | bytes 3145736 | tf_op jit(solution)/shard_map/ppermute | solution.py:59
  172.0 22.2 %collective-permute-start.27 = (bf16[512,1024]{1,0:T(8,128)(2,1)S(1)}, bf16[512,1024]{1,0:T(8,128)(2,1)S(1)}, u32[]{:S(2)}, u32[]{:S(2)}) collective-permute-start(bf16[512,1024]{1,0:T(8,128)(2,1)S(1)} %get-tuple-element.136.refs_7_), channel_id=1, source_target_pairs={{2,0},{0,2},{3,1},{1,3},{6,4},{4,6},{7,5},{5,7},{10,8},{8,10},{11,... | collective-permute-start | bytes 3145736 | tf_op jit(solution)/shard_map/ppermute | solution.py:59
  173.0 21.7 %collective-permute-start.28 = (bf16[256,2048]{1,0:T(8,128)(2,1)S(1)}, bf16[256,2048]{1,0:T(8,128)(2,1)S(1)}, u32[]{:S(2)}, u32[]{:S(2)}) collective-permute-start(bf16[256,2048]{1,0:T(8,128)(2,1)S(1)} %get-tuple-element.137), channel_id=1, source_target_pairs={{4,0},{0,4},{5,1},{1,5},{6,2},{2,6},{7,3},{3,7},{12,8},{8,12},{13,... | collective-permute-start | bytes 3145736 | tf_op jit(solution)/shard_map/ppermute | solution.py:59
  180.8 18.6 %collective-permute-start.31 = (bf16[640,1024]{1,0:T(8,128)(2,1)S(1)}, bf16[640,1024]{1,0:T(8,128)(2,1)S(1)}, u32[]{:S(2)}, u32[]{:S(2)}) collective-permute-start(bf16[640,1024]{1,0:T(8,128)(2,1)S(1)} %shard_map.467), channel_id=1, source_target_pairs={{1,0},{0,1},{3,2},{2,3},{5,4},{4,5},{7,6},{6,7},{9,8},{8,9},{11,10... | collective-permute-start | bytes 3932168 | tf_op jit(solution)/shard_map/ppermute | solution.py:59
  205.1 16.6 %collective-permute-start.32 = (bf16[640,1024]{1,0:T(8,128)(2,1)}, bf16[640,1024]{1,0:T(8,128)(2,1)}, u32[]{:S(2)}, u32[]{:S(2)}) collective-permute-start(bf16[640,1024]{1,0:T(8,128)(2,1)} %get-tuple-element.145.refs_3_.refs_0_), channel_id=1, source_target_pairs={{1,0},{0,1},{3,2},{2,3},{5,4},{4,5},{7,6},{6,7},{9,8},{8,9},{11,10... | collective-permute-start | bytes 3932168 | tf_op jit(solution)/shard_map/ppermute | solution.py:59
  205.1 20.0 %collective-permute-start.33 = (bf16[640,1024]{1,0:T(8,128)(2,1)}, bf16[640,1024]{1,0:T(8,128)(2,1)}, u32[]{:S(2)}, u32[]{:S(2)}) collective-permute-start(bf16[640,1024]{1,0:T(8,128)(2,1)} %shard_map.465.refs_5_), channel_id=1, source_target_pairs={{1,0},{0,1},{3,2},{2,3},{5,4},{4,5},{7,6},{6,7},{9,8},{8,9},{11,10... | collective-permute-start | bytes 3932168 | tf_op jit(solution)/shard_map/ppermute | solution.py:59
  206.9 30.7 %collective-permute-start.29 = (bf16[256,1024]{1,0:T(8,128)(2,1)}, bf16[256,1024]{1,0:T(8,128)(2,1)S(1)}, u32[]{:S(2)}, u32[]{:S(2)}) collective-permute-start(bf16[256,1024]{1,0:T(8,128)(2,1)} %copy-done.51), channel_id=1, source_target_pairs={{4,0},{0,4},{5,1},{1,5},{6,2},{2,6},{7,3},{3,7},{12,8},{8,12},{13,... | collective-permute-start | bytes 1572872 | tf_op jit(solution)/shard_map/ppermute | solution.py:59
  207.9 29.7 %collective-permute-start.30 = (bf16[256,1024]{1,0:T(8,128)(2,1)}, bf16[256,1024]{1,0:T(8,128)(2,1)S(1)}, u32[]{:S(2)}, u32[]{:S(2)}) collective-permute-start(bf16[256,1024]{1,0:T(8,128)(2,1)} %copy-done.50), channel_id=1, source_target_pairs={{2,0},{0,2},{3,1},{1,3},{6,4},{4,6},{7,5},{5,7},{10,8},{8,10},{11,... | collective-permute-start | bytes 1572872 | tf_op jit(solution)/shard_map/ppermute | solution.py:59
  218.3 46.5 %collective-permute-start.37 = (bf16[512,1024]{1,0:T(8,128)(2,1)S(1)}, bf16[512,1024]{1,0:T(8,128)(2,1)S(1)}, u32[]{:S(2)}, u32[]{:S(2)}) collective-permute-start(bf16[512,1024]{1,0:T(8,128)(2,1)S(1)} %get-tuple-element.146.refs_6_), channel_id=1, source_target_pairs={{2,0},{0,2},{3,1},{1,3},{6,4},{4,6},{7,5},{5,7},{10,8},{8,10},{11,... | collective-permute-start | bytes 3145736 | tf_op jit(solution)/shard_map/ppermute | solution.py:59
  221.8 43.1 %collective-permute-start.38 = (bf16[256,2048]{1,0:T(8,128)(2,1)S(1)}, bf16[256,2048]{1,0:T(8,128)(2,1)S(1)}, u32[]{:S(2)}, u32[]{:S(2)}) collective-permute-start(bf16[256,2048]{1,0:T(8,128)(2,1)S(1)} %get-tuple-element.157), channel_id=1, source_target_pairs={{4,0},{0,4},{5,1},{1,5},{6,2},{2,6},{7,3},{3,7},{12,8},{8,12},{13,... | collective-permute-start | bytes 3145736 | tf_op jit(solution)/shard_map/ppermute | solution.py:59
  237.5 11.5 %collective-permute-start.35 = (bf16[640,1024]{1,0:T(8,128)(2,1)S(1)}, bf16[640,1024]{1,0:T(8,128)(2,1)S(1)}, u32[]{:S(2)}, u32[]{:S(2)}) collective-permute-start(bf16[640,1024]{1,0:T(8,128)(2,1)S(1)} %shard_map.473.refs_4_), channel_id=1, source_target_pairs={{1,0},{0,1},{3,2},{2,3},{5,4},{4,5},{7,6},{6,7},{9,8},{8,9},{11,10... | collective-permute-start | bytes 3932168 | tf_op jit(solution)/shard_map/ppermute | solution.py:59
  237.9 21.6 %collective-permute-start.34 = (bf16[256,1024]{1,0:T(8,128)(2,1)S(1)}, bf16[256,1024]{1,0:T(8,128)(2,1)S(1)}, u32[]{:S(2)}, u32[]{:S(2)}) collective-permute-start(bf16[256,1024]{1,0:T(8,128)(2,1)S(1)} %get-tuple-element.150.refs_7_), channel_id=1, source_target_pairs={{8,0},{0,8},{24,16},{16,24},{9,1},{1,9},{25,17},{17,25},{10,2},{2,... | collective-permute-start | bytes 1572872 | tf_op jit(solution)/shard_map/ppermute | solution.py:59
  258.5 54.0 %collective-permute-start.39 = (bf16[512,1024]{1,0:T(8,128)(2,1)}, bf16[512,1024]{1,0:T(8,128)(2,1)}, u32[]{:S(2)}, u32[]{:S(2)}) collective-permute-start(bf16[512,1024]{1,0:T(8,128)(2,1)} %get-tuple-element.153.refs_2_), channel_id=1, source_target_pairs={{2,0},{0,2},{3,1},{1,3},{6,4},{4,6},{7,5},{5,7},{10,8},{8,10},{11,... | collective-permute-start | bytes 3145736 | tf_op jit(solution)/shard_map/ppermute | solution.py:59
  259.6 18.4 %collective-permute-start.36 = (bf16[128,1024]{1,0:T(8,128)(2,1)S(1)}, bf16[128,1024]{1,0:T(8,128)(2,1)S(1)}, u32[]{:S(2)}, u32[]{:S(2)}) collective-permute-start(bf16[128,1024]{1,0:T(8,128)(2,1)S(1)} %get-tuple-element.155.refs_6_), channel_id=1, source_target_pairs={{24,0},{16,8},{8,16},{0,24},{25,1},{17,9},{9,17},{1,25},{26,2},{18... | collective-permute-start | bytes 786440 | tf_op jit(solution)/shard_map/ppermute | solution.py:59
  261.2 51.4 %collective-permute-start.40 = (bf16[256,2048]{1,0:T(8,128)(2,1)}, bf16[256,2048]{1,0:T(8,128)(2,1)}, u32[]{:S(2)}, u32[]{:S(2)}) collective-permute-start(bf16[256,2048]{1,0:T(8,128)(2,1)} %get-tuple-element.163), channel_id=1, source_target_pairs={{4,0},{0,4},{5,1},{1,5},{6,2},{2,6},{7,3},{3,7},{12,8},{8,12},{13,... | collective-permute-start | bytes 3145736 | tf_op jit(solution)/shard_map/ppermute | solution.py:59
  271.3 26.2 %collective-permute-start.41 = (bf16[256,1024]{1,0:T(8,128)(2,1)}, bf16[256,1024]{1,0:T(8,128)(2,1)}, u32[]{:S(2)}, u32[]{:S(2)}) collective-permute-start(bf16[256,1024]{1,0:T(8,128)(2,1)} %get-tuple-element.158.refs_6_), channel_id=1, source_target_pairs={{4,0},{0,4},{5,1},{1,5},{6,2},{2,6},{7,3},{3,7},{12,8},{8,12},{13,... | collective-permute-start | bytes 1572872 | tf_op jit(solution)/shard_map/ppermute | solution.py:59
  272.2 25.3 %collective-permute-start.42 = (bf16[256,1024]{1,0:T(8,128)(2,1)}, bf16[256,1024]{1,0:T(8,128)(2,1)}, u32[]{:S(2)}, u32[]{:S(2)}) collective-permute-start(bf16[256,1024]{1,0:T(8,128)(2,1)} %get-tuple-element.166), channel_id=1, source_target_pairs={{2,0},{0,2},{3,1},{1,3},{6,4},{4,6},{7,5},{5,7},{10,8},{8,10},{11,... | collective-permute-start | bytes 1572872 | tf_op jit(solution)/shard_map/ppermute | solution.py:59
  299.8 12.6 %collective-permute-start.43 = (bf16[256,1024]{1,0:T(8,128)(2,1)S(1)}, bf16[256,1024]{1,0:T(8,128)(2,1)S(1)}, u32[]{:S(2)}, u32[]{:S(2)}) collective-permute-start(bf16[256,1024]{1,0:T(8,128)(2,1)S(1)} %get-tuple-element.169), channel_id=1, source_target_pairs={{8,0},{0,8},{24,16},{16,24},{9,1},{1,9},{25,17},{17,25},{10,2},{2,... | collective-permute-start | bytes 1572872 | tf_op jit(solution)/shard_map/ppermute | solution.py:59
  326.5 13.7 %collective-permute-start.44 = (bf16[256,1024]{1,0:T(8,128)(2,1)S(1)}, bf16[256,1024]{1,0:T(8,128)(2,1)S(1)}, u32[]{:S(2)}, u32[]{:S(2)}) collective-permute-start(bf16[256,1024]{1,0:T(8,128)(2,1)S(1)} %get-tuple-element.173.refs_1_), channel_id=1, source_target_pairs={{4,0},{0,4},{5,1},{1,5},{6,2},{2,6},{7,3},{3,7},{12,8},{8,12},{13,... | collective-permute-start | bytes 1572872 | tf_op jit(solution)/shard_map/ppermute | solution.py:59
  327.4 13.4 %collective-permute-start.45 = (bf16[256,1024]{1,0:T(8,128)(2,1)S(1)}, bf16[256,1024]{1,0:T(8,128)(2,1)S(1)}, u32[]{:S(2)}, u32[]{:S(2)}) collective-permute-start(bf16[256,1024]{1,0:T(8,128)(2,1)S(1)} %get-tuple-element.174), channel_id=1, source_target_pairs={{2,0},{0,2},{3,1},{1,3},{6,4},{4,6},{7,5},{5,7},{10,8},{8,10},{11,... | collective-permute-start | bytes 1572872 | tf_op jit(solution)/shard_map/ppermute | solution.py:59
  343.4 22.1 %collective-permute-start.48 = (bf16[128,1024]{1,0:T(8,128)(2,1)S(1)}, bf16[128,1024]{1,0:T(8,128)(2,1)S(1)}, u32[]{:S(2)}, u32[]{:S(2)}) collective-permute-start(bf16[128,1024]{1,0:T(8,128)(2,1)S(1)} %get-tuple-element.170.refs_8_), channel_id=1, source_target_pairs={{24,0},{16,8},{8,16},{0,24},{25,1},{17,9},{9,17},{1,25},{26,2},{18... | collective-permute-start | bytes 786440 | tf_op jit(solution)/shard_map/ppermute | solution.py:59
  345.0 18.2 %collective-permute-start.46 = (bf16[256,1024]{1,0:T(8,128)(2,1)S(1)}, bf16[256,1024]{1,0:T(8,128)(2,1)S(1)}, u32[]{:S(2)}, u32[]{:S(2)}) collective-permute-start(bf16[256,1024]{1,0:T(8,128)(2,1)S(1)} %get-tuple-element.176.refs_1_), channel_id=1, source_target_pairs={{8,0},{0,8},{24,16},{16,24},{9,1},{1,9},{25,17},{17,25},{10,2},{2,... | collective-permute-start | bytes 1572872 | tf_op jit(solution)/shard_map/ppermute | solution.py:59
  363.3 13.7 %collective-permute-start.47 = (bf16[128,1024]{1,0:T(8,128)(2,1)S(1)}, bf16[128,1024]{1,0:T(8,128)(2,1)S(1)}, u32[]{:S(2)}, u32[]{:S(2)}) collective-permute-start(bf16[128,1024]{1,0:T(8,128)(2,1)S(1)} %get-tuple-element.178.refs_5_.refs_1_.refs_7_), channel_id=1, source_target_pairs={{24,0},{16,8},{8,16},{0,24},{25,1},{17,9},{9,17},{1,25},{26,2},{18... | collective-permute-start | bytes 786440 | tf_op jit(solution)/shard_map/ppermute | solution.py:59
  365.5 9.7 %collective-permute-start.52 = (bf16[8,6992]{1,0:T(8,128)(2,1)S(1)}, bf16[8,6992]{1,0:T(8,128)(2,1)S(1)}, u32[]{:S(2)}, u32[]{:S(2)}) collective-permute-start(bf16[8,6992]{1,0:T(8,128)(2,1)S(1)} %shard_map.495), channel_id=1, source_target_pairs={{8,0},{0,8},{24,16},{16,24},{9,1},{1,9},{25,17},{17,25},{10,2},{2,... | collective-permute-start | bytes 335624 | tf_op jit(solution)/shard_map/ppermute | solution.py:59
  (126 other events, 929.0 us)

commit v2 on v1

--- a/solution.py
+++ b/solution.py
@@ -1285,7 +1285,8 @@
     qkv_kept, qkv_sent = kept_gradient(qkv_product, qkv_moved, (up_sent,))
     qkv_sent_second = qkv_sent[0]
     qkv_moved = swap(qkv_sent[0], "x"), swap(qkv_sent[1], "y")
-    qkv_kept, qkv_sent = third_gradient(qkv_kept, qkv_moved)
+    up_update = lamb(up_weight, up_moment, up_square, up_terms, deps=(qkv_sent_second,))
+    qkv_kept, qkv_sent = third_gradient(qkv_kept, qkv_moved, (up_update[3],))
     qkv_moved = from_xor(qkv_sent, *low_stage)
     qkv_terms, qkv_sent_last = fourth_gradient(qkv_kept, qkv_moved, low_axes)
 
@@ -1308,10 +1309,9 @@
     (message,) = gate((message,), (qkv_sent_second,))
     message = in_order(in_order(message, "pair", 0), "y", 0)
     (message,) = gate((message,), (qkv_sent,))
-    for axis, mask in low_stages(low_axes)[:-1]:
+    for axis, mask in low_stages(low_axes):
         message = jnp.concatenate([message, from_xor(message, axis, mask)], axis=0)
     (message,) = gate((message,), (qkv_sent_last,))
-    message = jnp.concatenate([message, from_xor(message, *low_stages(low_axes)[-1])], axis=0)
     messages = (message, swap(message, "x"))
     conds, tables = [], []
     y_first = lax.axis_index("y") == 0
@@ -1343,7 +1343,7 @@
     updates = [
         lamb(qkv_weight, qkv_moment, qkv_square, qkv_terms),
         lamb(out_weight, out_moment, out_square, qkv_terms, qkv_cols),
-        lamb(up_weight, up_moment, up_square, up_terms, deps=(qkv_sent_last,)),
+        up_update,
         down_update,
         lamb_ada(ada_weight, ada_moment, ada_square, conds, messages, (qkv_sent_last,)),
         (*bias_update, bias_sums),

time: 421 us -> 412 us (0.979)
  waiting for transfers between devices: 109 us -> 98.1 us
    ppermute x64, waiting for transfers between devices: 109 us -> 98.1 us  [from_xor(): return lax.ppermute(value, axes, [(at ^ mask, at) for at in range(size)])]
  transfers between devices with their start and end apart: 64 -> 64, of which waited for: 24 -> 24; matrix products, arithmetic and copies ran while one was open for 5% -> 5% of each run, Pallas kernels for 35% -> 38%
where the time goes in v2:
time: 412 us; the launch traced here: 408 us
  Pallas kernels  175 us (42%)
  waiting for transfers between devices  98.1 us (24%)
  starting transfers between devices  80.5 us (20%)
  local copies, waits for them, and re-layouts  34.2 us (8%)
  other arithmetic  13.4 us (3%)
    pallas_call x62, Pallas kernels, call(): pl.pallas_call(body, grid_spec=pltpu.PrefetchScalarGridSpec(num_scalar_pr...  175 us
    ppermute x64, waiting for transfers between devices, from_xor(): return lax.ppermute(value, axes, [(at ^ mask, at) for at in range(size)])  98.1 us
    ppermute x64, starting transfers between devices, from_xor(): return lax.ppermute(value, axes, [(at ^ mask, at) for at in range(size)])  80.5 us
    unnamed x221, local copies, waits for them, and re-layouts  26.5 us
  transfers between devices with their start and end apart: 64, of which 24 were waited for; matrix products, arithmetic and copies ran while one was open for 5% of the time, Pallas kernels for 38%

profile of v2, /device:TPU:0, one launch (start us, length us, event | category | flops | bytes accessed | tf_op | source)
XLA Modules:
  0.0 407.6 jit_solution(3866063410457527993)
XLA Ops:
  2.7 5.1 %collective-permute-start.1 = (bf16[128,1024]{1,0:T(8,128)(2,1)S(1)}, bf16[128,1024]{1,0:T(8,128)(2,1)S(1)}, u32[]{:S(2)}, u32[]{:S(2)}) collective-permute-start(bf16[128,1024]{1,0:T(8,128)(2,1)S(1)} %pad_maximum_fusion.9.refs_1_), channel_id=1, source_target_pairs={{24,0},{16,8},{8,16},{0,24},{25,1},{17,9},{9,17},{1,25},{26,2},{18... | collective-permute-start | bytes 786440 | tf_op jit(solution)/shard_map/ppermute | solution.py:59
  16.8 5.0 %collective-permute-start.3 = (bf16[256,1024]{1,0:T(8,128)(2,1)S(1)}, bf16[256,1024]{1,0:T(8,128)(2,1)S(1)}, u32[]{:S(2)}, u32[]{:S(2)}) collective-permute-start(bf16[256,1024]{1,0:T(8,128)(2,1)S(1)} %pad_maximum_fusion.6.refs_2_), channel_id=1, source_target_pairs={{8,0},{0,8},{24,16},{16,24},{9,1},{1,9},{25,17},{17,25},{10,2},{2,... | collective-permute-start | bytes 1572872 | tf_op jit(solution)/shard_map/ppermute | solution.py:59
  24.0 8.7 %collective-permute-done.3.refs_1_.refs_0_ = bf16[256,1024]{1,0:T(8,128)(2,1)S(1)} collective-permute-done((bf16[256,1024]{1,0:T(8,128)(2,1)S(1)}, bf16[256,1024]{1,0:T(8,128)(2,1)S(1)}, u32[]{:S(2)}, u32[]{:S(2)}) %collective-permute-start.3) | collective-permute-done | bytes 524320 | tf_op jit(solution)/shard_map/ppermute | solution.py:59
  38.9 6.0 %collective-permute-done.10 = bf16[128,1024]{1,0:T(8,128)(2,1)S(1)} collective-permute-done((bf16[128,1024]{1,0:T(8,128)(2,1)S(1)}, bf16[128,1024]{1,0:T(8,128)(2,1)S(1)}, u32[]{:S(2)}, u32[]{:S(2)}) %collective-permute-start.10) | collective-permute-done | bytes 262176 | tf_op jit(solution)/shard_map/ppermute | solution.py:59
  45.7 9.7 %collective-permute-start.11 = (bf16[256,1024]{1,0:T(8,128)(2,1)}, bf16[256,1024]{1,0:T(8,128)(2,1)}, u32[]{:S(2)}, u32[]{:S(2)}) collective-permute-start(bf16[256,1024]{1,0:T(8,128)(2,1)} %pad_maximum_fusion.7.refs_4_.refs_0_), channel_id=1, source_target_pairs={{8,0},{0,8},{24,16},{16,24},{9,1},{1,9},{25,17},{17,25},{10,2},{2,... | collective-permute-start | bytes 1572872 | tf_op jit(solution)/shard_map/ppermute | solution.py:59
  58.7 3.0 collective-permute-start.8
  61.7 4.9 %shard_map.443 = (f32[8,2,320,320]{3,2,1,0:T(8,128)S(1)}, f32[8,128]{1,0:T(8,128)S(1)}) custom-call(f32[320,24]{1,0:T(8,128)S(1)} %copy-done.57, f32[8,24,320]{2,1,0:T(8,128)S(1)} %copy.92.refs_1_, bf16[512,1024]{1,0:T(8,128)(2,1)S(1)} %shard_map.440.refs_1_.refs_2_, bf16[2,256,1024]{2,1,0:T(8,128)(2,1)} %pad_maximum_fusion.1.refs_2_.refs_3_, ...), custom_call_target="tpu_custom_call" | custom-call | flops 3449999872 | bytes 1 | tf_op jit(solution)/shard_map/pallas_call | solution.py:183
  66.6 3.2 copy-done.84
  77.4 3.5 shard_map.444
  89.1 3.7 shard_map.446.refs_6_
  92.8 3.7 shard_map.447.refs_1_
  96.5 6.9 %shard_map.448 = (bf16[1280,512]{1,0:T(8,128)(2,1)S(1)}, f32[4,4,320]{2,1,0:T(4,128)S(1)}) custom-call(s32[2]{0:T(128)S(1)} %get-tuple-element.246.refs_0_, bf16[1280,1536]{1,0:T(8,128)(2,1)S(1)} %shard_map.447.refs_1_, f32[8,2,320,320]{3,2,1,0:T(8,128)S(1)} %bitcast.88), custom_call_target="tpu_custom_call" | custom-call | flops 8049999872 | bytes 1 | tf_op jit(solution)/shard_map/pallas_call | solution.py:183
  110.4 6.9 %shard_map.449 = (bf16[1280,512]{1,0:T(8,128)(2,1)S(1)}, f32[4,4,320]{2,1,0:T(4,128)S(1)}) custom-call(s32[2]{0:T(128)S(1)} %get-tuple-element.247.refs_0_, bf16[1280,1536]{1,0:T(8,128)(2,1)S(1)} %shard_map.447.refs_1_, f32[8,2,320,320]{3,2,1,0:T(8,128)S(1)} %bitcast.90, ...), custom_call_target="tpu_custom_call", output_to_operand_aliasing={{0}: (3, {})} | custom-call | flops 8049999872 | bytes 1 | tf_op jit(solution)/shard_map/pallas_call | solution.py:183
  125.6 7.1 %collective-permute-done.19.refs_2_.refs_3_ = bf16[512,1024]{1,0:T(8,128)(2,1)S(1)} collective-permute-done((bf16[512,1024]{1,0:T(8,128)(2,1)S(1)}, bf16[512,1024]{1,0:T(8,128)(2,1)S(1)}, u32[]{:S(2)}, u32[]{:S(2)}) %collective-permute-start.19) | collective-permute-done | bytes 1048608 | tf_op jit(solution)/shard_map/ppermute | solution.py:59
  136.3 6.5 %shard_map.456 = (bf16[1280,2048]{1,0:T(8,128)(2,1)S(1)}, bf16[1280,2048]{1,0:T(8,128)(2,1)S(1)}) custom-call(bf16[640,1024]{1,0:T(8,128)(2,1)S(1)} %get-tuple-element.127.refs_0_, bf16[512,1024]{1,0:T(8,128)(2,1)S(1)} %pad_maximum_fusion.2.refs_6_.refs_1_, bf16[256,1024]{1,0:T(8,128)(2,1)} %get-tuple-element.121.refs_6_.refs_1_.refs_2_, ...), custom_call_target="tpu_custom_call" | custom-call | flops 8770666496 | bytes 1 | tf_op jit(solution)/shard_map/pallas_call | solution.py:183
  142.9 4.9 %collective-permute-done.23.refs_0_ = bf16[256,1024]{1,0:T(8,128)(2,1)S(1)} collective-permute-done((bf16[256,1024]{1,0:T(8,128)(2,1)S(1)}, bf16[256,1024]{1,0:T(8,128)(2,1)S(1)}, u32[]{:S(2)}, u32[]{:S(2)}) %collective-permute-start.23) | collective-permute-done | bytes 524320 | tf_op jit(solution)/shard_map/ppermute | solution.py:59
  149.9 7.0 %shard_map.458 = (bf16[1280,2048]{1,0:T(8,128)(2,1)S(1)}, bf16[1280,2048]{1,0:T(8,128)(2,1)S(1)}) custom-call(bf16[640,1024]{1,0:T(8,128)(2,1)S(1)} %collective-permute-done.18.refs_0_.refs_1_, bf16[512,1024]{1,0:T(8,128)(2,1)S(1)} %pad_maximum_fusion.2.refs_6_.refs_1_, ...), custom_call_target="tpu_custom_call", output_to_operand_aliasing={{0}: (6, {}), {1}: (7, {})} | custom-call | flops 8770666496 | bytes 1 | tf_op jit(solution)/shard_map/pallas_call | solution.py:183
  156.9 4.3 %shard_map.460 = (bf16[512,1024]{1,0:T(8,128)(2,1)S(1)}, bf16[256,2048]{1,0:T(8,128)(2,1)S(1)}) custom-call(bf16[1280,1024]{1,0:T(8,128)(2,1)S(1)} %get-tuple-element.133.refs_0_.refs_1_, bf16[1280,1024]{1,0:T(8,128)(2,1)S(1)} %get-tuple-element.133.refs_0_.refs_1_, bf16[1280,2048]{1,0:T(8,128)(2,1)S(1)} %get-tuple-element.132.refs_2_.refs_0_, ...), custom_call_target="tpu_custom_call" | custom-call | flops 3449999872 | bytes 1 | tf_op jit(solution)/shard_map/pallas_call | solution.py:183
  161.3 9.8 %collective-permute-done.25.refs_2_.refs_3_ = bf16[512,1024]{1,0:T(8,128)(2,1)S(1)} collective-permute-done((bf16[512,1024]{1,0:T(8,128)(2,1)S(1)}, bf16[512,1024]{1,0:T(8,128)(2,1)S(1)}, u32[]{:S(2)}, u32[]{:S(2)}) %collective-permute-start.25) | collective-permute-done | bytes 1048608 | tf_op jit(solution)/shard_map/ppermute | solution.py:59
  173.6 3.1 shard_map.462.refs_7_.refs_0_
  176.6 4.2 %shard_map.467 = bf16[640,1024]{1,0:T(8,128)(2,1)S(1)} custom-call(bf16[1280,2048]{1,0:T(8,128)(2,1)S(1)} %shard_map.462.refs_7_.refs_0_, bf16[512,1024]{1,0:T(8,128)(2,1)S(1)} %pad_maximum_fusion.2.refs_6_.refs_1_, bf16[256,1024]{1,0:T(8,128)(2,1)} %get-tuple-element.121.refs_6_.refs_1_.refs_2_, ...), custom_call_target="tpu_custom_call" | custom-call | flops 5400399872 | bytes 1 | tf_op jit(solution)/shard_map/pallas_call | solution.py:183
  180.9 3.1 shard_map.463.refs_0_.refs_2_
  184.0 4.6 %shard_map.464.refs_6_.refs_2_ = f32[640,1024]{1,0:T(8,128)S(1)} custom-call(bf16[1280,2048]{1,0:T(8,128)(2,1)S(1)} %shard_map.463.refs_0_.refs_2_, bf16[512,1024]{1,0:T(8,128)(2,1)S(1)} %pad_maximum_fusion.2.refs_6_.refs_1_, bf16[256,1024]{1,0:T(8,128)(2,1)} %get-tuple-element.121.refs_6_.refs_1_.refs_2_, ...), custom_call_target="tpu_custom_call" | custom-call | flops 5400399872 | bytes 1 | tf_op jit(solution)/shard_map/pallas_call | solution.py:183
  188.6 4.0 shard_map.465.refs_5_
  194.7 4.6 %shard_map.466 = (f32[256,1024]{1,0:T(8,128)S(1)}, f32[256,1024]{1,0:T(8,128)S(1)}, bf16[256,1024]{1,0:T(8,128)(2,1)S(1)}, bf16[256,1024]{1,0:T(8,128)(2,1)S(1)}) custom-call(bf16[1280,1024]{1,0:T(8,128)(2,1)S(1)} %get-tuple-element.133.refs_0_.refs_1_, bf16[1280,1024]{1,0:T(8,128)(2,1)S(1)} %get-tuple-element.133.refs_0_.refs_1_, ...), custom_call_target="tpu_custom_call" | custom-call | flops 4600000000 | bytes 1 | tf_op jit(solution)/shard_map/pallas_call | solution.py:183
  199.5 4.1 %shard_map.468 = (f32[640,1024]{1,0:T(8,128)S(1)}, bf16[640,1024]{1,0:T(8,128)(2,1)}, f32[3,1024]{1,0:T(4,128)S(1)}) custom-call(f32[640,1024]{1,0:T(8,128)S(1)} %copy-done.64, f32[640,1024]{1,0:T(8,128)S(1)} %copy-done.72, f32[640,1024]{1,0:T(8,128)S(1)} %copy-done.74, bf16[640,1024]{1,0:T(8,128)(2,1)S(1)} %collective-permute-done.31.refs_3_, ...), custom_call_target="tpu_custom_call" | custom-call | flops 3680000000 | bytes 1 | tf_op jit(solution)/shard_map/pallas_call | solution.py:183
  208.9 2.5 copy-done.13
  214.0 4.3 %shard_map.469 = (bf16[512,1024]{1,0:T(8,128)(2,1)S(1)}, bf16[256,2048]{1,0:T(8,128)(2,1)S(1)}) custom-call(bf16[640,1024]{1,0:T(8,128)(2,1)S(1)} %copy-done.42, bf16[640,1024]{1,0:T(8,128)(2,1)S(1)} %copy-done.45, bf16[1280,2048]{1,0:T(8,128)(2,1)S(1)} %copy-done.13, bf16[640,1024]{1,0:T(8,128)(2,1)} %get-tuple-element.145.refs_3_.refs_0_), custom_call_target="tpu_custom_call" | custom-call | flops 3449999872 | bytes 1 | tf_op jit(solution)/shard_map/pallas_call | solution.py:183
  225.2 9.8 %shard_map.472 = (bf16[1280,1536]{1,0:T(8,128)(2,1)S(1)}, f32[4,128,128]{2,1,0:T(8,128)S(1)}) custom-call(s32[2]{0:T(128)S(1)} %get-tuple-element.246.refs_0_, bf16[1280,1536]{1,0:T(8,128)(2,1)S(1)} %copy-done.76, bf16[1280,512]{1,0:T(8,128)(2,1)S(1)} %shard_map.471.refs_2_, f32[8,2,320,320]{3,2,1,0:T(8,128)S(1)} %bitcast.92, ...), custom_call_target="tpu_custom_call" | custom-call | flops 12650000384 | bytes 1 | tf_op jit(solution)/shard_map/pallas_call | solution.py:183
  235.0 2.5 shard_map.473.refs_4_
  239.2 9.8 %shard_map.475 = (bf16[1280,1536]{1,0:T(8,128)(2,1)S(1)}, f32[4,128,128]{2,1,0:T(8,128)S(1)}) custom-call(s32[2]{0:T(128)S(1)} %get-tuple-element.247.refs_0_, bf16[1280,1536]{1,0:T(8,128)(2,1)S(1)} %copy-done.76, bf16[1280,512]{1,0:T(8,128)(2,1)S(1)} %shard_map.471.refs_2_, f32[8,2,320,320]{3,2,1,0:T(8,128)S(1)} %bitcast.92, ...), custom_call_target="tpu_custom_call", output_to_operand_aliasing={{0}: (6, {})} | custom-call | flops 12650000384 | bytes 1 | tf_op jit(solution)/shard_map/pallas_call | solution.py:183
  249.0 9.6 %shard_map.476 = (bf16[512,1024]{1,0:T(8,128)(2,1)}, bf16[256,2048]{1,0:T(8,128)(2,1)}) custom-call(bf16[640,1024]{1,0:T(8,128)(2,1)} %get-tuple-element.120.refs_0_, bf16[640,1024]{1,0:T(8,128)(2,1)} %collective-permute-done.12.refs_0_.refs_1_, bf16[1280,1536]{1,0:T(8,128)(2,1)S(1)} %get-tuple-element.152.refs_2_.refs_0_, ...), custom_call_target="tpu_custom_call" | custom-call | flops 3449999872 | bytes 1 | tf_op jit(solution)/shard_map/pallas_call | solution.py:183
  262.4 2.4 shard_map.478.refs_5_.refs_2_
  264.9 5.4 %shard_map.479 = (f32[256,1024]{1,0:T(8,128)S(1)}, f32[256,1024]{1,0:T(8,128)S(1)}, bf16[256,1024]{1,0:T(8,128)(2,1)}, bf16[256,1024]{1,0:T(8,128)(2,1)}) custom-call(bf16[640,1024]{1,0:T(8,128)(2,1)S(1)} %copy-done.43, bf16[640,1024]{1,0:T(8,128)(2,1)S(1)} %copy-done.46, bf16[1280,2048]{1,0:T(8,128)(2,1)S(1)} %bitcast.79, ...), custom_call_target="tpu_custom_call" | custom-call | flops 4600000000 | bytes 1 | tf_op jit(solution)/shard_map/pallas_call | solution.py:183
  273.4 4.6 %shard_map.480 = (f32[640,1024]{1,0:T(8,128)}, f32[2,1024]{1,0:T(2,128)S(1)}) custom-call(s32[8]{0:T(128)S(1)} %stack.122.refs_0_, bf16[640,1024]{1,0:T(8,128)(2,1)S(1)} %copy-done.83, f32[640,1024]{1,0:T(8,128)S(1)} %shard_map.478.refs_5_.refs_2_, bf16[640,1024]{1,0:T(8,128)(2,1)S(1)} %collective-permute-done.35.refs_6_.refs_3_, ...), custom_call_target="tpu_custom_call" | custom-call | flops 4600000000 | bytes 1 | tf_op jit(solution)/shard_map/pallas_call | solution.py:183
  280.7 3.1 shard_map.482.refs_2_.refs_1_
  283.9 5.1 %shard_map.483 = (bf16[640,1024]{1,0:T(8,128)(2,1)}, f32[1,1024]{1,0:T(1,128)S(1)}) custom-call(s32[8]{0:T(128)S(1)} %stack.122.refs_0_, f32[640,1024]{1,0:T(8,128)S(1)} %copy-done.65, f32[640,1024]{1,0:T(8,128)S(1)} %shard_map.482.refs_2_.refs_1_, bf16[640,1024]{1,0:T(8,128)(2,1)} %collective-permute-done.33.refs_6_.refs_3_, ...), custom_call_target="tpu_custom_call" | custom-call | flops 4024999936 | bytes 1 | tf_op jit(solution)/shard_map/pallas_call | solution.py:183
  290.0 7.5 %collective-permute-done.41.refs_2_ = bf16[256,1024]{1,0:T(8,128)(2,1)} collective-permute-done((bf16[256,1024]{1,0:T(8,128)(2,1)}, bf16[256,1024]{1,0:T(8,128)(2,1)}, u32[]{:S(2)}, u32[]{:S(2)}) %collective-permute-start.41) | collective-permute-done | bytes 524320 | tf_op jit(solution)/shard_map/ppermute | solution.py:59
  300.7 11.7 %collective-permute-done.43.refs_1_ = bf16[256,1024]{1,0:T(8,128)(2,1)S(1)} collective-permute-done((bf16[256,1024]{1,0:T(8,128)(2,1)S(1)}, bf16[256,1024]{1,0:T(8,128)(2,1)S(1)}, u32[]{:S(2)}, u32[]{:S(2)}) %collective-permute-start.43) | collective-permute-done | bytes 524320 | tf_op jit(solution)/shard_map/ppermute | solution.py:59
  315.9 8.0 %shard_map.486 = (f32[256,1024]{1,0:T(8,128)S(1)}, f32[256,1024]{1,0:T(8,128)S(1)}, bf16[256,1024]{1,0:T(8,128)(2,1)S(1)}, bf16[256,1024]{1,0:T(8,128)(2,1)S(1)}) custom-call(bf16[640,1024]{1,0:T(8,128)(2,1)} %get-tuple-element.120.refs_0_, bf16[640,1024]{1,0:T(8,128)(2,1)} %collective-permute-done.12.refs_0_.refs_1_, bf16[1280,1536]{1,0:T(8,128)(2,1)S(1)} %copy-done.62, ...), custom_call_target="tpu_custom_call" | custom-call | flops 4600000000 | bytes 1 | tf_op jit(solution)/shard_map/pallas_call | solution.py:183
  331.1 6.1 %collective-permute-done.46.refs_4_ = bf16[128,1024]{1,0:T(8,128)(2,1)S(1)} collective-permute-done((bf16[128,1024]{1,0:T(8,128)(2,1)S(1)}, bf16[128,1024]{1,0:T(8,128)(2,1)S(1)}, u32[]{:S(2)}, u32[]{:S(2)}) %collective-permute-start.46) | collective-permute-done | bytes 262176 | tf_op jit(solution)/shard_map/ppermute | solution.py:59
  340.2 2.7 collective-permute-done.45.refs_3_
  344.8 4.8 %collective-permute-done.51 = bf16[4,6992]{1,0:T(4,128)(2,1)S(1)} collective-permute-done((bf16[4,6992]{1,0:T(4,128)(2,1)S(1)}, bf16[4,6992]{1,0:T(4,128)(2,1)S(1)}, u32[]{:S(2)}, u32[]{:S(2)}) %collective-permute-start.51) | collective-permute-done | bytes 55968 | tf_op jit(solution)/shard_map/ppermute | solution.py:59
  351.7 4.0 collective-permute-done.52
  355.8 7.2 %collective-permute-done.47.refs_1_ = bf16[256,1024]{1,0:T(8,128)(2,1)S(1)} collective-permute-done((bf16[256,1024]{1,0:T(8,128)(2,1)S(1)}, bf16[256,1024]{1,0:T(8,128)(2,1)S(1)}, u32[]{:S(2)}, u32[]{:S(2)}) %collective-permute-start.47) | collective-permute-done | bytes 524320 | tf_op jit(solution)/shard_map/ppermute | solution.py:59
  366.3 4.4 %collective-permute-done.53.refs_6_ = bf16[16,6992]{1,0:T(8,128)(2,1)S(1)} collective-permute-done((bf16[16,6992]{1,0:T(8,128)(2,1)S(1)}, bf16[16,6992]{1,0:T(8,128)(2,1)S(1)}, u32[]{:S(2)}, u32[]{:S(2)}) %collective-permute-start.53) | collective-permute-done | bytes 223776 | tf_op jit(solution)/shard_map/ppermute | solution.py:59
  371.5 10.6 %shard_map.496 = (f32[128,6144]{1,0:T(8,128)}, f32[128,6144]{1,0:T(8,128)}, f32[128,6144]{1,0:T(8,128)}, f32[2,128]{1,0:T(2,128)S(1)}) custom-call(f32[128,6144]{1,0:T(8,128)} %refs_13_.1, f32[128,6144]{1,0:T(8,128)} %refs_1_.12, f32[128,6144]{1,0:T(8,128)} %refs_2_.11, bf16[16,128]{1,0:T(8,128)(2,1)S(1)} %convolution_convert_fusion.1.refs_3_, ...), custom_call_target="tpu_custom_call" | custom-call | flops 9200000000 | bytes 1 | tf_op jit(solution)/shard_map/pallas_call | solution.py:183
  401.0 6.4 %shard_map.497 = (f32[128,768]{1,0:T(8,128)}, f32[128,256]{1,0:T(8,128)}, f32[128,1024]{1,0:T(8,128)}, f32[128,1024]{1,0:T(8,128)}, f32[128,6144]{1,0:T(8,128)}, /*index=5*/f32[4,45]{1,0:T(4,128)}, f32[3,6]{1,0:T(4,128)}) custom-call(f32[12,1]{1,0:T(8,128)S(1)} %copy-done.59, f32[12,128]{1,0:T(8,128)S(1)} %add_add_fusion.refs_1_, ...), custom_call_target="tpu_custom_call" | custom-call | flops 5750000128 | bytes 1 | tf_op jit(solution)/shard_map/pallas_call | solution.py:183
  (471 shorter events, 134.4 us)
Async XLA Ops:
  2.7 11.8 %collective-permute-start.1 = (bf16[128,1024]{1,0:T(8,128)(2,1)S(1)}, bf16[128,1024]{1,0:T(8,128)(2,1)S(1)}, u32[]{:S(2)}, u32[]{:S(2)}) collective-permute-start(bf16[128,1024]{1,0:T(8,128)(2,1)S(1)} %pad_maximum_fusion.9.refs_1_), channel_id=1, source_target_pairs={{24,0},{16,8},{8,16},{0,24},{25,1},{17,9},{9,17},{1,25},{26,2},{18... | collective-permute-start | bytes 786440 | tf_op jit(solution)/shard_map/ppermute | solution.py:59
  15.2 8.6 %collective-permute-start.2 = (f32[8,1536]{1,0:T(8,128)S(1)}, f32[8,1536]{1,0:T(8,128)S(1)}, u32[]{:S(2)}, u32[]{:S(2)}) collective-permute-start(f32[8,1536]{1,0:T(8,128)S(1)} %get-tuple-element.116), channel_id=1, source_target_pairs={{2,0},{0,2},{3,1},{1,3},{6,4},{4,6},{7,5},{5,7},{10,8},{8,10},{11,... | collective-permute-start | bytes 147464 | tf_op jit(solution)/shard_map/ppermute | solution.py:59
  16.8 15.9 %collective-permute-start.3 = (bf16[256,1024]{1,0:T(8,128)(2,1)S(1)}, bf16[256,1024]{1,0:T(8,128)(2,1)S(1)}, u32[]{:S(2)}, u32[]{:S(2)}) collective-permute-start(bf16[256,1024]{1,0:T(8,128)(2,1)S(1)} %pad_maximum_fusion.6.refs_2_), channel_id=1, source_target_pairs={{8,0},{0,8},{24,16},{16,24},{9,1},{1,9},{25,17},{17,25},{10,2},{2,... | collective-permute-start | bytes 1572872 | tf_op jit(solution)/shard_map/ppermute | solution.py:59
  21.8 16.4 %collective-permute-start.6 = (bf16[256,1024]{1,0:T(8,128)(2,1)S(1)}, bf16[256,1024]{1,0:T(8,128)(2,1)S(1)}, u32[]{:S(2)}, u32[]{:S(2)}) collective-permute-start(bf16[256,1024]{1,0:T(8,128)(2,1)S(1)} %pad_maximum_fusion.6.refs_2_), channel_id=1, source_target_pairs={{4,0},{0,4},{5,1},{1,5},{6,2},{2,6},{7,3},{3,7},{12,8},{8,12},{13,... | collective-permute-start | bytes 1572872 | tf_op jit(solution)/shard_map/ppermute | solution.py:59
  23.3 9.5 %collective-permute-start.9 = (f32[4,45]{1,0:T(4,128)S(1)}, f32[4,45]{1,0:T(4,128)S(1)}, u32[]{:S(2)}, u32[]{:S(2)}) collective-permute-start(f32[4,45]{1,0:T(4,128)S(1)} %get-tuple-element.117), channel_id=1, source_target_pairs={{2,0},{0,2},{3,1},{1,3},{6,4},{4,6},{7,5},{5,7},{10,8},{8,10},{11,... | collective-permute-start | bytes 2168 | tf_op jit(solution)/shard_map/ppermute | solution.py:59
  33.8 11.1 %collective-permute-start.10 = (bf16[128,1024]{1,0:T(8,128)(2,1)S(1)}, bf16[128,1024]{1,0:T(8,128)(2,1)S(1)}, u32[]{:S(2)}, u32[]{:S(2)}) collective-permute-start(bf16[128,1024]{1,0:T(8,128)(2,1)S(1)} %shard_map.442), channel_id=1, source_target_pairs={{24,0},{16,8},{8,16},{0,24},{25,1},{17,9},{9,17},{1,25},{26,2},{18... | collective-permute-start | bytes 786440 | tf_op jit(solution)/shard_map/ppermute | solution.py:59
  36.6 18.8 %collective-permute-start.5 = (f32[8,2,2,1536]{3,2,1,0:T(2,128)S(1)}, f32[8,2,2,1536]{3,2,1,0:T(2,128)S(1)}, u32[]{:S(2)}, u32[]{:S(2)}) collective-permute-start(f32[8,2,2,1536]{3,2,1,0:T(2,128)S(1)} %pad_maximum_fusion.11), channel_id=1, source_target_pairs={{24,0},{16,8},{8,16},{0,24},{25,1},{17,9},{9,17},{1,25},{26,2},{18... | collective-permute-start | bytes 589832 | tf_op jit(solution)/shard_map/ppermute | solution.py:59
  38.3 17.3 %collective-permute-start.7 = (bf16[256,1024]{1,0:T(8,128)(2,1)S(1)}, bf16[256,1024]{1,0:T(8,128)(2,1)S(1)}, u32[]{:S(2)}, u32[]{:S(2)}) collective-permute-start(bf16[256,1024]{1,0:T(8,128)(2,1)S(1)} %shard_map.439.refs_2_), channel_id=1, source_target_pairs={{2,0},{0,2},{3,1},{1,3},{6,4},{4,6},{7,5},{5,7},{10,8},{8,10},{11,... | collective-permute-start | bytes 1572872 | tf_op jit(solution)/shard_map/ppermute | solution.py:59
  45.7 30.4 %collective-permute-start.11 = (bf16[256,1024]{1,0:T(8,128)(2,1)}, bf16[256,1024]{1,0:T(8,128)(2,1)}, u32[]{:S(2)}, u32[]{:S(2)}) collective-permute-start(bf16[256,1024]{1,0:T(8,128)(2,1)} %pad_maximum_fusion.7.refs_4_.refs_0_), channel_id=1, source_target_pairs={{8,0},{0,8},{24,16},{16,24},{9,1},{1,9},{25,17},{17,25},{10,2},{2,... | collective-permute-start | bytes 1572872 | tf_op jit(solution)/shard_map/ppermute | solution.py:59
  55.6 28.2 %collective-permute-start.13 = (bf16[512,1024]{1,0:T(8,128)(2,1)S(1)}, bf16[512,1024]{1,0:T(8,128)(2,1)S(1)}, u32[]{:S(2)}, u32[]{:S(2)}) collective-permute-start(bf16[512,1024]{1,0:T(8,128)(2,1)S(1)} %shard_map.440.refs_1_.refs_2_), channel_id=1, source_target_pairs={{2,0},{0,2},{3,1},{1,3},{6,4},{4,6},{7,5},{5,7},{10,8},{8,10},{11,... | collective-permute-start | bytes 3145736 | tf_op jit(solution)/shard_map/ppermute | solution.py:59
  57.2 26.5 %collective-permute-start.14 = (bf16[2,256,1024]{2,1,0:T(8,128)(2,1)}, bf16[2,256,1024]{2,1,0:T(8,128)(2,1)S(1)}, u32[]{:S(2)}, u32[]{:S(2)}) collective-permute-start(bf16[2,256,1024]{2,1,0:T(8,128)(2,1)} %pad_maximum_fusion.1.refs_2_.refs_3_), channel_id=1, source_target_pairs={{4,0},{0,4},{5,1},{1,5},{6,2},{2,6},{7,3},{3,7},{12,8},{8,12},{13,... | collective-permute-start | bytes 3145736 | tf_op jit(solution)/shard_map/ppermute | solution.py:59
  58.7 12.5 %collective-permute-start.8 = (f32[8,2,2,1536]{3,2,1,0:T(2,128)S(1)}, f32[8,2,2,1536]{3,2,1,0:T(2,128)S(1)}, u32[]{:S(2)}, u32[]{:S(2)}) collective-permute-start(f32[8,2,2,1536]{3,2,1,0:T(2,128)S(1)} %shard_map.441), channel_id=1, source_target_pairs={{8,0},{0,8},{24,16},{16,24},{9,1},{1,9},{25,17},{17,25},{10,2},{2,... | collective-permute-start | bytes 589832 | tf_op jit(solution)/shard_map/ppermute | solution.py:59
  81.9 10.9 %collective-permute-start.12 = (bf16[640,1024]{1,0:T(8,128)(2,1)}, bf16[640,1024]{1,0:T(8,128)(2,1)}, u32[]{:S(2)}, u32[]{:S(2)}) collective-permute-start(bf16[640,1024]{1,0:T(8,128)(2,1)} %get-tuple-element.120.refs_0_), channel_id=1, source_target_pairs={{1,0},{0,1},{3,2},{2,3},{5,4},{4,5},{7,6},{6,7},{9,8},{8,9},{11,10... | collective-permute-start | bytes 3932168 | tf_op jit(solution)/shard_map/ppermute | solution.py:59
  84.8 18.6 %collective-permute-start.15 = (bf16[256,1024]{1,0:T(8,128)(2,1)}, bf16[256,1024]{1,0:T(8,128)(2,1)S(1)}, u32[]{:S(2)}, u32[]{:S(2)}) collective-permute-start(bf16[256,1024]{1,0:T(8,128)(2,1)} %get-tuple-element.125), channel_id=1, source_target_pairs={{4,0},{0,4},{5,1},{1,5},{6,2},{2,6},{7,3},{3,7},{12,8},{8,12},{13,... | collective-permute-start | bytes 1572872 | tf_op jit(solution)/shard_map/ppermute | solution.py:59
  86.3 18.5 %collective-permute-start.16 = (bf16[256,1024]{1,0:T(8,128)(2,1)}, bf16[256,1024]{1,0:T(8,128)(2,1)S(1)}, u32[]{:S(2)}, u32[]{:S(2)}) collective-permute-start(bf16[256,1024]{1,0:T(8,128)(2,1)} %get-tuple-element.121.refs_6_.refs_1_.refs_2_), channel_id=1, source_target_pairs={{2,0},{0,2},{3,1},{1,3},{6,4},{4,6},{7,5},{5,7},{10,8},{8,10},{11,... | collective-permute-start | bytes 1572872 | tf_op jit(solution)/shard_map/ppermute | solution.py:59
  86.8 19.2 %collective-permute-start.21 = (bf16[128,1024]{1,0:T(8,128)(2,1)S(1)}, bf16[128,1024]{1,0:T(8,128)(2,1)S(1)}, u32[]{:S(2)}, u32[]{:S(2)}) collective-permute-start(bf16[128,1024]{1,0:T(8,128)(2,1)S(1)} %shard_map.454), channel_id=1, source_target_pairs={{24,0},{16,8},{8,16},{0,24},{25,1},{17,9},{9,17},{1,25},{26,2},{18... | collective-permute-start | bytes 786440 | tf_op jit(solution)/shard_map/ppermute | solution.py:59
  105.9 12.5 %collective-permute-start.17 = (bf16[640,1024]{1,0:T(8,128)(2,1)S(1)}, bf16[640,1024]{1,0:T(8,128)(2,1)S(1)}, u32[]{:S(2)}, u32[]{:S(2)}) collective-permute-start(bf16[640,1024]{1,0:T(8,128)(2,1)S(1)} %shard_map.452), channel_id=1, source_target_pairs={{1,0},{0,1},{3,2},{2,3},{5,4},{4,5},{7,6},{6,7},{9,8},{8,9},{11,10... | collective-permute-start | bytes 3932168 | tf_op jit(solution)/shard_map/ppermute | solution.py:59
  106.1 19.5 %collective-permute-start.22 = (bf16[256,1024]{1,0:T(8,128)(2,1)S(1)}, bf16[256,1024]{1,0:T(8,128)(2,1)S(1)}, u32[]{:S(2)}, u32[]{:S(2)}) collective-permute-start(bf16[256,1024]{1,0:T(8,128)(2,1)S(1)} %pad_maximum_fusion.8.refs_0_), channel_id=1, source_target_pairs={{8,0},{0,8},{24,16},{16,24},{9,1},{1,9},{25,17},{17,25},{10,2},{2,... | collective-permute-start | bytes 1572872 | tf_op jit(solution)/shard_map/ppermute | solution.py:59
  107.4 25.3 %collective-permute-start.19 = (bf16[512,1024]{1,0:T(8,128)(2,1)S(1)}, bf16[512,1024]{1,0:T(8,128)(2,1)S(1)}, u32[]{:S(2)}, u32[]{:S(2)}) collective-permute-start(bf16[512,1024]{1,0:T(8,128)(2,1)S(1)} %pad_maximum_fusion.2.refs_6_.refs_1_), channel_id=1, source_target_pairs={{2,0},{0,2},{3,1},{1,3},{6,4},{4,6},{7,5},{5,7},{10,8},{8,10},{11,... | collective-permute-start | bytes 3145736 | tf_op jit(solution)/shard_map/ppermute | solution.py:59
  109.8 25.1 %collective-permute-start.20 = (bf16[2,256,1024]{2,1,0:T(8,128)(2,1)S(1)}, bf16[2,256,1024]{2,1,0:T(8,128)(2,1)S(1)}, u32[]{:S(2)}, u32[]{:S(2)}) collective-permute-start(bf16[2,256,1024]{2,1,0:T(8,128)(2,1)S(1)} %pad_maximum_fusion.3), channel_id=1, source_target_pairs={{4,0},{0,4},{5,1},{1,5},{6,2},{2,6},{7,3},{3,7},{12,8},{8,12},{13,... | collective-permute-start | bytes 3145736 | tf_op jit(solution)/shard_map/ppermute | solution.py:59
  123.6 26.3 %collective-permute-start.18 = (bf16[640,1024]{1,0:T(8,128)(2,1)S(1)}, bf16[640,1024]{1,0:T(8,128)(2,1)S(1)}, u32[]{:S(2)}, u32[]{:S(2)}) collective-permute-start(bf16[640,1024]{1,0:T(8,128)(2,1)S(1)} %get-tuple-element.127.refs_0_), channel_id=1, source_target_pairs={{1,0},{0,1},{3,2},{2,3},{5,4},{4,5},{7,6},{6,7},{9,8},{8,9},{11,10... | collective-permute-start | bytes 3932168 | tf_op jit(solution)/shard_map/ppermute | solution.py:59
  134.8 12.9 %collective-permute-start.23 = (bf16[256,1024]{1,0:T(8,128)(2,1)S(1)}, bf16[256,1024]{1,0:T(8,128)(2,1)S(1)}, u32[]{:S(2)}, u32[]{:S(2)}) collective-permute-start(bf16[256,1024]{1,0:T(8,128)(2,1)S(1)} %get-tuple-element.131), channel_id=1, source_target_pairs={{4,0},{0,4},{5,1},{1,5},{6,2},{2,6},{7,3},{3,7},{12,8},{8,12},{13,... | collective-permute-start | bytes 1572872 | tf_op jit(solution)/shard_map/ppermute | solution.py:59
  135.4 13.5 %collective-permute-start.24 = (bf16[256,1024]{1,0:T(8,128)(2,1)S(1)}, bf16[256,1024]{1,0:T(8,128)(2,1)S(1)}, u32[]{:S(2)}, u32[]{:S(2)}) collective-permute-start(bf16[256,1024]{1,0:T(8,128)(2,1)S(1)} %get-tuple-element.128.refs_6_.refs_2_), channel_id=1, source_target_pairs={{2,0},{0,2},{3,1},{1,3},{6,4},{4,6},{7,5},{5,7},{10,8},{8,10},{11,... | collective-permute-start | bytes 1572872 | tf_op jit(solution)/shard_map/ppermute | solution.py:59
  147.8 23.3 %collective-permute-start.25 = (bf16[512,1024]{1,0:T(8,128)(2,1)S(1)}, bf16[512,1024]{1,0:T(8,128)(2,1)S(1)}, u32[]{:S(2)}, u32[]{:S(2)}) collective-permute-start(bf16[512,1024]{1,0:T(8,128)(2,1)S(1)} %pad_maximum_fusion.4.refs_8_.refs_3_.refs_1_), channel_id=1, source_target_pairs={{2,0},{0,2},{3,1},{1,3},{6,4},{4,6},{7,5},{5,7},{10,8},{8,10},{11,... | collective-permute-start | bytes 3145736 | tf_op jit(solution)/shard_map/ppermute | solution.py:59
  149.0 23.0 %collective-permute-start.26 = (bf16[2,256,1024]{2,1,0:T(8,128)(2,1)S(1)}, bf16[2,256,1024]{2,1,0:T(8,128)(2,1)S(1)}, u32[]{:S(2)}, u32[]{:S(2)}) collective-permute-start(bf16[2,256,1024]{2,1,0:T(8,128)(2,1)S(1)} %pad_maximum_fusion.5), channel_id=1, source_target_pairs={{4,0},{0,4},{5,1},{1,5},{6,2},{2,6},{7,3},{3,7},{12,8},{8,12},{13,... | collective-permute-start | bytes 3145736 | tf_op jit(solution)/shard_map/ppermute | solution.py:59
  172.0 22.2 %collective-permute-start.27 = (bf16[512,1024]{1,0:T(8,128)(2,1)S(1)}, bf16[512,1024]{1,0:T(8,128)(2,1)S(1)}, u32[]{:S(2)}, u32[]{:S(2)}) collective-permute-start(bf16[512,1024]{1,0:T(8,128)(2,1)S(1)} %get-tuple-element.136.refs_7_), channel_id=1, source_target_pairs={{2,0},{0,2},{3,1},{1,3},{6,4},{4,6},{7,5},{5,7},{10,8},{8,10},{11,... | collective-permute-start | bytes 3145736 | tf_op jit(solution)/shard_map/ppermute | solution.py:59
  173.0 21.7 %collective-permute-start.28 = (bf16[256,2048]{1,0:T(8,128)(2,1)S(1)}, bf16[256,2048]{1,0:T(8,128)(2,1)S(1)}, u32[]{:S(2)}, u32[]{:S(2)}) collective-permute-start(bf16[256,2048]{1,0:T(8,128)(2,1)S(1)} %get-tuple-element.137), channel_id=1, source_target_pairs={{4,0},{0,4},{5,1},{1,5},{6,2},{2,6},{7,3},{3,7},{12,8},{8,12},{13,... | collective-permute-start | bytes 3145736 | tf_op jit(solution)/shard_map/ppermute | solution.py:59
  180.8 18.6 %collective-permute-start.31 = (bf16[640,1024]{1,0:T(8,128)(2,1)S(1)}, bf16[640,1024]{1,0:T(8,128)(2,1)S(1)}, u32[]{:S(2)}, u32[]{:S(2)}) collective-permute-start(bf16[640,1024]{1,0:T(8,128)(2,1)S(1)} %shard_map.467), channel_id=1, source_target_pairs={{1,0},{0,1},{3,2},{2,3},{5,4},{4,5},{7,6},{6,7},{9,8},{8,9},{11,10... | collective-permute-start | bytes 3932168 | tf_op jit(solution)/shard_map/ppermute | solution.py:59
  205.1 16.6 %collective-permute-start.32 = (bf16[640,1024]{1,0:T(8,128)(2,1)}, bf16[640,1024]{1,0:T(8,128)(2,1)}, u32[]{:S(2)}, u32[]{:S(2)}) collective-permute-start(bf16[640,1024]{1,0:T(8,128)(2,1)} %get-tuple-element.145.refs_3_.refs_0_), channel_id=1, source_target_pairs={{1,0},{0,1},{3,2},{2,3},{5,4},{4,5},{7,6},{6,7},{9,8},{8,9},{11,10... | collective-permute-start | bytes 3932168 | tf_op jit(solution)/shard_map/ppermute | solution.py:59
  205.1 20.0 %collective-permute-start.33 = (bf16[640,1024]{1,0:T(8,128)(2,1)}, bf16[640,1024]{1,0:T(8,128)(2,1)}, u32[]{:S(2)}, u32[]{:S(2)}) collective-permute-start(bf16[640,1024]{1,0:T(8,128)(2,1)} %shard_map.465.refs_5_), channel_id=1, source_target_pairs={{1,0},{0,1},{3,2},{2,3},{5,4},{4,5},{7,6},{6,7},{9,8},{8,9},{11,10... | collective-permute-start | bytes 3932168 | tf_op jit(solution)/shard_map/ppermute | solution.py:59
  206.9 30.7 %collective-permute-start.29 = (bf16[256,1024]{1,0:T(8,128)(2,1)}, bf16[256,1024]{1,0:T(8,128)(2,1)S(1)}, u32[]{:S(2)}, u32[]{:S(2)}) collective-permute-start(bf16[256,1024]{1,0:T(8,128)(2,1)} %copy-done.52), channel_id=1, source_target_pairs={{4,0},{0,4},{5,1},{1,5},{6,2},{2,6},{7,3},{3,7},{12,8},{8,12},{13,... | collective-permute-start | bytes 1572872 | tf_op jit(solution)/shard_map/ppermute | solution.py:59
  207.9 29.7 %collective-permute-start.30 = (bf16[256,1024]{1,0:T(8,128)(2,1)}, bf16[256,1024]{1,0:T(8,128)(2,1)S(1)}, u32[]{:S(2)}, u32[]{:S(2)}) collective-permute-start(bf16[256,1024]{1,0:T(8,128)(2,1)} %copy-done.51), channel_id=1, source_target_pairs={{2,0},{0,2},{3,1},{1,3},{6,4},{4,6},{7,5},{5,7},{10,8},{8,10},{11,... | collective-permute-start | bytes 1572872 | tf_op jit(solution)/shard_map/ppermute | solution.py:59
  218.3 46.5 %collective-permute-start.37 = (bf16[512,1024]{1,0:T(8,128)(2,1)S(1)}, bf16[512,1024]{1,0:T(8,128)(2,1)S(1)}, u32[]{:S(2)}, u32[]{:S(2)}) collective-permute-start(bf16[512,1024]{1,0:T(8,128)(2,1)S(1)} %get-tuple-element.146.refs_6_), channel_id=1, source_target_pairs={{2,0},{0,2},{3,1},{1,3},{6,4},{4,6},{7,5},{5,7},{10,8},{8,10},{11,... | collective-permute-start | bytes 3145736 | tf_op jit(solution)/shard_map/ppermute | solution.py:59
  221.8 43.1 %collective-permute-start.38 = (bf16[256,2048]{1,0:T(8,128)(2,1)S(1)}, bf16[256,2048]{1,0:T(8,128)(2,1)S(1)}, u32[]{:S(2)}, u32[]{:S(2)}) collective-permute-start(bf16[256,2048]{1,0:T(8,128)(2,1)S(1)} %get-tuple-element.157), channel_id=1, source_target_pairs={{4,0},{0,4},{5,1},{1,5},{6,2},{2,6},{7,3},{3,7},{12,8},{8,12},{13,... | collective-permute-start | bytes 3145736 | tf_op jit(solution)/shard_map/ppermute | solution.py:59
  237.5 11.5 %collective-permute-start.35 = (bf16[640,1024]{1,0:T(8,128)(2,1)S(1)}, bf16[640,1024]{1,0:T(8,128)(2,1)S(1)}, u32[]{:S(2)}, u32[]{:S(2)}) collective-permute-start(bf16[640,1024]{1,0:T(8,128)(2,1)S(1)} %shard_map.473.refs_4_), channel_id=1, source_target_pairs={{1,0},{0,1},{3,2},{2,3},{5,4},{4,5},{7,6},{6,7},{9,8},{8,9},{11,10... | collective-permute-start | bytes 3932168 | tf_op jit(solution)/shard_map/ppermute | solution.py:59
  237.9 21.6 %collective-permute-start.34 = (bf16[256,1024]{1,0:T(8,128)(2,1)S(1)}, bf16[256,1024]{1,0:T(8,128)(2,1)S(1)}, u32[]{:S(2)}, u32[]{:S(2)}) collective-permute-start(bf16[256,1024]{1,0:T(8,128)(2,1)S(1)} %get-tuple-element.150.refs_7_), channel_id=1, source_target_pairs={{8,0},{0,8},{24,16},{16,24},{9,1},{1,9},{25,17},{17,25},{10,2},{2,... | collective-permute-start | bytes 1572872 | tf_op jit(solution)/shard_map/ppermute | solution.py:59
  258.5 54.0 %collective-permute-start.39 = (bf16[512,1024]{1,0:T(8,128)(2,1)}, bf16[512,1024]{1,0:T(8,128)(2,1)}, u32[]{:S(2)}, u32[]{:S(2)}) collective-permute-start(bf16[512,1024]{1,0:T(8,128)(2,1)} %get-tuple-element.153.refs_2_), channel_id=1, source_target_pairs={{2,0},{0,2},{3,1},{1,3},{6,4},{4,6},{7,5},{5,7},{10,8},{8,10},{11,... | collective-permute-start | bytes 3145736 | tf_op jit(solution)/shard_map/ppermute | solution.py:59
  259.6 18.4 %collective-permute-start.36 = (bf16[128,1024]{1,0:T(8,128)(2,1)S(1)}, bf16[128,1024]{1,0:T(8,128)(2,1)S(1)}, u32[]{:S(2)}, u32[]{:S(2)}) collective-permute-start(bf16[128,1024]{1,0:T(8,128)(2,1)S(1)} %get-tuple-element.155.refs_6_), channel_id=1, source_target_pairs={{24,0},{16,8},{8,16},{0,24},{25,1},{17,9},{9,17},{1,25},{26,2},{18... | collective-permute-start | bytes 786440 | tf_op jit(solution)/shard_map/ppermute | solution.py:59
  261.2 51.4 %collective-permute-start.40 = (bf16[256,2048]{1,0:T(8,128)(2,1)}, bf16[256,2048]{1,0:T(8,128)(2,1)}, u32[]{:S(2)}, u32[]{:S(2)}) collective-permute-start(bf16[256,2048]{1,0:T(8,128)(2,1)} %get-tuple-element.163), channel_id=1, source_target_pairs={{4,0},{0,4},{5,1},{1,5},{6,2},{2,6},{7,3},{3,7},{12,8},{8,12},{13,... | collective-permute-start | bytes 3145736 | tf_op jit(solution)/shard_map/ppermute | solution.py:59
  271.3 26.2 %collective-permute-start.41 = (bf16[256,1024]{1,0:T(8,128)(2,1)}, bf16[256,1024]{1,0:T(8,128)(2,1)}, u32[]{:S(2)}, u32[]{:S(2)}) collective-permute-start(bf16[256,1024]{1,0:T(8,128)(2,1)} %get-tuple-element.158.refs_6_), channel_id=1, source_target_pairs={{4,0},{0,4},{5,1},{1,5},{6,2},{2,6},{7,3},{3,7},{12,8},{8,12},{13,... | collective-permute-start | bytes 1572872 | tf_op jit(solution)/shard_map/ppermute | solution.py:59
  272.2 25.3 %collective-permute-start.42 = (bf16[256,1024]{1,0:T(8,128)(2,1)}, bf16[256,1024]{1,0:T(8,128)(2,1)}, u32[]{:S(2)}, u32[]{:S(2)}) collective-permute-start(bf16[256,1024]{1,0:T(8,128)(2,1)} %get-tuple-element.166), channel_id=1, source_target_pairs={{2,0},{0,2},{3,1},{1,3},{6,4},{4,6},{7,5},{5,7},{10,8},{8,10},{11,... | collective-permute-start | bytes 1572872 | tf_op jit(solution)/shard_map/ppermute | solution.py:59
  299.8 12.6 %collective-permute-start.43 = (bf16[256,1024]{1,0:T(8,128)(2,1)S(1)}, bf16[256,1024]{1,0:T(8,128)(2,1)S(1)}, u32[]{:S(2)}, u32[]{:S(2)}) collective-permute-start(bf16[256,1024]{1,0:T(8,128)(2,1)S(1)} %get-tuple-element.169), channel_id=1, source_target_pairs={{8,0},{0,8},{24,16},{16,24},{9,1},{1,9},{25,17},{17,25},{10,2},{2,... | collective-permute-start | bytes 1572872 | tf_op jit(solution)/shard_map/ppermute | solution.py:59
  326.5 13.7 %collective-permute-start.44 = (bf16[256,1024]{1,0:T(8,128)(2,1)S(1)}, bf16[256,1024]{1,0:T(8,128)(2,1)S(1)}, u32[]{:S(2)}, u32[]{:S(2)}) collective-permute-start(bf16[256,1024]{1,0:T(8,128)(2,1)S(1)} %get-tuple-element.173.refs_5_.refs_1_), channel_id=1, source_target_pairs={{4,0},{0,4},{5,1},{1,5},{6,2},{2,6},{7,3},{3,7},{12,8},{8,12},{13,... | collective-permute-start | bytes 1572872 | tf_op jit(solution)/shard_map/ppermute | solution.py:59
  327.4 9.7 %collective-permute-start.46 = (bf16[128,1024]{1,0:T(8,128)(2,1)S(1)}, bf16[128,1024]{1,0:T(8,128)(2,1)S(1)}, u32[]{:S(2)}, u32[]{:S(2)}) collective-permute-start(bf16[128,1024]{1,0:T(8,128)(2,1)S(1)} %get-tuple-element.170.refs_8_), channel_id=1, source_target_pairs={{24,0},{16,8},{8,16},{0,24},{25,1},{17,9},{9,17},{1,25},{26,2},{18... | collective-permute-start | bytes 786440 | tf_op jit(solution)/shard_map/ppermute | solution.py:59
  329.7 13.2 %collective-permute-start.45 = (bf16[256,1024]{1,0:T(8,128)(2,1)S(1)}, bf16[256,1024]{1,0:T(8,128)(2,1)S(1)}, u32[]{:S(2)}, u32[]{:S(2)}) collective-permute-start(bf16[256,1024]{1,0:T(8,128)(2,1)S(1)} %get-tuple-element.174), channel_id=1, source_target_pairs={{2,0},{0,2},{3,1},{1,3},{6,4},{4,6},{7,5},{5,7},{10,8},{8,10},{11,... | collective-permute-start | bytes 1572872 | tf_op jit(solution)/shard_map/ppermute | solution.py:59
  343.2 6.4 %collective-permute-start.51 = (bf16[4,6992]{1,0:T(4,128)(2,1)S(1)}, bf16[4,6992]{1,0:T(4,128)(2,1)S(1)}, u32[]{:S(2)}, u32[]{:S(2)}) collective-permute-start(bf16[4,6992]{1,0:T(4,128)(2,1)S(1)} %shard_map.494), channel_id=1, source_target_pairs={{24,0},{16,8},{8,16},{0,24},{25,1},{17,9},{9,17},{1,25},{26,2},{18... | collective-permute-start | bytes 167816 | tf_op jit(solution)/shard_map/ppermute | solution.py:59
  349.7 13.3 %collective-permute-start.47 = (bf16[256,1024]{1,0:T(8,128)(2,1)S(1)}, bf16[256,1024]{1,0:T(8,128)(2,1)S(1)}, u32[]{:S(2)}, u32[]{:S(2)}) collective-permute-start(bf16[256,1024]{1,0:T(8,128)(2,1)S(1)} %get-tuple-element.178.refs_1_), channel_id=1, source_target_pairs={{8,0},{0,8},{24,16},{16,24},{9,1},{1,9},{25,17},{17,25},{10,2},{2,... | collective-permute-start | bytes 1572872 | tf_op jit(solution)/shard_map/ppermute | solution.py:59
  363.1 19.7 %collective-permute-start.48 = (bf16[128,1024]{1,0:T(8,128)(2,1)S(1)}, bf16[128,1024]{1,0:T(8,128)(2,1)S(1)}, u32[]{:S(2)}, u32[]{:S(2)}) collective-permute-start(bf16[128,1024]{1,0:T(8,128)(2,1)S(1)} %get-tuple-element.180.refs_1_.refs_7_), channel_id=1, source_target_pairs={{24,0},{16,8},{8,16},{0,24},{25,1},{17,9},{9,17},{1,25},{26,2},{18... | collective-permute-start | bytes 786440 | tf_op jit(solution)/shard_map/ppermute | solution.py:59
  (126 other events, 953.7 us)
